TPU v7x, 32 devices: a whole 2x2x4 slice. The times are simulated.
32 devices in a mesh: dp: 2 (over x), fsdp: 16 (over z, y, core).
Axes of the slice: x: 2, y: 2, z: 4, core: 2. Of those that a mesh axis runs over, the one named last changes fastest.
Arguments:
- tokens: bfloat16 [49152, 768], P(('dp', 'fsdp')), may hold values from -14 to 14
- masked_pos: int32 [96, 104], P(('dp', 'fsdp')), may hold values from 0 to 511, as said below
- masked_count: int32 [96], P(('dp', 'fsdp')), may hold values from 52 to 104, as said below
- out_grad: bfloat16 [96, 104, 768], P(('dp', 'fsdp')), may hold values from -6 to 6
- weights: bfloat16 [9216, 768], P('fsdp'), may hold values from -5 to 5
- vectors: float32 [12, 768], replicated, may hold values from -2 to 2
- owner_list: int32 [192], replicated, may hold values from 0 to 15, as said below
- master_slots: float32 [384, 48, 768], P('fsdp'), may hold values from -5 to 5
- first_slots: float32 [384, 48, 768], P('fsdp')
- second_slots: float32 [384, 48, 768], P('fsdp'), as said below
- vector_first: float32 [12, 768], replicated
- vector_second: float32 [12, 768], replicated, as said below
Outputs:
- layer_out: bfloat16 [49152, 768], P(('dp', 'fsdp'))
- token_grad: float32 [49152, 768], P(('dp', 'fsdp'))
- new_weights: float32 [9216, 768], P('fsdp')
- new_first: float32 [384, 48, 768], P('fsdp')
- new_second: float32 [384, 48, 768], P('fsdp')
- new_vectors: float32 [12, 768], replicated
- new_vector_first: float32 [12, 768], replicated
- new_vector_second: float32 [12, 768], replicated
Inputs may be any that keep to these rules, and one draw needn't show every extreme that they name: `masked_pos`: within a page the 104 positions are distinct; only the first masked_count of them are used. `masked_count`: some page of every draw uses exactly 104. `owner_list`: each fsdp index owns at most 24 blocks, and some index owns exactly 24. `second_slots`: Positive. `vector_second`: Positive.
All inputs are finite; a program needn't handle non-finite values.
Results may differ from a plain program's by a relative error of at most 0.011.
Values may be sent and summed in bfloat16 or wider, within the bound.
No kernel may reach another device: no remote copies, remote signals or barrier semaphores. Data moves between devices by JAX's collectives and lax.ppermute only.
A program may use at most 320 MiB of HBM per device.

v0:
```python
import jax
import jax.numpy as jnp
from jax import lax
from jax.sharding import PartitionSpec as P

MODEL_WIDTH = 768
HEADS = 12
HD = 64
FF = 3072
PAGE = 512
MASKM = 104
BLOCK_ROWS = 48
STEP = 10
NBLK = 192


QUERY_SCALE = 0.125
NORM_EPSILON = 1e-06
INV_ROOT_TWO = 0.7071067811865476
INV_ROOT_TAU = 0.3989422804014327
FIRST_DECAY = 0.5
SECOND_DECAY = 0.5
LEARN_RATE = 0.05
VECTOR_RATE = 0.3
WEIGHT_DECAY = 0.01
ADAM_EPSILON = 1e-08
CONTRACT_LAST = (((1,), (1,)), ((), ()))
CONTRACT_FIRST = (((0,), (0,)), ((), ()))


def matmul(left_side, right_side):
    return jnp.dot(left_side, right_side, preferred_element_type=jnp.float32)


def times_last(left_side, right_side):
    return lax.dot_general(left_side, right_side, CONTRACT_LAST, preferred_element_type=jnp.float32)


def times_first(left_side, right_side):
    return lax.dot_general(
        left_side, right_side, CONTRACT_FIRST, preferred_element_type=jnp.float32
    )


def normalize(token_rows, gain_row, shift_row):
    center = token_rows - jnp.mean(token_rows, axis=1, keepdims=True)
    inverse = lax.rsqrt(jnp.mean(center * center, axis=1, keepdims=True) + NORM_EPSILON)
    unit_rows = center * inverse
    return (unit_rows * gain_row + shift_row, unit_rows, inverse)


def norm_backward(grad_out, gain_row, unit_rows, inverse):
    grad_unit = grad_out * gain_row
    centered = grad_unit - jnp.mean(grad_unit, axis=1, keepdims=True)
    return inverse * (centered - unit_rows * jnp.mean(grad_unit * unit_rows, axis=1, keepdims=True))


def gelu_value(preact):
    return 0.5 * preact * (1.0 + jax.scipy.special.erf(preact * INV_ROOT_TWO))


def gelu_slope(preact):
    return (
        0.5 * (1.0 + jax.scipy.special.erf(preact * INV_ROOT_TWO))
        + preact * jnp.exp(-0.5 * preact * preact) * INV_ROOT_TAU
    )


def attend_forward(operands):
    queries, key_rows, values = operands
    scores = jnp.einsum("hqd,hkd->hqk", queries, key_rows, preferred_element_type=jnp.float32)
    row_max = jnp.max(scores, axis=2, keepdims=True)
    exponent = jnp.exp(scores - row_max)
    row_total = jnp.sum(exponent, axis=2, keepdims=True)
    probability = (exponent / row_total).astype(jnp.bfloat16)
    context = jnp.einsum("hqk,hkd->hqd", probability, values, preferred_element_type=jnp.float32)
    return (context, row_max + jnp.log(row_total))


def attend_backward(operands):
    queries, key_rows, values, grad_context, log_total = operands
    scores = jnp.einsum("hqd,hkd->hqk", queries, key_rows, preferred_element_type=jnp.float32)
    probability = jnp.exp(scores - log_total)
    grad_prob = jnp.einsum("hqd,hkd->hqk", grad_context, values, preferred_element_type=jnp.float32)
    grad_values = jnp.einsum(
        "hqk,hqd->hkd",
        probability.astype(jnp.bfloat16),
        grad_context,
        preferred_element_type=jnp.float32,
    )
    spread = jnp.sum(probability * grad_prob, axis=2, keepdims=True)
    grad_scores = (probability * (grad_prob - spread)).astype(jnp.bfloat16)
    grad_queries = jnp.einsum(
        "hqk,hkd->hqd", grad_scores, key_rows, preferred_element_type=jnp.float32
    )
    grad_keys = jnp.einsum("hqk,hqd->hkd", grad_scores, queries, preferred_element_type=jnp.float32)
    return (
        grad_queries.astype(jnp.bfloat16),
        grad_keys.astype(jnp.bfloat16),
        grad_values.astype(jnp.bfloat16),
    )


def split_stack(stack_rows):
    return (
        stack_rows[0:MODEL_WIDTH],
        stack_rows[MODEL_WIDTH : 2 * MODEL_WIDTH],
        stack_rows[2 * MODEL_WIDTH : 3 * MODEL_WIDTH],
        stack_rows[3 * MODEL_WIDTH : 4 * MODEL_WIDTH],
        stack_rows[4 * MODEL_WIDTH : 4 * MODEL_WIDTH + FF],
        stack_rows[4 * MODEL_WIDTH + FF : 4 * MODEL_WIDTH + 2 * FF],
    )


def adam_step(parameter, moment_one, moment_two, gradient, rate):
    moment_one = FIRST_DECAY * moment_one + (1.0 - FIRST_DECAY) * gradient
    moment_two = SECOND_DECAY * moment_two + (1.0 - SECOND_DECAY) * gradient * gradient
    ascent = (
        moment_one
        / (1.0 - FIRST_DECAY**STEP)
        / (jnp.sqrt(moment_two / (1.0 - SECOND_DECAY**STEP)) + ADAM_EPSILON)
    )
    return (parameter - rate * (ascent + WEIGHT_DECAY * parameter), moment_one, moment_two)


def local(
    tokens,
    masked_pos,
    masked_count,
    out_grad,
    weights,
    vectors,
    owner_list,
    master_slots,
    first_slots,
    second_slots,
    vector_first,
    vector_second,
):
    page_count = masked_pos.shape[0]
    token_count = tokens.shape[0]
    up_rows = FF // MODEL_WIDTH
    gathered_stack = lax.all_gather(weights, "fsdp", axis=0, tiled=True)
    weight_query, weight_key, weight_value, weight_out, weight_up, weight_down = split_stack(
        gathered_stack
    )
    bias_query = vectors[0]
    bias_value = vectors[1]
    bias_out = vectors[2]
    bias_up = vectors[3 : 3 + up_rows].reshape(FF)
    bias_down = vectors[3 + up_rows]
    gain_one = vectors[4 + up_rows]
    shift_one = vectors[5 + up_rows]
    gain_two = vectors[6 + up_rows]
    shift_two = vectors[7 + up_rows]

    def heads_first(tensor):
        return tensor.reshape(page_count, PAGE, HEADS, HD).transpose(0, 2, 1, 3)

    def heads_joined(tensor):
        return tensor.transpose(0, 2, 1, 3).reshape(token_count, MODEL_WIDTH)

    token_float = tokens.astype(jnp.float32)
    queries = ((matmul(tokens, weight_query) + bias_query) * QUERY_SCALE).astype(jnp.bfloat16)
    key_rows = matmul(tokens, weight_key).astype(jnp.bfloat16)
    values = (matmul(tokens, weight_value) + bias_value).astype(jnp.bfloat16)
    query_heads = heads_first(queries)
    key_heads = heads_first(key_rows)
    value_heads = heads_first(values)
    context_heads, log_totals = lax.map(attend_forward, (query_heads, key_heads, value_heads))
    context = heads_joined(context_heads).astype(jnp.bfloat16)
    resid_one = token_float + matmul(context, weight_out) + bias_out
    hidden_one, unit_one, inverse_one = normalize(resid_one, gain_one, shift_one)
    hidden_low = hidden_one.astype(jnp.bfloat16)
    up_pre = times_last(hidden_low, weight_up) + bias_up
    activation = gelu_value(up_pre).astype(jnp.bfloat16)
    resid_two = hidden_one + matmul(activation, weight_down) + bias_down
    normed_two, unit_two, inverse_two = normalize(resid_two, gain_two, shift_two)
    layer_out = normed_two.astype(jnp.bfloat16)
    regathered = lax.all_gather(weights, "fsdp", axis=0, tiled=True)
    back_query, back_key, back_value, back_out, back_up, back_down = split_stack(regathered)
    live_slots = jnp.arange(MASKM, dtype=jnp.int32)[None, :] < masked_count[:, None]
    placed = (
        (masked_pos[:, :, None] == jnp.arange(PAGE, dtype=jnp.int32)[None, None, :])
        & live_slots[:, :, None]
    ).astype(jnp.bfloat16)
    cotangent = jnp.einsum(
        "pms,pmd->psd", placed, out_grad, preferred_element_type=jnp.float32
    ).reshape(token_count, MODEL_WIDTH)
    grad_resid_two = norm_backward(cotangent, gain_two, unit_two, inverse_two)
    grad_gain_two = jnp.sum(cotangent * unit_two, axis=0)
    grad_shift_two = jnp.sum(cotangent, axis=0)
    grad_down = grad_resid_two.astype(jnp.bfloat16)
    grad_bias_down = jnp.sum(grad_down, axis=0, dtype=jnp.float32)
    grad_weight_down = times_first(activation, grad_down)
    grad_up = (times_last(grad_down, back_down) * gelu_slope(up_pre)).astype(jnp.bfloat16)
    grad_bias_up = jnp.sum(grad_up, axis=0, dtype=jnp.float32).reshape(up_rows, MODEL_WIDTH)
    grad_weight_up = times_first(grad_up, hidden_low)
    grad_hidden = grad_resid_two + matmul(grad_up, back_up)
    grad_resid_one = norm_backward(grad_hidden, gain_one, unit_one, inverse_one)
    grad_gain_one = jnp.sum(grad_hidden * unit_one, axis=0)
    grad_shift_one = jnp.sum(grad_hidden, axis=0)
    grad_attn = grad_resid_one.astype(jnp.bfloat16)
    grad_bias_out = jnp.sum(grad_attn, axis=0, dtype=jnp.float32)
    grad_weight_out = times_first(context, grad_attn)
    grad_context = times_last(grad_attn, back_out).astype(jnp.bfloat16)
    query_back, key_back, value_back = lax.map(
        attend_backward,
        (query_heads, key_heads, value_heads, heads_first(grad_context), log_totals),
    )
    grad_queries = heads_joined(query_back) * QUERY_SCALE
    grad_keys = heads_joined(key_back)
    grad_values = heads_joined(value_back)
    grad_weight_query = times_first(tokens, grad_queries)
    grad_weight_key = times_first(tokens, grad_keys)
    grad_weight_value = times_first(tokens, grad_values)
    grad_bias_query = jnp.sum(grad_queries, axis=0, dtype=jnp.float32)
    grad_bias_value = jnp.sum(grad_values, axis=0, dtype=jnp.float32)
    token_grad = (
        grad_resid_one
        + times_last(grad_queries, back_query)
        + times_last(grad_keys, back_key)
        + times_last(grad_values, back_value)
    )
    grad_stack = jnp.concatenate(
        [
            grad_weight_query,
            grad_weight_key,
            grad_weight_value,
            grad_weight_out,
            grad_weight_up,
            grad_weight_down,
        ],
        axis=0,
    )
    grad_local_vectors = jnp.concatenate(
        [
            grad_bias_query[None],
            grad_bias_value[None],
            grad_bias_out[None],
            grad_bias_up,
            grad_bias_down[None],
            grad_gain_one[None],
            grad_shift_one[None],
            grad_gain_two[None],
            grad_shift_two[None],
        ],
        axis=0,
    )
    capacity = master_slots.shape[0]
    shard_rows = weights.shape[0]
    shard_blocks = shard_rows // BLOCK_ROWS
    fsdp_index = lax.axis_index("fsdp")
    block_ids = jnp.arange(NBLK, dtype=jnp.int32)
    same_owner = owner_list[:, None] == owner_list[None, :]
    block_rank = jnp.sum(
        (same_owner & (block_ids[None, :] < block_ids[:, None])).astype(jnp.int32), axis=1
    )
    block_slot_map = owner_list * capacity + block_rank
    grad_blocks = grad_stack.reshape(NBLK, BLOCK_ROWS, MODEL_WIDTH)
    wanted = jnp.arange(capacity * lax.axis_size("fsdp"), dtype=jnp.int32)
    match_flags = block_slot_map[:, None] == wanted[None, :]
    present = jnp.any(match_flags, axis=0)
    chosen = jnp.sum(jnp.where(match_flags, block_ids[:, None], 0), axis=0)
    owned_grad = lax.psum_scatter(
        jnp.where(present[:, None, None], jnp.take(grad_blocks, chosen, axis=0), 0.0).astype(
            jnp.bfloat16
        ),
        "fsdp",
        scatter_dimension=0,
        tiled=True,
    ).astype(jnp.float32)
    owned_grad = lax.psum(owned_grad.astype(jnp.bfloat16), "dp").astype(jnp.float32)
    vector_grad = lax.psum(grad_local_vectors, ("dp", "fsdp"))
    new_master, new_first, new_second = adam_step(
        master_slots, first_slots, second_slots, owned_grad, LEARN_RATE
    )
    new_vectors, new_vector_first, new_vector_second = adam_step(
        vectors, vector_first, vector_second, vector_grad, VECTOR_RATE
    )
    held_blocks = fsdp_index * shard_blocks + jnp.arange(shard_blocks, dtype=jnp.int32)
    held_slots = jnp.take(block_slot_map, held_blocks)
    blank_rows = jnp.zeros((shard_blocks, BLOCK_ROWS, MODEL_WIDTH), jnp.float32)
    shard_piece = lax.all_gather(
        new_master.astype(jnp.bfloat16), "fsdp", axis=0, tiled=True
    ).astype(jnp.float32)
    inside = (held_slots >= 0) & (held_slots < shard_piece.shape[0])
    picked = jnp.take(shard_piece, jnp.clip(held_slots, 0, shard_piece.shape[0] - 1), axis=0)
    new_weights = jnp.where(inside[:, None, None], picked, blank_rows).reshape(
        shard_rows, MODEL_WIDTH
    )
    return (
        layer_out,
        token_grad,
        new_weights,
        new_first,
        new_second,
        new_vectors,
        new_vector_first,
        new_vector_second,
    )


def solution(mesh):
    placed = (
        P(("dp", "fsdp"), None),
        P(("dp", "fsdp"), None),
        P(("dp", "fsdp")),
        P(("dp", "fsdp"), None, None),
        P("fsdp", None),
        P(),
        P(),
        P("fsdp", None, None),
        P("fsdp", None, None),
        P("fsdp", None, None),
        P(),
        P(),
    )
    return jax.shard_map(
        local,
        mesh=mesh,
        in_specs=placed,
        out_specs=(
            P(("dp", "fsdp"), None),
            P(("dp", "fsdp"), None),
            P("fsdp", None),
            P("fsdp", None, None),
            P("fsdp", None, None),
            P(),
            P(),
            P(),
        ),
        check_vma=False,
    )
```

profile of v0, /device:TPU:0, one launch (start us, length us, event | category | flops | bytes accessed | tf_op | source)
XLA Modules:
  0.0 1113.9 jit_solution(8871009478880002811)
XLA Ops:
  18.2 6.4 copy.115
  26.7 97.0 %all-gather.3.cloned.1.call-done = bf16[9216,768]{1,0:T(8,128)(2,1)} async-done(((bf16[576,768]{1,0:T(8,128)(2,1)}), bf16[9216,768]{1,0:T(8,128)(2,1)}) %all-gather.3.cloned.1.call-update) | async-done | bytes 14155792 | tf_op jit(solution)/shard_map/all_gather | solution.py:143
  170.4 132.6 %while.26 = (s32[]{:T(128)}, bf16[3,12,512,64]{3,2,1,0:T(8,128)(2,1)}, f32[3,12,512,1]{2,1,3,0:T(8,128)S(1)}, bf16[3,12,512,64]{2,0,3,1:T(4,128)(2,1)}, bf16[3,1...) while((s32[]{:T(128)}, bf16[3,12,512,64]{3,2,1,0:T(8,128)(2,1)}, ...), condition=%wide.region_3.4_spmd, body=%wide.region_0.3_spmd.sunk | while | flops 1217390592 | bytes 51290268 | solution.py:170
  177.3 7.8 constant_dynamic-slice_fusion.6
  192.9 14.8 %dot_general.106 = f32[12,512,64]{2,1,0:T(8,128)} custom-call(bf16[12,512,64]{2,1,0:T(8,128)(2,1)} %bitcast.172, bf16[12,512,64]{2,1,0:T(8,128)(2,1)} %bitcast.173, bf16[12,512,64]{2,1,0:T(8,128)(2,1)} %bitcast.174), custom_call_target="tpu_custom_call" | custom-call | flops 805306368 | bytes 2359296 | tf_op jit(solution)/shard_map/while/body/eval_jaxpr/hqk,hkd->hqd/dot_general | solution.py:76
  221.4 7.8 constant_dynamic-slice_fusion.6
  237.1 14.8 %dot_general.106 = f32[12,512,64]{2,1,0:T(8,128)} custom-call(bf16[12,512,64]{2,1,0:T(8,128)(2,1)} %bitcast.172, bf16[12,512,64]{2,1,0:T(8,128)(2,1)} %bitcast.173, bf16[12,512,64]{2,1,0:T(8,128)(2,1)} %bitcast.174), custom_call_target="tpu_custom_call" | custom-call | flops 805306368 | bytes 2359296 | tf_op jit(solution)/shard_map/while/body/eval_jaxpr/hqk,hkd->hqd/dot_general | solution.py:76
  265.6 7.8 constant_dynamic-slice_fusion.6
  281.2 14.8 %dot_general.106 = f32[12,512,64]{2,1,0:T(8,128)} custom-call(bf16[12,512,64]{2,1,0:T(8,128)(2,1)} %bitcast.172, bf16[12,512,64]{2,1,0:T(8,128)(2,1)} %bitcast.173, bf16[12,512,64]{2,1,0:T(8,128)(2,1)} %bitcast.174), custom_call_target="tpu_custom_call" | custom-call | flops 805306368 | bytes 2359296 | tf_op jit(solution)/shard_map/while/body/eval_jaxpr/hqk,hkd->hqd/dot_general | solution.py:76
  303.1 7.8 copy.113
  318.8 19.2 %multiply_convert_fusion.1 = (bf16[1536,3072]{1,0:T(8,128)(2,1)}, f32[1536,3072]{1,0:T(8,128)}) fusion(f32[3072]{0:T(1024)S(1)} %add.275, bf16[9216,768]{1,0:T(8,128)(2,1)} %all-gather.3.cloned.1.call-done, f32[1536,768]{0,1:T(8,128)S(1)} %get-tuple-element.244, f32[768]{0:T(1024)S(1)} %get-tuple-element.188, f32[768]{0:T(1024)S(1)} %get-tuple-element.189, ...), kind=kOutput, calls=%fused_computation.58 | convolution fusion | flops 7281967104 | bytes 37779456 | tf_op jit(solution)/shard_map/dot_general | solution.py:36
  338.0 13.8 %fusion.94 = (f32[1536]{0:T(1024)S(1)}, f32[1536,768]{0,1:T(8,128)S(1)}) fusion(f32[768]{0:T(1024)S(1)} %get-tuple-element.187, bf16[1536,3072]{1,0:T(8,128)(2,1)} %get-tuple-element.245, bf16[9216,768]{1,0:T(8,128)(2,1)} %all-gather.3.cloned.1.call-done, f32[768]{0:T(1024)S(1)} %get-tuple-element.188, f32[768]{0:T(1024)S(1)} %get-tuple-element.189, ...), kind=kOutput, calls=%fused_computation.175 | convolution fusion | flops 7256013312 | bytes 23620608 | tf_op jit(solution)/shard_map/dot_general | solution.py:32
  358.5 20.8 %convert_reduce_fusion = (f32[3072]{0:T(1024)}, bf16[1536,3072]{1,0:T(8,128)(2,1)}) fusion(f32[1536,3072]{1,0:T(8,128)} %get-tuple-element.246, f32[3072]{0:T(1024)S(1)} %add.275, bf16[9216,768]{1,0:T(8,128)(2,1)} %all-gather.3.cloned.1.call-done, f32[1536,768]{0,1:T(8,128)S(1)} %get-tuple-element.228), kind=kOutput, calls=%fused_computation.57 | convolution fusion | flops 7310275584 | bytes 37773312 | tf_op jit(solution)/shard_map/dot_general | solution.py:36
  379.3 16.0 %multiply_reduce_fusion.2 = (f32[768]{0:T(1024)}, f32[1536]{0:T(1024)S(1)}, f32[1536]{0:T(1024)S(1)}, f32[768]{0:T(1024)}, f32[1536,768]{0,1:T(8,128)}) fusion(f32[1536,768]{0,1:T(8,128)S(1)} %bitcast.184, f32[1536]{0:T(1024)S(1)} %add_rsqrt_fusion.1, f32[1536]{0:T(1024)S(1)} %broadcast_multiply_fusion.5, f32[768]{0:T(1024)S(1)} %get-tuple-element.189, ...), kind=kOutput, calls=%fused_computation.65 | convolution fusion | flops 7259548672 | bytes 28345344 | tf_op jit(solution)/shard_map/dot_general | solution.py:32
  417.4 92.8 %while.27 = (s32[]{:T(128)}, bf16[3,12,512,64]{2,3,1,0:T(8,128)(2,1)}, bf16[3,12,512,64]{2,3,1,0:T(8,128)(2,1)}, bf16[3,12,512,64]{2,3,1,0:T(8,128)(2,1)}, bf16[...) while((s32[]{:T(128)}, ...), condition=%wide.region_14.15_spmd, body=%wide.region_12.14_spmd.sunk | while | flops 2042750976 | bytes 121287840 | solution.py:207
  425.2 8.6 multiply_reduce_fusion.10
  433.8 6.8 multiply_convert_fusion.4
  455.9 8.6 multiply_reduce_fusion.10
  464.6 6.8 multiply_convert_fusion.4
  486.6 8.6 multiply_reduce_fusion.10
  495.3 6.8 multiply_convert_fusion.4
  533.6 14.2 %convolution_dynamic-update-slice_fusion.1 = bf16[9216,768]{1,0:T(8,128)(2,1)} fusion(bf16[9216,768]{1,0:T(8,128)(2,1)} %convolution_dynamic-update-slice_fusion.2, bf16[1536,3072]{1,0:T(8,128)(2,1)} %get-tuple-element.252, f32[1536,768]{0,1:T(8,128)S(1)} %bitcast.186, f32[768]{0:T(1024)S(1)} %copy-done.48, f32[768]{0:T(1024)S(1)} %copy-done.38, ...), kind=kOutput, calls=%fused_computation.61 | convolution fusion | flops 7253655552 | bytes 23611392 | tf_op jit(solution)/shard_map/dot_general | solution.py:40
  547.9 10.4 convolution_dynamic-update-slice_fusion
  558.3 19.3 %gather_fusion.1 = bf16[384,48,768]{2,1,0:T(8,128)(2,1)} fusion(bf16[192,48,768]{2,1,0:T(8,128)(2,1)} %bitcast.26, s32[1024]{0:T(1024)S(1)} %copy-done.45), kind=kCustom, calls=%fused_computation.1 | custom fusion | bytes 56624640 | tf_op jit(solution)/shard_map/jit(_take)/gather | solution.py:266
  577.6 20.2 %select_convert_fusion = bf16[384,48,768]{2,1,0:T(8,128)(2,1)} fusion(bf16[384,48,768]{2,1,0:T(8,128)(2,1)} %gather_fusion.1, pred[384]{0:T(512)(128)(4,1)S(1)} %copy-done.52, pred[384]{0:T(512)(128)(4,1)S(1)} %copy-done.53), kind=kLoop, calls=%fused_computation.49 | loop fusion | flops 28311552 | bytes 56623872 | tf_op jit(solution)/shard_map/convert_element_type | solution.py:266
  597.8 267.5 %reduce-scatter.2.cloned.1.call-done = bf16[24,48,768]{2,1,0:T(8,128)(2,1)} async-done(((bf16[384,48,768]{2,1,0:T(8,128)(2,1)}), bf16[24,48,768]{2,1,0:T(8,128)(2,1)}) %reduce-scatter.2.cloned.1.call-update) | async-done | bytes 1769488 | tf_op jit(solution)/shard_map/reduce_scatter | solution.py:265
  865.5 57.1 %all-reduce.2.cloned.1.call-done = bf16[24,48,768]{2,1,0:T(8,128)(2,1)} async-done(((bf16[24,48,768]{2,1,0:T(8,128)(2,1)}), bf16[24,48,768]{2,1,0:T(8,128)(2,1)}) %all-reduce.2.cloned.1.call-update) | async-done | bytes 1769488 | tf_op jit(solution)/shard_map/psum | solution.py:273
  922.6 8.2 subtract_convert_fusion
  953.3 6.1 copy.130
  959.4 40.5 %psum.15 = f32[12,768]{1,0:T(8,128)S(1)} all-reduce(f32[12,768]{1,0:T(8,128)S(1)} %concatenate.7), channel_id=1, replica_groups=mesh['dp'=2,'fsdp'=16] {'dp','fsdp'}, use_global_device_ids=true, to_apply=%region_29.30 | all-reduce | flops 9216 | bytes 73728 | tf_op jit(solution)/shard_map/psum | solution.py:274
  1000.6 74.9 %all-gather.5.cloned.1.call-done = bf16[384,48,768]{2,1,0:T(8,128)(2,1)} async-done(((bf16[24,48,768]{2,1,0:T(8,128)(2,1)}), bf16[384,48,768]{2,1,0:T(8,128)(2,1)}) %all-gather.5.cloned.1.call-update) | async-done | bytes 28311568 | tf_op jit(solution)/shard_map/all_gather | solution.py:284
  1075.5 27.8 %convert_element_type.114 = f32[384,48,768]{2,1,0:T(8,128)} convert(bf16[384,48,768]{2,1,0:T(8,128)(2,1)} %all-gather.5.cloned.1.call-done) | non-fusion elementwise | flops 14155776 | bytes 84934656 | tf_op jit(solution)/shard_map/convert_element_type | solution.py:286
  (299 shorter events, 256.6 us)
Async XLA Ops:
  7.2 116.5 %all-gather.3.cloned.1.call-start = ((), (), s32[]{:S(2)}) async-start(), calls=%async_computation.1 | async-start | bytes 15040512 | tf_op jit(solution)/shard_map/all_gather | solution.py:143
  8.0 857.4 %reduce-scatter.2.cloned.1.call-start = ((), (), s32[]{:S(2)}) async-start(), calls=%async_computation.2 | async-start | bytes 30081024 | tf_op jit(solution)/shard_map/reduce_scatter | solution.py:265
  13.7 324.3 %copy-start.47 = (f32[768]{0:T(1024)}, f32[768]{0:T(1024)S(1)}, u32[]{:S(2)}) copy-start(f32[768]{0:T(1024)S(1)} %get-tuple-element.188) | copy-start | bytes 9220
  13.7 381.6 %copy-start.37 = (f32[768]{0:T(1024)}, f32[768]{0:T(1024)S(1)}, u32[]{:S(2)}) copy-start(f32[768]{0:T(1024)S(1)} %get-tuple-element.189) | copy-start | bytes 9220
  18.1 105.5 %copy-start.15 = (bf16[1536,768]{1,0:T(8,128)(2,1)S(1)}, bf16[1536,768]{1,0:T(8,128)(2,1)}, u32[]{:S(2)}) copy-start(bf16[1536,768]{1,0:T(8,128)(2,1)} %param.16) | copy-start | bytes 7077892
  24.7 103.7 %copy-start.4 = (s32[192]{0:T(256)}, s32[192]{0:T(256)S(1)}, u32[]{:S(2)}) copy-start(s32[192]{0:T(256)S(1)} %multiply_add_fusion.3) | copy-start | bytes 2308
  318.2 19.8 %copy-start.6 = (f32[1536,768]{0,1:T(8,128)}, f32[1536,768]{0,1:T(8,128)S(1)}, u32[]{:S(2)}) copy-start(f32[1536,768]{0,1:T(8,128)S(1)} %get-tuple-element.244) | copy-start | bytes 14155780
  318.2 77.0 %copy-start.28 = (f32[1536]{0:T(1024)}, f32[1536]{0:T(1024)S(1)}, u32[]{:S(2)}) copy-start(f32[1536]{0:T(1024)S(1)} %broadcast_multiply_fusion.5) | copy-start | bytes 18436
  318.8 76.5 %copy-start.34 = (f32[1536]{0:T(1024)}, f32[1536]{0:T(1024)S(1)}, u32[]{:S(2)}) copy-start(f32[1536]{0:T(1024)S(1)} %add_rsqrt_fusion.1) | copy-start | bytes 18436
  338.0 14.4 %slice-start = ((s8[4718592]{0:T(1024)(128)(4,1)}), s8[4194304]{0:T(1024)(128)(4,1)S(1)}, s32[]{:S(2)}) async-start(s8[4718592]{0:T(1024)(128)(4,1)} %bitcast.181), calls=%async_computation.5 | async-start | bytes 8388608
  338.0 14.4 %slice-start.1 = ((s8[4718592]{0:T(1024)(128)(4,1)}), s8[524288]{0:T(1024)(128)(4,1)S(1)}, s32[]{:S(2)}) async-start(s8[4718592]{0:T(1024)(128)(4,1)} %bitcast.181), calls=%async_computation.6 | async-start | bytes 1048576
  354.5 24.8 %slice-start.2 = ((s8[4718592]{0:T(1024)(128)(4,1)}), s8[524288]{0:T(1024)(128)(4,1)S(1)}, s32[]{:S(2)}) async-start(s8[4718592]{0:T(1024)(128)(4,1)} %bitcast.183), calls=%async_computation.7 | async-start | bytes 1048576
  358.4 20.8 %copy-start.14 = (f32[1536,768]{0,1:T(8,128)}, f32[1536,768]{0,1:T(8,128)S(1)}, u32[]{:S(2)}) copy-start(f32[1536,768]{0,1:T(8,128)S(1)} %get-tuple-element.228) | copy-start | bytes 14155780
  358.4 20.8 %slice-start.3 = ((s8[4718592]{0:T(1024)(128)(4,1)}), s8[4194304]{0:T(1024)(128)(4,1)S(1)}, s32[]{:S(2)}) async-start(s8[4718592]{0:T(1024)(128)(4,1)} %bitcast.183), calls=%async_computation.8 | async-start | bytes 8388608
  530.5 17.4 %slice-start.10 = ((s8[4718592]{0:T(1024)(128)(4,1)}), s8[4194304]{0:T(1024)(128)(4,1)S(1)}, s32[]{:S(2)}) async-start(s8[4718592]{0:T(1024)(128)(4,1)} %bitcast.201), calls=%async_computation.15 | async-start | bytes 8388608
  530.5 17.4 %slice-start.12 = ((s8[9437184]{0:T(1024)(128)(4,1)}), s8[4194304]{0:T(1024)(128)(4,1)S(1)}, s32[]{:S(2)}) async-start(s8[9437184]{0:T(1024)(128)(4,1)} %bitcast.210), calls=%async_computation.17 | async-start | bytes 8388608
  533.6 14.3 %slice-start.11 = ((s8[4718592]{0:T(1024)(128)(4,1)}), s8[524288]{0:T(1024)(128)(4,1)S(1)}, s32[]{:S(2)}) async-start(s8[4718592]{0:T(1024)(128)(4,1)} %bitcast.201), calls=%async_computation.16 | async-start | bytes 1048576
  533.6 14.3 %slice-start.13 = ((s8[9437184]{0:T(1024)(128)(4,1)}), s8[4194304]{0:T(1024)(128)(4,1)S(1)}, s32[]{:S(2)}) async-start(s8[9437184]{0:T(1024)(128)(4,1)} %bitcast.210), calls=%async_computation.18 | async-start | bytes 8388608
  533.6 14.3 %slice-start.14 = ((s8[9437184]{0:T(1024)(128)(4,1)}), s8[1048576]{0:T(1024)(128)(4,1)S(1)}, s32[]{:S(2)}) async-start(s8[9437184]{0:T(1024)(128)(4,1)} %bitcast.210), calls=%async_computation.19 | async-start | bytes 2097152
  558.3 19.3 %copy-start.52 = (pred[384]{0:T(512)(128)(4,1)S(1)}, pred[384]{0:T(512)(128)(4,1)}, u32[]{:S(2)}) copy-start(pred[384]{0:T(512)(128)(4,1)} %compare_and_fusion) | copy-start | bytes 1156
  558.3 19.3 %copy-start.53 = (pred[384]{0:T(512)(128)(4,1)S(1)}, pred[384]{0:T(512)(128)(4,1)}, u32[]{:S(2)}) copy-start(pred[384]{0:T(512)(128)(4,1)} %fusion.77) | copy-start | bytes 1156
  597.8 324.8 %all-reduce.2.cloned.1.call-start = ((), (), s32[]{:S(2)}) async-start(), calls=%async_computation.3 | async-start | bytes 3538944 | tf_op jit(solution)/shard_map/psum | solution.py:273
  865.4 65.5 %copy-start.5 = (s32[192]{0:T(256)S(1)}, s32[192]{0:T(256)}, u32[]{:S(2)}) copy-start(s32[192]{0:T(256)} %copy-done.4) | copy-start | bytes 2308
  865.4 66.7 %copy-start.41 = (f32[768]{0:T(1024)S(1)}, f32[768]{0:T(1024)}, u32[]{:S(2)}) copy-start(f32[768]{0:T(1024)} %get-tuple-element.183) | copy-start | bytes 9220
  865.4 66.8 %copy-start.39 = (f32[768]{0:T(1024)S(1)}, f32[768]{0:T(1024)}, u32[]{:S(2)}) copy-start(f32[768]{0:T(1024)} %get-tuple-element.178) | copy-start | bytes 9220
  865.4 66.8 %copy-start.44 = (f32[3072]{0:T(1024)S(1)}, f32[3072]{0:T(1024)}, u32[]{:S(2)}) copy-start(f32[3072]{0:T(1024)} %get-tuple-element.251) | copy-start | bytes 36868
  865.4 66.8 %copy-start.43 = (f32[768]{0:T(1024)S(1)}, f32[768]{0:T(1024)}, u32[]{:S(2)}) copy-start(f32[768]{0:T(1024)} %get-tuple-element.227) | copy-start | bytes 9220
  865.5 210.1 %all-gather.5.cloned.1.call-start = ((), (), s32[]{:S(2)}) async-start(), calls=%async_computation.4 | async-start | bytes 30081024 | tf_op jit(solution)/shard_map/all_gather | solution.py:284
  953.3 46.7 %copy-start.27 = (f32[12,768]{1,0:T(8,128)S(1)}, f32[12,768]{1,0:T(8,128)}, u32[]{:S(2)}) copy-start(f32[12,768]{1,0:T(8,128)} %param.21) | copy-start | bytes 110596
  953.3 46.7 %copy-start.32 = (f32[12,768]{1,0:T(8,128)S(1)}, f32[12,768]{1,0:T(8,128)}, u32[]{:S(2)}) copy-start(f32[12,768]{1,0:T(8,128)} %param.26) | copy-start | bytes 110596
  953.3 46.7 %copy-start.33 = (f32[12,768]{1,0:T(8,128)S(1)}, f32[12,768]{1,0:T(8,128)}, u32[]{:S(2)}) copy-start(f32[12,768]{1,0:T(8,128)} %param.27) | copy-start | bytes 110596
  1075.5 31.4 %copy-start.1 = (bf16[3,104,768]{2,1,0:T(8,128)(2,1)S(1)}, bf16[3,104,768]{2,1,0:T(8,128)(2,1)}, u32[]{:S(2)}) copy-start(bf16[3,104,768]{2,1,0:T(8,128)(2,1)} %param.19) | copy-start | bytes 1437700
  (50 other events, 213.2 us)
Sparse Core Ops, SparseCore 0:
  10.3 113.3 all-gather.2
  597.9 267.4 reduce-scatter.1
  867.7 54.8 all-reduce.1
  931.0 144.4 all-gather.4
where the time goes:
time: 1120 us; the launch traced here: 1110 us
  waiting for transfers between devices  497 us (44%)
  matrix products  220 us (20%)
  local copies, waits for them, and re-layouts  192 us (17%)
  other arithmetic  103 us (9%)
  Pallas kernels  44.4 us (4%)
  blocking collectives  40.5 us (4%)
  between operations  15.1 us (1%)
    reduce_scatter x1, waiting for transfers between devices, local(): lax.psum_scatter(jnp.where(present[:, None, None], jnp.take(grad_blocks,...  268 us
    all_gather x1, waiting for transfers between devices, local(): gathered_stack = lax.all_gather(weights, 'fsdp', axis=0, tiled=True)  97 us
    all_gather x1, waiting for transfers between devices, local(): lax.all_gather(new_master.astype(jnp.bfloat16), 'fsdp', axis=0, tiled=True)  74.9 us
    dynamic_slice x15, local copies, waits for them, and re-layouts, local(): lax.map(attend_forward, (query_heads, key_heads, value_heads))  66.7 us
    dot_general x6, matrix products, times_last(): lax.dot_general(left_side, right_side, CONTRACT_LAST, preferred_element_t...  58 us
    psum x1, waiting for transfers between devices, local(): lax.psum(owned_grad.astype(jnp.bfloat16), 'dp').astype(jnp.float32)  57.1 us
    dot_general x6, matrix products, matmul(): return jnp.dot(left_side, right_side, preferred_element_type=jnp.float32)  48.4 us
    dot_general x3, Pallas kernels, attend_forward(): jnp.einsum('hqk,hkd->hqd', probability, values, preferred_element_type=jn...  44.4 us
  transfers between devices with their start and end apart: 4, of which 4 were waited for; matrix products, arithmetic and copies ran while one was open for 4% of the time, Pallas kernels for 0%

commit v1 on v0

v1 whole, which is shorter than its diff:
```python
import functools

import jax
import jax.numpy as jnp
from jax import lax
from jax.experimental import pallas as pl
from jax.experimental.pallas import tpu as pltpu
from jax.sharding import PartitionSpec as P

WIDTH = 768
HEADS = 12
HD = 64
FF = 3072
PAGE = 512
MASKM = 104
ROWS = 48
STEP = 10
NBLK = 192
PAD = 128
UP_ROWS = FF // WIDTH

QUERY_SCALE = 0.125
NORM_EPSILON = 1e-06
INV_ROOT_TWO = 0.7071067811865476
INV_ROOT_TAU = 0.3989422804014327
FIRST_DECAY = 0.5
SECOND_DECAY = 0.5
LEARN_RATE = 0.05
VECTOR_RATE = 0.3
WEIGHT_DECAY = 0.01
ADAM_EPSILON = 1e-08

BF = jnp.bfloat16
F32 = jnp.float32
VMEM_LIMIT = 60 * 1024 * 1024
ANY = pl.BlockSpec(memory_space=pl.ANY)


def mm(a, b):
    return lax.dot_general(a, b, (((1,), (0,)), ((), ())), preferred_element_type=F32)


def mm_last(a, b):
    return lax.dot_general(a, b, (((1,), (1,)), ((), ())), preferred_element_type=F32)


def mm_first(a, b):
    return lax.dot_general(a, b, (((0,), (0,)), ((), ())), preferred_element_type=F32)


def row_sum(x):
    return jnp.sum(x, axis=0, keepdims=True)


def unit_of(x):
    center = x - jnp.mean(x, axis=1, keepdims=True)
    inverse = lax.rsqrt(jnp.mean(center * center, axis=1, keepdims=True) + NORM_EPSILON)
    return center * inverse, inverse


def unit_back(grad_out, gain, unit, inverse):
    grad_unit = grad_out * gain
    centered = grad_unit - jnp.mean(grad_unit, axis=1, keepdims=True)
    return inverse * (centered - unit * jnp.mean(grad_unit * unit, axis=1, keepdims=True))


def gelu_cdf(u):
    return 0.5 * (1.0 + lax.erf(u * INV_ROOT_TWO))


def half_masks():
    lane = lax.broadcasted_iota(jnp.int32, (1, 2 * HD), 1)
    low = jnp.where(lane < HD, 1.0, 0.0)
    return (low.astype(BF), (1.0 - low).astype(BF)), lane < HD


def softmax(scores):
    top = jnp.max(scores, axis=1, keepdims=True)
    exponent = jnp.exp(scores - top)
    total = jnp.sum(exponent, axis=1, keepdims=True)
    return exponent * (1.0 / total)


def one_hot_rows(pos):
    return jnp.where(
        pos == lax.broadcasted_iota(jnp.int32, (PAD, PAGE), 1), 1.0, 0.0
    ).astype(BF)


def project_kernel(
    pos_ref, tok_ref, vec_ref, w_any, q_ref, k_ref, v_ref, tm_ref, qm_ref, cm_ref, w_ref, sem
):
    @pl.when(pl.program_id(0) == 0)
    def _():
        copy = pltpu.make_async_copy(w_any.at[pl.ds(0, 3 * WIDTH)], w_ref, sem)
        copy.start()
        copy.wait()

    tok = tok_ref[...]
    q = ((mm(tok, w_ref[0:WIDTH]) + vec_ref[0:1]) * QUERY_SCALE).astype(BF)
    k = mm(tok, w_ref[WIDTH : 2 * WIDTH]).astype(BF)
    v = (mm(tok, w_ref[2 * WIDTH : 3 * WIDTH]) + vec_ref[1:2]).astype(BF)
    q_ref[...] = q
    k_ref[...] = k
    v_ref[...] = v
    pick = one_hot_rows(pos_ref[0])
    tm_ref[...] = mm(pick, tok).astype(BF)
    qm = mm(pick, q).astype(BF)
    qm_ref[...] = qm
    masks, low = half_masks()
    for pair in range(HEADS // 2):
        cols = slice(pair * 2 * HD, (pair + 1) * 2 * HD)
        kp, vp, qp = k[:, cols], v[:, cols], qm[:, cols]
        parts = []
        for mask in masks:
            prob = softmax(mm_last(qp * mask, kp)).astype(BF)
            parts.append(mm(prob, vp))
        cm_ref[:, cols] = jnp.where(low, parts[0], parts[1]).astype(BF)


def project(tokens, pos, vectors, stack):
    pages = tokens.shape[0] // PAGE
    tall = jax.ShapeDtypeStruct((pages * PAGE, WIDTH), BF)
    short = jax.ShapeDtypeStruct((pages * PAD, WIDTH), BF)
    page = pl.BlockSpec((PAGE, WIDTH), lambda i: (i, 0))
    few = pl.BlockSpec((PAD, WIDTH), lambda i: (i, 0))
    return pl.pallas_call(
        project_kernel,
        grid=(pages,),
        in_specs=[
            pl.BlockSpec((1, PAD, 1), lambda i: (i, 0, 0)),
            page,
            pl.BlockSpec((12, WIDTH), lambda i: (0, 0)),
            ANY,
        ],
        out_specs=[page, page, page, few, few, few],
        out_shape=[tall, tall, tall, short, short, short],
        scratch_shapes=[pltpu.VMEM((3 * WIDTH, WIDTH), BF), pltpu.SemaphoreType.DMA],
        compiler_params=pltpu.CompilerParams(vmem_limit_bytes=VMEM_LIMIT),
        name="project",
    )(pos, tokens, vectors, stack)


def masked_kernel(
    place_ref,
    tm_ref,
    cm_ref,
    cot_ref,
    vec_ref,
    w_any,
    gr_ref,
    gc_ref,
    gv_ref,
    dw_any,
    w_ref,
    up_ref,
    act_ref,
    hid_ref,
    stage_ref,
    in_sem,
    out_sem,
):
    parts = 1 + 2 * UP_ROWS
    loads = [
        pltpu.make_async_copy(
            w_any.at[pl.ds((3 + i) * WIDTH, WIDTH)], w_ref.at[i], in_sem.at[i]
        )
        for i in range(parts)
    ]
    for load in loads:
        load.start()
    per = WIDTH // ROWS

    def send(part, value):
        stage_ref[pl.ds(part * per, per)] = value.astype(BF).reshape(per, ROWS, WIDTH)

        @pl.loop(0, per)
        def _(i):
            block = part * per + i
            pltpu.make_async_copy(
                stage_ref.at[block], dw_any.at[place_ref[3 * per + block]], out_sem
            ).start()

    gain_one, shift_one = vec_ref[8:9], vec_ref[9:10]
    gain_two = vec_ref[10:11]
    cm = cm_ref[...]
    loads[0].wait()
    resid_one = tm_ref[...].astype(F32) + mm(cm, w_ref[0]) + vec_ref[2:3]
    unit_one, inv_one = unit_of(resid_one)
    hidden_one = unit_one * gain_one + shift_one
    hid_ref[...] = hidden_one.astype(BF)
    hid = hid_ref[...]
    for c in range(UP_ROWS):
        cols = slice(c * WIDTH, (c + 1) * WIDTH)
        loads[1 + c].wait()
        up = mm_last(hid, w_ref[1 + c]) + vec_ref[3 + c : 4 + c]
        up_ref[:, cols] = up
        act_ref[:, cols] = (up * gelu_cdf(up)).astype(BF)
    resid_two = hidden_one + vec_ref[7:8]
    for c in range(UP_ROWS):
        cols = slice(c * WIDTH, (c + 1) * WIDTH)
        loads[1 + UP_ROWS + c].wait()
        resid_two = resid_two + mm(act_ref[:, cols], w_ref[1 + UP_ROWS + c])
    unit_two, inv_two = unit_of(resid_two)
    cot = cot_ref[...].astype(F32)
    grad_two = unit_back(cot, gain_two, unit_two, inv_two)
    gv_ref[...] = jnp.zeros_like(gv_ref)
    gv_ref[10:11] = row_sum(cot * unit_two)
    gv_ref[11:12] = row_sum(cot)
    down = grad_two.astype(BF)
    gv_ref[7:8] = row_sum(down.astype(F32))
    grad_hidden = grad_two
    for c in range(UP_ROWS):
        cols = slice(c * WIDTH, (c + 1) * WIDTH)
        send(1 + UP_ROWS + c, mm_first(act_ref[:, cols], down))
        up = up_ref[:, cols]
        slope = gelu_cdf(up) + up * jnp.exp(-0.5 * up * up) * INV_ROOT_TAU
        grad_up = (mm_last(down, w_ref[1 + UP_ROWS + c]) * slope).astype(BF)
        gv_ref[3 + c : 4 + c] = row_sum(grad_up.astype(F32))
        send(1 + c, mm_first(grad_up, hid))
        grad_hidden = grad_hidden + mm(grad_up, w_ref[1 + c])
    gv_ref[8:9] = row_sum(grad_hidden * unit_one)
    gv_ref[9:10] = row_sum(grad_hidden)
    grad_one = unit_back(grad_hidden, gain_one, unit_one, inv_one)
    gr_ref[...] = grad_one
    attn = grad_one.astype(BF)
    gv_ref[2:3] = row_sum(attn.astype(F32))
    send(0, mm_first(cm, attn))
    gc_ref[...] = mm_last(attn, w_ref[0]).astype(BF)
    total = parts * per
    pltpu.make_async_copy(stage_ref, dw_any.at[pl.ds(0, total)], out_sem).wait()


def masked_part(place, tm, cm, cot, vectors, stack):
    rows = tm.shape[0]
    parts = 1 + 2 * UP_ROWS
    vm = pl.BlockSpec(memory_space=pltpu.VMEM)
    return pl.pallas_call(
        masked_kernel,
        grid_spec=pltpu.PrefetchScalarGridSpec(
            num_scalar_prefetch=1,
            grid=(),
            in_specs=[vm, vm, vm, vm, ANY],
            out_specs=[vm, vm, vm, ANY],
            scratch_shapes=[
                pltpu.VMEM((parts, WIDTH, WIDTH), BF),
                pltpu.VMEM((rows, FF), F32),
                pltpu.VMEM((rows, FF), BF),
                pltpu.VMEM((rows, WIDTH), BF),
                pltpu.VMEM((parts * WIDTH // ROWS, ROWS, WIDTH), BF),
                pltpu.SemaphoreType.DMA((parts,)),
                pltpu.SemaphoreType.DMA,
            ],
        ),
        out_shape=[
            jax.ShapeDtypeStruct((rows, WIDTH), F32),
            jax.ShapeDtypeStruct((rows, WIDTH), BF),
            jax.ShapeDtypeStruct((16, WIDTH), F32),
            jax.ShapeDtypeStruct((NBLK, ROWS, WIDTH), BF),
        ],
        compiler_params=pltpu.CompilerParams(vmem_limit_bytes=VMEM_LIMIT),
        name="masked",
    )(place, tm, cm, cot, vectors, stack)


def attention_back_kernel(
    place_ref,
    tok_ref,
    k_ref,
    v_ref,
    tm_ref,
    qm_ref,
    gc_ref,
    dw_in,
    dq_ref,
    dk_ref,
    dv_ref,
    gv_ref,
    dw_any,
    sum_ref,
    stage_ref,
    out_sem,
):
    page, last = pl.program_id(0), pl.num_programs(0) - 1
    per = WIDTH // ROWS
    masks, low = half_masks()

    @pl.when(page == 0)
    def _():
        sum_ref[...] = jnp.zeros_like(sum_ref)
        gv_ref[...] = jnp.zeros_like(gv_ref)

    for pair in range(HEADS // 2):
        cols = slice(pair * 2 * HD, (pair + 1) * 2 * HD)
        kp, vp, qp, gp = k_ref[:, cols], v_ref[:, cols], qm_ref[:, cols], gc_ref[:, cols]
        grad_v, grad_k, grad_q = None, None, []
        for mask in masks:
            qh, gh = qp * mask, gp * mask
            prob = softmax(mm_last(qh, kp))
            grad_prob = mm_last(gh, vp)
            spread = jnp.sum(prob * grad_prob, axis=1, keepdims=True)
            grad_s = (prob * (grad_prob - spread)).astype(BF)
            one_v = mm_first(prob.astype(BF), gh)
            one_k = mm_first(grad_s, qh)
            grad_v = one_v if grad_v is None else grad_v + one_v
            grad_k = one_k if grad_k is None else grad_k + one_k
            grad_q.append(mm(grad_s, kp))
        dv_ref[:, cols] = grad_v.astype(BF)
        dk_ref[:, cols] = grad_k.astype(BF)
        dq_ref[:, cols] = jnp.where(low, grad_q[0], grad_q[1]).astype(BF) * QUERY_SCALE
    dq, dk, dv = dq_ref[...], dk_ref[...], dv_ref[...]
    gv_ref[0:1] += row_sum(dq.astype(F32))
    gv_ref[1:2] += row_sum(dv.astype(F32))
    tok = tok_ref[...]
    sum_ref[0] += mm_first(tm_ref[...], dq)
    sum_ref[1] += mm_first(tok, dk)
    sum_ref[2] += mm_first(tok, dv)

    @pl.when(page == last)
    def _():
        for i in range(3):
            stage_ref[pl.ds(i * per, per)] = (
                sum_ref[i].astype(BF).reshape(per, ROWS, WIDTH)
            )

        @pl.loop(0, 3 * per)
        def _(i):
            pltpu.make_async_copy(
                stage_ref.at[i], dw_any.at[place_ref[i]], out_sem
            ).start()

        pltpu.make_async_copy(stage_ref, dw_any.at[pl.ds(0, 3 * per)], out_sem).wait()


def attention_back(place, tokens, k, v, tm, qm, gc, dw):
    pages = tokens.shape[0] // PAGE
    page = pl.BlockSpec((PAGE, WIDTH), lambda i, s: (i, 0))
    few = pl.BlockSpec((PAD, WIDTH), lambda i, s: (i, 0))
    tall = jax.ShapeDtypeStruct((pages * PAGE, WIDTH), BF)
    return pl.pallas_call(
        attention_back_kernel,
        grid_spec=pltpu.PrefetchScalarGridSpec(
            num_scalar_prefetch=1,
            grid=(pages,),
            in_specs=[page, page, page, few, few, few, ANY],
            out_specs=[few, page, page, pl.BlockSpec((8, WIDTH), lambda i, s: (0, 0)), ANY],
            scratch_shapes=[
                pltpu.VMEM((3, WIDTH, WIDTH), F32),
                pltpu.VMEM((3 * WIDTH // ROWS, ROWS, WIDTH), BF),
                pltpu.SemaphoreType.DMA,
            ],
        ),
        out_shape=[
            jax.ShapeDtypeStruct((pages * PAD, WIDTH), BF),
            tall,
            tall,
            jax.ShapeDtypeStruct((8, WIDTH), F32),
            jax.ShapeDtypeStruct(dw.shape, BF),
        ],
        input_output_aliases={7: 4},
        compiler_params=pltpu.CompilerParams(vmem_limit_bytes=VMEM_LIMIT),
        name="attention_back",
    )(place, tokens, k, v, tm, qm, gc, dw)


def forward_kernel(tok_ref, q_ref, k_ref, v_ref, vec_ref, w_any, out_ref, w_ref, ctx_ref, sem):
    parts = 1 + 2 * UP_ROWS

    @pl.when(pl.program_id(0) == 0)
    def _():
        pltpu.make_async_copy(w_any.at[pl.ds(3 * WIDTH, parts * WIDTH)], w_ref, sem).start()

    masks, low = half_masks()
    for pair in range(HEADS // 2):
        cols = slice(pair * 2 * HD, (pair + 1) * 2 * HD)
        kp, vp, qp = k_ref[:, cols], v_ref[:, cols], q_ref[:, cols]
        halves = []
        for mask in masks:
            prob = softmax(mm_last(qp * mask, kp)).astype(BF)
            halves.append(mm(prob, vp))
        ctx_ref[:, cols] = jnp.where(low, halves[0], halves[1]).astype(BF)

    @pl.when(pl.program_id(0) == 0)
    def _():
        pltpu.make_async_copy(w_any.at[pl.ds(3 * WIDTH, parts * WIDTH)], w_ref, sem).wait()

    resid_one = tok_ref[...].astype(F32) + mm(ctx_ref[...], w_ref[0:WIDTH]) + vec_ref[2:3]
    unit_one, _ = unit_of(resid_one)
    hidden_one = unit_one * vec_ref[8:9] + vec_ref[9:10]
    hid = hidden_one.astype(BF)
    resid_two = hidden_one + vec_ref[7:8]
    for c in range(UP_ROWS):
        at, to = (1 + c) * WIDTH, (1 + UP_ROWS + c) * WIDTH
        up = mm_last(hid, w_ref[at : at + WIDTH]) + vec_ref[3 + c : 4 + c]
        act = (up * gelu_cdf(up)).astype(BF)
        resid_two = resid_two + mm(act, w_ref[to : to + WIDTH])
    unit_two, _ = unit_of(resid_two)
    out_ref[...] = (unit_two * vec_ref[10:11] + vec_ref[11:12]).astype(BF)


def forward_rest(tokens, q, k, v, vectors, stack):
    pages = tokens.shape[0] // PAGE
    page = pl.BlockSpec((PAGE, WIDTH), lambda i: (i, 0))
    return pl.pallas_call(
        forward_kernel,
        grid=(pages,),
        in_specs=[page, page, page, page, pl.BlockSpec((12, WIDTH), lambda i: (0, 0)), ANY],
        out_specs=page,
        out_shape=jax.ShapeDtypeStruct(tokens.shape, BF),
        scratch_shapes=[
            pltpu.VMEM(((1 + 2 * UP_ROWS) * WIDTH, WIDTH), BF),
            pltpu.VMEM((PAGE, WIDTH), BF),
            pltpu.SemaphoreType.DMA,
        ],
        compiler_params=pltpu.CompilerParams(vmem_limit_bytes=VMEM_LIMIT),
        name="forward_rest",
    )(tokens, q, k, v, vectors, stack)


def input_grad_kernel(pos_ref, dq_ref, dk_ref, dv_ref, gr_ref, w_any, out_ref, w_ref, sem):
    @pl.when(pl.program_id(0) == 0)
    def _():
        copy = pltpu.make_async_copy(w_any.at[pl.ds(0, 3 * WIDTH)], w_ref, sem)
        copy.start()
        copy.wait()

    few = gr_ref[...] + mm_last(dq_ref[...], w_ref[0:WIDTH])
    high = few.astype(BF)
    rest = (few - high.astype(F32)).astype(BF)
    pick = one_hot_rows(pos_ref[0])
    out_ref[...] = (
        mm_last(dk_ref[...], w_ref[WIDTH : 2 * WIDTH])
        + mm_last(dv_ref[...], w_ref[2 * WIDTH : 3 * WIDTH])
        + (mm_first(pick, high) + mm_first(pick, rest))
    )


def input_grad(pos, dq, dk, dv, gr, stack):
    pages = dk.shape[0] // PAGE
    page = pl.BlockSpec((PAGE, WIDTH), lambda i: (i, 0))
    few = pl.BlockSpec((PAD, WIDTH), lambda i: (i, 0))
    return pl.pallas_call(
        input_grad_kernel,
        grid=(pages,),
        in_specs=[pl.BlockSpec((1, PAD, 1), lambda i: (i, 0, 0)), few, page, page, few, ANY],
        out_specs=page,
        out_shape=jax.ShapeDtypeStruct(dk.shape, F32),
        scratch_shapes=[pltpu.VMEM((3 * WIDTH, WIDTH), BF), pltpu.SemaphoreType.DMA],
        compiler_params=pltpu.CompilerParams(vmem_limit_bytes=VMEM_LIMIT),
        name="input_grad",
    )(pos, dq, dk, dv, gr, stack)


def adam_step(parameter, moment_one, moment_two, gradient, rate):
    moment_one = FIRST_DECAY * moment_one + (1.0 - FIRST_DECAY) * gradient
    moment_two = SECOND_DECAY * moment_two + (1.0 - SECOND_DECAY) * gradient * gradient
    ascent = (
        moment_one
        / (1.0 - FIRST_DECAY**STEP)
        / (jnp.sqrt(moment_two / (1.0 - SECOND_DECAY**STEP)) + ADAM_EPSILON)
    )
    return (parameter - rate * (ascent + WEIGHT_DECAY * parameter), moment_one, moment_two)


def weight_step_kernel(from_ref, grad_ref, state_ref, out_ref):
    new, _, _ = adam_step(
        state_ref[0, 0].astype(F32),
        state_ref[0, 1].astype(F32),
        state_ref[0, 2].astype(F32),
        grad_ref[0].astype(F32),
        LEARN_RATE,
    )
    out_ref[0] = new.astype(BF)


def weight_step(source, grads, states):
    return pl.pallas_call(
        weight_step_kernel,
        grid_spec=pltpu.PrefetchScalarGridSpec(
            num_scalar_prefetch=1,
            grid=(grads.shape[0],),
            in_specs=[
                pl.BlockSpec((1, ROWS, WIDTH), lambda i, s: (i, 0, 0)),
                pl.BlockSpec((1, 3, ROWS, WIDTH), lambda i, s: (s[i], 0, 0, 0)),
            ],
            out_specs=pl.BlockSpec((1, ROWS, WIDTH), lambda i, s: (i, 0, 0)),
        ),
        out_shape=jax.ShapeDtypeStruct(grads.shape, BF),
        name="weight_step",
    )(source, grads, states)


def moment_step_kernel(from_ref, live_ref, grad_ref, first_ref, second_ref, one_ref, two_ref):
    live = live_ref[pl.program_id(0)] > 0
    grad = jnp.where(live, grad_ref[0].astype(F32), 0.0)
    one_ref[0] = FIRST_DECAY * first_ref[0] + (1.0 - FIRST_DECAY) * grad
    two_ref[0] = SECOND_DECAY * second_ref[0] + (1.0 - SECOND_DECAY) * grad * grad


def moment_step(source, live, grads, first, second):
    slot = pl.BlockSpec((1, ROWS, WIDTH), lambda i, s, n: (i, 0, 0))
    shape = jax.ShapeDtypeStruct(first.shape, F32)
    return pl.pallas_call(
        moment_step_kernel,
        grid_spec=pltpu.PrefetchScalarGridSpec(
            num_scalar_prefetch=2,
            grid=(first.shape[0],),
            in_specs=[
                pl.BlockSpec((1, ROWS, WIDTH), lambda i, s, n: (s[i], 0, 0)),
                slot,
                slot,
            ],
            out_specs=[slot, slot],
        ),
        out_shape=[shape, shape],
        name="moment_step",
    )(source, live, grads, first, second)


def take_kernel(from_ref, in_ref, out_ref):
    out_ref[0] = in_ref[0].astype(F32)


def take_blocks(source, blocks):
    count = source.shape[0]
    return pl.pallas_call(
        take_kernel,
        grid_spec=pltpu.PrefetchScalarGridSpec(
            num_scalar_prefetch=1,
            grid=(count,),
            in_specs=[pl.BlockSpec((1, ROWS, WIDTH), lambda i, s: (s[i], 0, 0))],
            out_specs=pl.BlockSpec((1, ROWS, WIDTH), lambda i, s: (i, 0, 0)),
        ),
        out_shape=jax.ShapeDtypeStruct((count, ROWS, WIDTH), F32),
        name="take_blocks",
    )(source, blocks)


def local(
    groups,
    tokens,
    masked_pos,
    masked_count,
    out_grad,
    weights,
    vectors,
    owner_list,
    master_slots,
    first_slots,
    second_slots,
    vector_first,
    vector_second,
):
    pages = masked_pos.shape[0]
    capacity = master_slots.shape[0]
    held = weights.shape[0] // ROWS
    spread = lax.axis_size("fsdp")
    me_f = lax.axis_index("fsdp")
    ids = groups * spread
    each = NBLK // ids
    lanes = -(-capacity // ids)
    base = lax.axis_index("dp") * spread if groups > 1 else 0
    me = base + me_f

    blocks = jnp.arange(NBLK, dtype=jnp.int32)
    lower = owner_list[None, :] < owner_list[:, None]
    tied = (owner_list[None, :] == owner_list[:, None]) & (blocks[None, :] < blocks[:, None])
    rank = jnp.sum((lower | tied).astype(jnp.int32), axis=1)
    place = (rank % ids) * each + rank // ids
    owners = jnp.arange(spread, dtype=jnp.int32)
    start = jnp.sum((owner_list[None, :] < owners[:, None]).astype(jnp.int32), axis=1)
    count = jnp.sum((owner_list[None, :] == owners[:, None]).astype(jnp.int32), axis=1)
    turn = jnp.arange(lanes, dtype=jnp.int32) * ids

    my_start, my_count = start[me_f], count[me_f]
    slot_to = ((base + owners - my_start) % ids)[:, None] + turn[None, :]
    slot_to = jnp.minimum(slot_to, capacity - 1).reshape(-1)
    slot_at = ((me - start) % ids)[:, None] + turn[None, :]
    send_to = jnp.clip((start[:, None] + slot_at) // ids, 0, each - 1).reshape(-1)
    my_rank = me + ids * jnp.arange(each, dtype=jnp.int32)
    my_owner = jnp.sum((start + count)[None, :] <= my_rank[:, None], axis=1).astype(jnp.int32)
    my_lane = (my_rank - start[my_owner]) // ids
    state_at = my_owner * lanes + my_lane
    slots = jnp.arange(capacity, dtype=jnp.int32)
    grad_at = ((my_start + slots) % ids) * lanes + slots // ids
    grad_live = (slots < my_count).astype(jnp.int32)
    held_at = lax.dynamic_slice(place, (me_f * held,), (held,))

    states = jnp.stack(
        [
            jnp.take(master_slots, slot_to, axis=0).astype(BF),
            jnp.take(first_slots, slot_to, axis=0).astype(BF),
            jnp.take(second_slots, slot_to, axis=0).astype(BF),
        ],
        axis=1,
    )
    states = lax.all_to_all(states, "fsdp", 0, 0, tiled=True)

    live = jnp.arange(MASKM, dtype=jnp.int32)[None, :] < masked_count[:, None]
    pos = jnp.pad(
        jnp.where(live, masked_pos, -1), ((0, 0), (0, PAD - MASKM)), constant_values=-1
    )[:, :, None]
    cot = jnp.pad(
        jnp.where(live[:, :, None], out_grad, jnp.zeros((), BF)), ((0, 0), (0, PAD - MASKM), (0, 0))
    ).reshape(pages * PAD, WIDTH)

    stack = lax.all_gather(weights, "fsdp", axis=0, tiled=True)
    q, k, v, tm, qm, cm = project(tokens, pos, vectors, stack)
    gr, gc, gv, dw = masked_part(place, tm, cm, cot, vectors, stack)
    dq, dk, dv, gv_attn, dw = attention_back(place, tokens, k, v, tm, qm, gc, dw)
    grad_vectors = jnp.concatenate([gv_attn[0:2], gv[2:12]], axis=0)
    if groups > 1:
        mine = lax.psum_scatter(dw, ("dp", "fsdp"), scatter_dimension=0, tiled=True)
    else:
        mine = lax.psum(lax.psum_scatter(dw, "fsdp", scatter_dimension=0, tiled=True), "dp")
    layer_out = forward_rest(tokens, q, k, v, vectors, stack)
    token_grad = input_grad(pos, dq, dk, dv, gr, stack)
    grad_vectors = jnp.sum(lax.all_gather(grad_vectors, ("dp", "fsdp")), axis=0)

    new_mine = weight_step(state_at, mine, states)
    if groups > 1:
        new_all = lax.all_gather(new_mine, ("dp", "fsdp"), axis=0, tiled=True)
    else:
        new_all = lax.all_gather(new_mine, "fsdp", axis=0, tiled=True)
    owned = lax.all_to_all(jnp.take(mine, send_to, axis=0), "fsdp", 0, 0, tiled=True)
    if groups > 1:
        owned = lax.all_gather(owned, "dp", axis=0, tiled=True)
    new_first, new_second = moment_step(grad_at, grad_live, owned, first_slots, second_slots)
    new_weights = take_blocks(held_at, new_all).reshape(held * ROWS, WIDTH)
    new_vectors, new_vector_first, new_vector_second = adam_step(
        vectors, vector_first, vector_second, grad_vectors, VECTOR_RATE
    )
    return (
        layer_out,
        token_grad,
        new_weights,
        new_first,
        new_second,
        new_vectors,
        new_vector_first,
        new_vector_second,
    )


def solution(mesh):
    dp, fsdp = mesh.shape["dp"], mesh.shape["fsdp"]
    groups = 2 if dp == 2 and NBLK % (2 * fsdp) == 0 else 1
    both = ("dp", "fsdp")
    return jax.shard_map(
        functools.partial(local, groups),
        mesh=mesh,
        in_specs=(
            P(both, None),
            P(both, None),
            P(both),
            P(both, None, None),
            P("fsdp", None),
            P(),
            P(),
            P("fsdp", None, None),
            P("fsdp", None, None),
            P("fsdp", None, None),
            P(),
            P(),
        ),
        out_specs=(
            P(both, None),
            P(both, None),
            P("fsdp", None),
            P("fsdp", None, None),
            P("fsdp", None, None),
            P(),
            P(),
            P(),
        ),
        check_vma=False,
    )
```

time: 1120 us -> 667 us (0.60)
  matrix products: 220 us -> 0 us
  local copies, waits for them, and re-layouts: 192 us -> 19.9 us
  Pallas kernels: 44.4 us -> 164 us
  other arithmetic: 103 us -> 18.6 us
  waiting for transfers between devices: 497 us -> 428 us
  blocking collectives: 40.5 us -> 0 us
  starting transfers between devices: 0.16 us -> 12.1 us
    dot_general x37 -> x0, matrix products: 220 us -> none  [the longest x6 58 us: times_last(): lax.dot_general(left_side, right_side, CONTRACT_LAST, preferred_element_t...]
    pallas_call x0 -> x8, Pallas kernels: none -> 164 us  [the longest x1 38.4 us: forward_rest(): pl.pallas_call(forward_kernel, grid=(pages,), in_specs=[page, page, page,...]
    reduce_scatter x1, waiting for transfers between devices: 268 us -> 161 us  [local(): mine = lax.psum_scatter(dw, ('dp', 'fsdp'), scatter_dimension=0, tiled=True)]
    convert_element_type x6 -> x1, other arithmetic: 76.5 us -> 1.22 us  [local(): grad_live = (slots < my_count).astype(jnp.int32)]
    all_to_all x0 -> x2, waiting for transfers between devices: none -> 73.7 us  [the longest x1 63.9 us: local(): states = lax.all_to_all(states, 'fsdp', 0, 0, tiled=True)]
    dynamic_slice x15 -> x3, local copies, waits for them, and re-layouts: 66.7 us -> 1.9 us  [the longest x2 1.24 us: local(): my_start, my_count = (start[me_f], count[me_f])]
    psum x1 -> x0, waiting for transfers between devices: 57.1 us -> none  [local(): lax.psum(owned_grad.astype(jnp.bfloat16), 'dp').astype(jnp.float32)]
    dot_general x3 -> x0, Pallas kernels: 44.4 us -> none  [attend_forward(): jnp.einsum('hqk,hkd->hqd', probability, values, preferred_element_type=jn...]
  transfers between devices with their start and end apart: 4 -> 7, of which waited for: 4 -> 5; matrix products, arithmetic and copies ran while one was open for 4% -> 5% of each run, Pallas kernels for 0% -> 11%
where the time goes in v1:
time: 667 us; the launch traced here: 657 us
  waiting for transfers between devices  428 us (64%)
  Pallas kernels  164 us (25%)
  local copies, waits for them, and re-layouts  19.9 us (3%)
  other arithmetic  18.6 us (3%)
  between operations  14.4 us (2%)
  starting transfers between devices  12.1 us (2%)
    reduce_scatter x1, waiting for transfers between devices, local(): mine = lax.psum_scatter(dw, ('dp', 'fsdp'), scatter_dimension=0, tiled=True)  161 us
    all_gather x1, waiting for transfers between devices, local(): stack = lax.all_gather(weights, 'fsdp', axis=0, tiled=True)  110 us
    all_gather x1, waiting for transfers between devices, local(): new_all = lax.all_gather(new_mine, ('dp', 'fsdp'), axis=0, tiled=True)  81.4 us
    all_to_all x1, waiting for transfers between devices, local(): states = lax.all_to_all(states, 'fsdp', 0, 0, tiled=True)  63.9 us
    pallas_call x1, Pallas kernels, forward_rest(): pl.pallas_call(forward_kernel, grid=(pages,), in_specs=[page, page, page,...  38.4 us
    pallas_call x1, Pallas kernels, attention_back(): pl.pallas_call(attention_back_kernel, grid_spec=pltpu.PrefetchScalarGridS...  31.1 us
    pallas_call x1, Pallas kernels, masked_part(): pl.pallas_call(masked_kernel, grid_spec=pltpu.PrefetchScalarGridSpec(num_...  29.2 us
    pallas_call x1, Pallas kernels, project(): pl.pallas_call(project_kernel, grid=(pages,), in_specs=[pl.BlockSpec((1,...  23 us
  transfers between devices with their start and end apart: 7, of which 5 were waited for; matrix products, arithmetic and copies ran while one was open for 5% of the time, Pallas kernels for 11%

profile of v1, /device:TPU:0, one launch (start us, length us, event | category | flops | bytes accessed | tf_op | source)
XLA Modules:
  0.0 656.5 jit_solution(3975611461340387179)
XLA Ops:
  8.0 1.0 broadcast_select_fusion.2
  9.0 0.8 copy.25.pos_ref
  10.6 1.1 broadcast_select_fusion.1
  11.7 0.9 pad.9
  13.4 110.3 %all-gather.7.cloned.1.call-done.w_any = bf16[9216,768]{1,0:T(8,128)(2,1)} async-done(((bf16[576,768]{1,0:T(8,128)(2,1)}), bf16[9216,768]{1,0:T(8,128)(2,1)}) %all-gather.7.cloned.1.call-update) | async-done | bytes 14155792 | tf_op jit(solution)/shard_map/all_gather | solution.py:607
  123.7 23.0 %project.1 = (bf16[1536,768]{1,0:T(8,128)(2,1)}, bf16[1536,768]{1,0:T(8,128)(2,1)}, bf16[1536,768]{1,0:T(8,128)(2,1)}, bf16[384,768]{1,0:T(8,128)(2,1)}, bf16[38...) custom-call(s32[3,128,1]{2,1,0:T(8,128)} %copy.25.pos_ref, bf16[1536,768]{1,0:T(8,128)(2,1)} %tok_ref.5, f32[12,768]{1,0:T(8,128)} %vec_ref.5, ...), custom_call_target="tpu_custom_call" | custom-call | tf_op jit(solution)/shard_map/project/pallas_call | solution.py:127
  146.7 29.2 %masked.1 = (f32[384,768]{1,0:T(8,128)}, bf16[384,768]{1,0:T(8,128)(2,1)}, f32[16,768]{1,0:T(8,128)}, bf16[192,48,768]{2,1,0:T(8,128)(2,1)}) custom-call(s32[192]{0:T(256)} %fusion.7.place_ref, bf16[384,768]{1,0:T(8,128)(2,1)} %get-tuple-element.29.tm_ref, bf16[384,768]{1,0:T(8,128)(2,1)} %get-tuple-element.31.cm_ref, bf16[384,768]{1,0:T(8,128)(2,1)} %bitcast.29, ...), custom_call_target="tpu_custom_call" | custom-call | tf_op jit(solution)/shard_map/masked/pallas_call | solution.py:238
  175.9 31.1 %attention_back.1 = (bf16[384,768]{1,0:T(8,128)(2,1)}, bf16[1536,768]{1,0:T(8,128)(2,1)}, bf16[1536,768]{1,0:T(8,128)(2,1)}, f32[8,768]{1,0:T(8,128)}, bf16[192,48,768]{2,1,0:T(8,128)(2,1)}) custom-call(s32[192]{0:T(256)} %fusion.7.place_ref, bf16[1536,768]{1,0:T(8,128)(2,1)} %tok_ref.5, ...), custom_call_target="tpu_custom_call", output_to_operand_aliasing={{4}: (7, {})} | custom-call | tf_op jit(solution)/shard_map/attention_back/pallas_call | solution.py:340
  207.2 161.0 %reduce-scatter.2.cloned.1.call-done.grad_ref = bf16[6,48,768]{2,1,0:T(8,128)(2,1)} async-done(((bf16[192,48,768]{2,1,0:T(8,128)(2,1)}), bf16[6,48,768]{2,1,0:T(8,128)(2,1)}) %reduce-scatter.2.cloned.1.call-update) | async-done | bytes 442384 | tf_op jit(solution)/shard_map/reduce_scatter | solution.py:613
  368.2 2.6 gather_fusion.1
  370.9 2.5 broadcast_select_fusion
  373.4 4.4 all-to-all-start.1
  379.2 1.7 gather_fusion.2
  380.9 3.7 gather_fusion.3
  384.6 3.8 gather_fusion.4
  388.3 2.8 fusion
  391.1 2.0 pad_maximum_fusion
  393.1 9.8 %all-to-all-done.1 = bf16[16,48,768]{2,1,0:T(8,128)(2,1)} async-done(((bf16[16,48,768]{2,1,0:T(8,128)(2,1)}), bf16[16,48,768]{2,1,0:T(8,128)(2,1)}, u32[]{:S(2)}, u32[]{:S(2)}) %all-to-all-start.1) | async-done | bytes 1179680 | tf_op jit(solution)/shard_map/all_to_all | solution.py:625
  403.0 7.5 %all-to-all-start = ((bf16[16,3,48,768]{3,2,1,0:T(8,128)(2,1)}), bf16[16,3,48,768]{3,2,1,0:T(8,128)(2,1)S(1)}, u32[]{:S(2)}, u32[]{:S(2)}) async-start(bf16[16,3,48,768]{3,2,1,0:T(8,128)(2,1)} %pad_maximum_fusion), calls=%async_computation.1 | async-start | bytes 7077888 | tf_op jit(solution)/shard_map/all_to_all | solution.py:597
  410.5 0.8 slice.7
  414.7 1.2 fusion.18.from_ref
  415.9 63.9 %all-to-all-done.state_ref = bf16[16,3,48,768]{3,2,1,0:T(8,128)(2,1)S(1)} async-done(((bf16[16,3,48,768]{3,2,1,0:T(8,128)(2,1)}), bf16[16,3,48,768]{3,2,1,0:T(8,128)(2,1)S(1)}, u32[]{:S(2)}, u32[]{:S(2)}) %all-to-all-start) | async-done | bytes 3538976 | tf_op jit(solution)/shard_map/all_to_all | solution.py:597
  479.8 1.8 copy-done.2
  481.6 5.7 weight_step.1
  488.6 1.3 fusion.8.from_ref
  489.8 1.2 compare_convert_fusion.live_ref
  491.0 38.4 %forward_rest.1 = bf16[1536,768]{1,0:T(8,128)(2,1)} custom-call(bf16[1536,768]{1,0:T(8,128)(2,1)} %tok_ref.5, bf16[1536,768]{1,0:T(8,128)(2,1)} %get-tuple-element.26.q_ref, bf16[1536,768]{1,0:T(8,128)(2,1)} %get-tuple-element.27.k_ref, bf16[1536,768]{1,0:T(8,128)(2,1)} %get-tuple-element.28.v_ref, f32[12,768]{1,0:T(8,128)} %vec_ref.5, ...), custom_call_target="tpu_custom_call" | custom-call | tf_op jit(solution)/shard_map/forward_rest/pallas_call | solution.py:404
  529.4 11.5 %input_grad.1 = f32[1536,768]{1,0:T(8,128)} custom-call(s32[3,128,1]{2,1,0:T(8,128)} %copy.25.pos_ref, bf16[384,768]{1,0:T(8,128)(2,1)} %get-tuple-element.34.dq_ref, bf16[1536,768]{1,0:T(8,128)(2,1)} %get-tuple-element.35.dk_ref, bf16[1536,768]{1,0:T(8,128)(2,1)} %get-tuple-element.36.dv_ref, f32[384,768]{1,0:T(8,128)} %get-tuple-element.37.gr_ref, ...), custom_call_target="tpu_custom_call" | custom-call | tf_op jit(solution)/shard_map/input_grad/pallas_call | solution.py:442
  541.0 1.5 reduce_sum.55
  543.3 16.6 %moment_step.1 = (f32[24,48,768]{2,1,0:T(8,128)}, f32[24,48,768]{2,1,0:T(8,128)}) custom-call(s32[24]{0:T(128)} %fusion.8.from_ref, s32[24]{0:T(128)} %compare_convert_fusion.live_ref, bf16[32,48,768]{2,1,0:T(8,128)(2,1)} %all-gather.11.cloned.1.call-done.grad_ref, f32[24,48,768]{2,1,0:T(8,128)} %first_ref.1, f32[24,48,768]{2,1,0:T(8,128)} %second_ref.1), custom_call_target="tpu_custom_call" | custom-call | tf_op jit(solution)/shard_map/moment_step/pallas_call | solution.py:503
  559.8 81.4 %all-gather.9.cloned.1.call-done.in_ref = bf16[192,48,768]{2,1,0:T(8,128)(2,1)} async-done(((bf16[6,48,768]{2,1,0:T(8,128)(2,1)}), bf16[192,48,768]{2,1,0:T(8,128)(2,1)}) %all-gather.9.cloned.1.call-update) | async-done | bytes 14155792 | tf_op jit(solution)/shard_map/all_gather | solution.py:622
  641.2 8.3 %take_blocks.1 = f32[12,48,768]{2,1,0:T(8,128)} custom-call(s32[12]{0:T(128)} %dynamic_slice.9.from_ref, bf16[192,48,768]{2,1,0:T(8,128)(2,1)} %all-gather.9.cloned.1.call-done.in_ref), custom_call_target="tpu_custom_call" | custom-call | tf_op jit(solution)/shard_map/take_blocks/pallas_call | solution.py:526
  (51 shorter events, 9.2 us)
Async XLA Ops:
  7.2 372.0 %copy-start = (f32[24,48,768]{2,1,0:T(8,128)S(1)}, f32[24,48,768]{2,1,0:T(8,128)}, u32[]{:S(2)}) copy-start(f32[24,48,768]{2,1,0:T(8,128)} %param.21) | copy-start | bytes 10616836
  7.2 116.5 %all-gather.7.cloned.1.call-start = ((), (), s32[]{:S(2)}) async-start(), calls=%async_computation.3 | async-start | bytes 15040512 | tf_op jit(solution)/shard_map/all_gather | solution.py:607
  7.9 4.7 copy-start.7
  7.9 360.3 %reduce-scatter.2.cloned.1.call-start = ((), (), s32[]{:S(2)}) async-start(), calls=%async_computation.4 | async-start | bytes 14598144 | tf_op jit(solution)/shard_map/reduce_scatter | solution.py:613
  373.4 29.5 %all-to-all-start.1 = ((bf16[16,48,768]{2,1,0:T(8,128)(2,1)}), bf16[16,48,768]{2,1,0:T(8,128)(2,1)}, u32[]{:S(2)}, u32[]{:S(2)}) async-start(bf16[16,48,768]{2,1,0:T(8,128)(2,1)} %broadcast_select_fusion), calls=%async_computation.2 | async-start | bytes 2359296 | tf_op jit(solution)/shard_map/all_to_all | solution.py:625
  403.0 76.8 %all-to-all-start = ((bf16[16,3,48,768]{3,2,1,0:T(8,128)(2,1)}), bf16[16,3,48,768]{3,2,1,0:T(8,128)(2,1)S(1)}, u32[]{:S(2)}, u32[]{:S(2)}) async-start(bf16[16,3,48,768]{3,2,1,0:T(8,128)(2,1)} %pad_maximum_fusion), calls=%async_computation.1 | async-start | bytes 7077888 | tf_op jit(solution)/shard_map/all_to_all | solution.py:597
  410.4 130.6 %all-gather.13.cloned.1.call-start = ((), (), s32[]{:S(2)}) async-start(), calls=%async_computation.7 | async-start | bytes 1622016 | tf_op jit(solution)/shard_map/all_gather | solution.py:618
  412.7 130.6 %all-gather.11.cloned.1.call-start = ((), (), s32[]{:S(2)}) async-start(), calls=%async_computation.6 | async-start | bytes 3538944 | tf_op jit(solution)/shard_map/all_gather | solution.py:627
  413.2 228.0 %all-gather.9.cloned.1.call-start = ((), (), s32[]{:S(2)}) async-start(), calls=%async_computation.5 | async-start | bytes 14598144 | tf_op jit(solution)/shard_map/all_gather | solution.py:622
  413.5 0.5 copy-start.8
  415.9 72.0 %copy-start.6 = (s32[192]{0:T(256)S(1)}, s32[192]{0:T(256)}, u32[]{:S(2)}) copy-start(s32[192]{0:T(256)} %fusion.7.place_ref) | copy-start | bytes 2308
  479.8 1.8 copy-start.2
  541.0 1.6 copy-start.3
  541.0 1.6 copy-start.4
  541.0 1.6 copy-start.5
  641.2 8.3 %copy-start.1 = (f32[24,48,768]{2,1,0:T(8,128)S(1)}, f32[24,48,768]{2,1,0:T(8,128)}, u32[]{:S(2)}) copy-start(f32[24,48,768]{2,1,0:T(8,128)} %param.21) | copy-start | bytes 10616836
Sparse Core Ops, SparseCore 0:
  10.3 113.3 all-gather.6
  207.1 161.0 reduce-scatter.1
  414.7 83.2 all-gather.12
  499.5 35.7 all-gather.10
  538.0 103.1 all-gather.8

commit v2 on v1

--- a/solution.py
+++ b/solution.py
@@ -34,6 +34,12 @@
 F32 = jnp.float32
 VMEM_LIMIT = 60 * 1024 * 1024
 ANY = pl.BlockSpec(memory_space=pl.ANY)
+
+
+def cost(tflop, mbytes):
+    return pl.CostEstimate(
+        flops=int(tflop * 1e12), bytes_accessed=int(mbytes * 1e6), transcendentals=0
+    )
 
 
 def mm(a, b):
@@ -137,6 +143,7 @@
         out_shape=[tall, tall, tall, short, short, short],
         scratch_shapes=[pltpu.VMEM((3 * WIDTH, WIDTH), BF), pltpu.SemaphoreType.DMA],
         compiler_params=pltpu.CompilerParams(vmem_limit_bytes=VMEM_LIMIT),
+        cost_estimate=cost(0.018, 20),
         name="project",
     )(pos, tokens, vectors, stack)
 
@@ -259,6 +266,7 @@
             jax.ShapeDtypeStruct((NBLK, ROWS, WIDTH), BF),
         ],
         compiler_params=pltpu.CompilerParams(vmem_limit_bytes=VMEM_LIMIT),
+        cost_estimate=cost(0.024, 30),
         name="masked",
     )(place, tm, cm, cot, vectors, stack)
 
@@ -359,6 +367,7 @@
         ],
         input_output_aliases={7: 4},
         compiler_params=pltpu.CompilerParams(vmem_limit_bytes=VMEM_LIMIT),
+        cost_estimate=cost(0.025, 30),
         name="attention_back",
     )(place, tokens, k, v, tm, qm, gc, dw)
 
@@ -413,6 +422,7 @@
             pltpu.SemaphoreType.DMA,
         ],
         compiler_params=pltpu.CompilerParams(vmem_limit_bytes=VMEM_LIMIT),
+        cost_estimate=cost(0.036, 30),
         name="forward_rest",
     )(tokens, q, k, v, vectors, stack)
 
@@ -447,6 +457,7 @@
         out_shape=jax.ShapeDtypeStruct(dk.shape, F32),
         scratch_shapes=[pltpu.VMEM((3 * WIDTH, WIDTH), BF), pltpu.SemaphoreType.DMA],
         compiler_params=pltpu.CompilerParams(vmem_limit_bytes=VMEM_LIMIT),
+        cost_estimate=cost(0.010, 20),
         name="input_grad",
     )(pos, dq, dk, dv, gr, stack)
 
@@ -460,6 +471,15 @@
         / (jnp.sqrt(moment_two / (1.0 - SECOND_DECAY**STEP)) + ADAM_EPSILON)
     )
     return (parameter - rate * (ascent + WEIGHT_DECAY * parameter), moment_one, moment_two)
+
+
+def all_sum(x):
+    for axis in ("fsdp", "dp"):
+        size, step = lax.axis_size(axis), 1
+        while step < size:
+            x = x + lax.ppermute(x, axis, [(i, i ^ step) for i in range(size)])
+            step *= 2
+    return x
 
 
 def weight_step_kernel(from_ref, grad_ref, state_ref, out_ref):
@@ -486,35 +506,40 @@
             out_specs=pl.BlockSpec((1, ROWS, WIDTH), lambda i, s: (i, 0, 0)),
         ),
         out_shape=jax.ShapeDtypeStruct(grads.shape, BF),
+        cost_estimate=cost(0.0, 2),
         name="weight_step",
     )(source, grads, states)
 
 
-def moment_step_kernel(from_ref, live_ref, grad_ref, first_ref, second_ref, one_ref, two_ref):
-    live = live_ref[pl.program_id(0)] > 0
-    grad = jnp.where(live, grad_ref[0].astype(F32), 0.0)
+def moment_step_kernel(
+    from_ref, live_ref, grad_ref, other_ref, first_ref, second_ref, one_ref, two_ref
+):
+    live = live_ref[pl.program_id(0)]
+    grad = jnp.where(
+        live == 1,
+        grad_ref[0].astype(F32),
+        jnp.where(live == 2, other_ref[0].astype(F32), 0.0),
+    )
     one_ref[0] = FIRST_DECAY * first_ref[0] + (1.0 - FIRST_DECAY) * grad
     two_ref[0] = SECOND_DECAY * second_ref[0] + (1.0 - SECOND_DECAY) * grad * grad
 
 
-def moment_step(source, live, grads, first, second):
+def moment_step(source, live, grads, other, first, second):
     slot = pl.BlockSpec((1, ROWS, WIDTH), lambda i, s, n: (i, 0, 0))
+    near = pl.BlockSpec((1, ROWS, WIDTH), lambda i, s, n: (s[i], 0, 0))
     shape = jax.ShapeDtypeStruct(first.shape, F32)
     return pl.pallas_call(
         moment_step_kernel,
         grid_spec=pltpu.PrefetchScalarGridSpec(
             num_scalar_prefetch=2,
             grid=(first.shape[0],),
-            in_specs=[
-                pl.BlockSpec((1, ROWS, WIDTH), lambda i, s, n: (s[i], 0, 0)),
-                slot,
-                slot,
-            ],
+            in_specs=[near, near, slot, slot],
             out_specs=[slot, slot],
         ),
         out_shape=[shape, shape],
+        cost_estimate=cost(0.0, 18),
         name="moment_step",
-    )(source, live, grads, first, second)
+    )(source, live, grads, other, first, second)
 
 
 def take_kernel(from_ref, in_ref, out_ref):
@@ -532,6 +557,7 @@
             out_specs=pl.BlockSpec((1, ROWS, WIDTH), lambda i, s: (i, 0, 0)),
         ),
         out_shape=jax.ShapeDtypeStruct((count, ROWS, WIDTH), F32),
+        cost_estimate=cost(0.0, 3),
         name="take_blocks",
     )(source, blocks)
 
@@ -582,19 +608,21 @@
     my_lane = (my_rank - start[my_owner]) // ids
     state_at = my_owner * lanes + my_lane
     slots = jnp.arange(capacity, dtype=jnp.int32)
-    grad_at = ((my_start + slots) % ids) * lanes + slots // ids
-    grad_live = (slots < my_count).astype(jnp.int32)
+    slot_id = (my_start + slots) % ids
+    grad_at = (slot_id % spread) * lanes + slots // ids
+    grad_live = (slots < my_count).astype(jnp.int32) * (1 + (slot_id // spread != base // spread))
     held_at = lax.dynamic_slice(place, (me_f * held,), (held,))
 
     states = jnp.stack(
         [
-            jnp.take(master_slots, slot_to, axis=0).astype(BF),
-            jnp.take(first_slots, slot_to, axis=0).astype(BF),
-            jnp.take(second_slots, slot_to, axis=0).astype(BF),
+            jnp.take(master_slots, slot_to, axis=0, mode="clip").astype(BF),
+            jnp.take(first_slots, slot_to, axis=0, mode="clip").astype(BF),
+            jnp.take(second_slots, slot_to, axis=0, mode="clip").astype(BF),
         ],
         axis=1,
     )
     states = lax.all_to_all(states, "fsdp", 0, 0, tiled=True)
+    states, tokens = lax.optimization_barrier((states, tokens))
 
     live = jnp.arange(MASKM, dtype=jnp.int32)[None, :] < masked_count[:, None]
     pos = jnp.pad(
@@ -615,17 +643,21 @@
         mine = lax.psum(lax.psum_scatter(dw, "fsdp", scatter_dimension=0, tiled=True), "dp")
     layer_out = forward_rest(tokens, q, k, v, vectors, stack)
     token_grad = input_grad(pos, dq, dk, dv, gr, stack)
-    grad_vectors = jnp.sum(lax.all_gather(grad_vectors, ("dp", "fsdp")), axis=0)
+    grad_vectors = all_sum(grad_vectors)
+    mine, layer_out, token_grad, grad_vectors = lax.optimization_barrier(
+        (mine, layer_out, token_grad, grad_vectors)
+    )
 
     new_mine = weight_step(state_at, mine, states)
     if groups > 1:
         new_all = lax.all_gather(new_mine, ("dp", "fsdp"), axis=0, tiled=True)
     else:
         new_all = lax.all_gather(new_mine, "fsdp", axis=0, tiled=True)
-    owned = lax.all_to_all(jnp.take(mine, send_to, axis=0), "fsdp", 0, 0, tiled=True)
-    if groups > 1:
-        owned = lax.all_gather(owned, "dp", axis=0, tiled=True)
-    new_first, new_second = moment_step(grad_at, grad_live, owned, first_slots, second_slots)
+    owned = lax.all_to_all(jnp.take(mine, send_to, axis=0, mode="clip"), "fsdp", 0, 0, tiled=True)
+    other = lax.ppermute(owned, "dp", [(0, 1), (1, 0)]) if groups > 1 else owned
+    new_first, new_second = moment_step(
+        grad_at, grad_live, owned, other, first_slots, second_slots
+    )
     new_weights = take_blocks(held_at, new_all).reshape(held * ROWS, WIDTH)
     new_vectors, new_vector_first, new_vector_second = adam_step(
         vectors, vector_first, vector_second, grad_vectors, VECTOR_RATE

time: 667 us -> 590 us (0.88)
  waiting for transfers between devices: 428 us -> 318 us
  blocking collectives: 0 us -> 43 us
  other arithmetic: 18.6 us -> 11.3 us
    all_gather x1, waiting for transfers between devices: 110 us -> 40.5 us  [local(): stack = lax.all_gather(weights, 'fsdp', axis=0, tiled=True)]
    reduce_scatter x1, waiting for transfers between devices: 161 us -> 97.9 us  [local(): mine = lax.psum_scatter(dw, ('dp', 'fsdp'), scatter_dimension=0, tiled=True)]
    all_gather x1, waiting for transfers between devices: 81.4 us -> 26 us  [local(): new_all = lax.all_gather(new_mine, ('dp', 'fsdp'), axis=0, tiled=True)]
    all_to_all x1, waiting for transfers between devices: 63.9 us -> 114 us  [local(): states = lax.all_to_all(states, 'fsdp', 0, 0, tiled=True)]
    all_to_all x0 -> x1, blocking collectives: none -> 43 us  [local(): lax.all_to_all(jnp.take(mine, send_to, axis=0, mode='clip'), 'fsdp', 0, 0...]
    ppermute x0 -> x6, waiting for transfers between devices: none -> 38.5 us  [the longest x1 32.1 us: local(): other = lax.ppermute(owned, 'dp', [(0, 1), (1, 0)]) if groups > 1 else owned]
    all_to_all x1 -> x0, waiting for transfers between devices: 9.82 us -> none  [local(): lax.all_to_all(jnp.take(mine, send_to, axis=0), 'fsdp', 0, 0, tiled=True)]
  transfers between devices with their start and end apart: 7 -> 10, of which waited for: 5 -> 8; matrix products, arithmetic and copies ran while one was open for 5% -> 4% of each run, Pallas kernels for 11% -> 12%
where the time goes in v2:
time: 590 us; the launch traced here: 579 us
  waiting for transfers between devices  318 us (54%)
  Pallas kernels  165 us (28%)
  blocking collectives  43 us (7%)
  local copies, waits for them, and re-layouts  16.1 us (3%)
  between operations  14.2 us (2%)
  starting transfers between devices  12.1 us (2%)
  other arithmetic  11.3 us (2%)
    all_to_all x1, waiting for transfers between devices, local(): states = lax.all_to_all(states, 'fsdp', 0, 0, tiled=True)  114 us
    reduce_scatter x1, waiting for transfers between devices, local(): mine = lax.psum_scatter(dw, ('dp', 'fsdp'), scatter_dimension=0, tiled=True)  97.9 us
    all_to_all x1, blocking collectives, local(): lax.all_to_all(jnp.take(mine, send_to, axis=0, mode='clip'), 'fsdp', 0, 0...  43 us
    all_gather x1, waiting for transfers between devices, local(): stack = lax.all_gather(weights, 'fsdp', axis=0, tiled=True)  40.5 us
    pallas_call x1, Pallas kernels, forward_rest(): pl.pallas_call(forward_kernel, grid=(pages,), in_specs=[page, page, page,...  38.8 us
    ppermute x1, waiting for transfers between devices, local(): other = lax.ppermute(owned, 'dp', [(0, 1), (1, 0)]) if groups > 1 else owned  32.1 us
    pallas_call x1, Pallas kernels, attention_back(): pl.pallas_call(attention_back_kernel, grid_spec=pltpu.PrefetchScalarGridS...  31.5 us
    pallas_call x1, Pallas kernels, masked_part(): pl.pallas_call(masked_kernel, grid_spec=pltpu.PrefetchScalarGridSpec(num_...  29.3 us
  transfers between devices with their start and end apart: 10, of which 8 were waited for; matrix products, arithmetic and copies ran while one was open for 4% of the time, Pallas kernels for 12%

profile of v2, /device:TPU:0, one launch (start us, length us, event | category | flops | bytes accessed | tf_op | source)
XLA Modules:
  0.0 579.5 jit_solution(10556593406162418423)
XLA Ops:
  7.9 1.6 convert_reduce_fusion.1
  10.7 3.7 gather_fusion.2
  14.4 3.7 gather_fusion.1
  18.1 1.7 gather_fusion
  19.8 3.7 pad_maximum_fusion
  23.5 7.5 %all-to-all-start = ((bf16[16,3,48,768]{3,2,1,0:T(8,128)(2,1)}), bf16[16,3,48,768]{3,2,1,0:T(8,128)(2,1)S(1)}, u32[]{:S(2)}, u32[]{:S(2)}) async-start(bf16[16,3,48,768]{3,2,1,0:T(8,128)(2,1)} %pad_maximum_fusion), calls=%async_computation | async-start | bytes 7077888 | tf_op jit(solution)/shard_map/all_to_all | solution.py:624
  31.1 0.8 copy.25.pos_ref
  32.0 1.1 broadcast_select_fusion
  33.2 0.9 pad.9
  34.8 113.9 %all-to-all-done.state_ref = bf16[16,3,48,768]{3,2,1,0:T(8,128)(2,1)S(1)} async-done(((bf16[16,3,48,768]{3,2,1,0:T(8,128)(2,1)}), bf16[16,3,48,768]{3,2,1,0:T(8,128)(2,1)S(1)}, u32[]{:S(2)}, u32[]{:S(2)}) %all-to-all-start) | async-done | bytes 3538976 | tf_op jit(solution)/shard_map/all_to_all | solution.py:624
  148.7 40.5 %all-gather.3.cloned.1.call-done.w_any = bf16[9216,768]{1,0:T(8,128)(2,1)} async-done(((bf16[576,768]{1,0:T(8,128)(2,1)}), bf16[9216,768]{1,0:T(8,128)(2,1)}) %all-gather.3.cloned.1.call-update) | async-done | bytes 14155792 | tf_op jit(solution)/shard_map/all_gather | solution.py:635
  189.2 23.0 %project.1 = (bf16[1536,768]{1,0:T(8,128)(2,1)}, bf16[1536,768]{1,0:T(8,128)(2,1)}, bf16[1536,768]{1,0:T(8,128)(2,1)}, bf16[384,768]{1,0:T(8,128)(2,1)}, bf16[38...) custom-call(s32[3,128,1]{2,1,0:T(8,128)} %copy.25.pos_ref, bf16[1536,768]{1,0:T(8,128)(2,1)} %tok_ref.2, f32[12,768]{1,0:T(8,128)} %vec_ref.5, ...), custom_call_target="tpu_custom_call" | custom-call | flops 17999998976 | bytes 20000000 | tf_op jit(solution)/shard_map/project/pallas_call | solution.py:133
  212.2 29.3 %masked.1 = (f32[384,768]{1,0:T(8,128)}, bf16[384,768]{1,0:T(8,128)(2,1)}, f32[16,768]{1,0:T(8,128)}, bf16[192,48,768]{2,1,0:T(8,128)(2,1)}) custom-call(s32[192]{0:T(256)} %fusion.4.place_ref, bf16[384,768]{1,0:T(8,128)(2,1)} %get-tuple-element.34.tm_ref, bf16[384,768]{1,0:T(8,128)(2,1)} %get-tuple-element.36.cm_ref, bf16[384,768]{1,0:T(8,128)(2,1)} %bitcast.36, ...), custom_call_target="tpu_custom_call" | custom-call | flops 24000000000 | bytes 30000000 | tf_op jit(solution)/shard_map/masked/pallas_call | solution.py:245
  241.5 31.5 %attention_back.1 = (bf16[384,768]{1,0:T(8,128)(2,1)}, bf16[1536,768]{1,0:T(8,128)(2,1)}, bf16[1536,768]{1,0:T(8,128)(2,1)}, f32[8,768]{1,0:T(8,128)}, bf16[192,48,768]{2,1,0:T(8,128)(2,1)}) custom-call(s32[192]{0:T(256)} %fusion.4.place_ref, bf16[1536,768]{1,0:T(8,128)(2,1)} %tok_ref.2, ...), custom_call_target="tpu_custom_call", output_to_operand_aliasing={{4}: (7, {})} | custom-call | flops 24999999488 | bytes 30000000 | tf_op jit(solution)/shard_map/attention_back/pallas_call | solution.py:348
  273.8 0.7 slice.6
  274.9 1.0 collective-permute-done
  275.9 1.6 collective-permute-start.1
  278.2 1.9 collective-permute-done.1
  280.7 3.6 collective-permute-done.2
  284.3 38.8 %forward_rest.1 = bf16[1536,768]{1,0:T(8,128)(2,1)} custom-call(bf16[1536,768]{1,0:T(8,128)(2,1)} %tok_ref.2, bf16[1536,768]{1,0:T(8,128)(2,1)} %get-tuple-element.40.q_ref, bf16[1536,768]{1,0:T(8,128)(2,1)} %get-tuple-element.32.k_ref, bf16[1536,768]{1,0:T(8,128)(2,1)} %get-tuple-element.33.v_ref, f32[12,768]{1,0:T(8,128)} %vec_ref.5, ...), custom_call_target="tpu_custom_call" | custom-call | flops 35999997952 | bytes 30000000 | tf_op jit(solution)/shard_map/forward_rest/pallas_call | solution.py:413
  323.2 1.5 collective-permute-start.4
  324.6 12.1 %input_grad.1 = f32[1536,768]{1,0:T(8,128)} custom-call(s32[3,128,1]{2,1,0:T(8,128)} %copy.25.pos_ref, bf16[384,768]{1,0:T(8,128)(2,1)} %get-tuple-element.41.dq_ref, bf16[1536,768]{1,0:T(8,128)(2,1)} %get-tuple-element.42.dk_ref, bf16[1536,768]{1,0:T(8,128)(2,1)} %get-tuple-element.43.dv_ref, f32[384,768]{1,0:T(8,128)} %get-tuple-element.44.gr_ref, ...), custom_call_target="tpu_custom_call" | custom-call | flops 10000000000 | bytes 20000000 | tf_op jit(solution)/shard_map/input_grad/pallas_call | solution.py:452
  336.8 97.9 %reduce-scatter.2.cloned.1.call-done.grad_ref = bf16[6,48,768]{2,1,0:T(8,128)(2,1)} async-done(((bf16[192,48,768]{2,1,0:T(8,128)(2,1)}), bf16[6,48,768]{2,1,0:T(8,128)(2,1)}) %reduce-scatter.2.cloned.1.call-update) | async-done | bytes 442384 | tf_op jit(solution)/shard_map/reduce_scatter | solution.py:641
  434.7 5.5 weight_step.1
  440.9 43.0 %all_to_all.10.grad_ref = bf16[16,48,768]{2,1,0:T(8,128)(2,1)S(1)} all-to-all(bf16[16,48,768]{2,1,0:T(8,128)(2,1)S(1)} %gather_fusion.4), channel_id=1, replica_groups=mesh['dp'=2,'fsdp'=16] {'fsdp'}, dimensions={0} | all-to-all | bytes 2359296 | tf_op jit(solution)/shard_map/all_to_all | solution.py:656
  483.9 0.9 collective-permute-start.5
  486.1 1.8 compare_select_fusion.7
  488.5 32.1 %collective-permute-done.5.other_ref = bf16[16,48,768]{2,1,0:T(8,128)(2,1)S(1)} collective-permute-done((bf16[16,48,768]{2,1,0:T(8,128)(2,1)S(1)}, bf16[16,48,768]{2,1,0:T(8,128)(2,1)S(1)}, u32[]{:S(2)}, u32[]{:S(2)}) %collective-permute-start.5) | collective-permute-done | bytes 1179680 | tf_op jit(solution)/shard_map/ppermute | solution.py:657
  520.6 1.0 copy-done.5
  521.7 16.7 %moment_step.1 = (f32[24,48,768]{2,1,0:T(8,128)}, f32[24,48,768]{2,1,0:T(8,128)}) custom-call(s32[24]{0:T(128)} %get-tuple-element.60.from_ref, s32[24]{0:T(128)} %get-tuple-element.59.live_ref, bf16[16,48,768]{2,1,0:T(8,128)(2,1)} %copy-done.4, bf16[16,48,768]{2,1,0:T(8,128)(2,1)} %copy-done.5, f32[24,48,768]{2,1,0:T(8,128)} %first_ref.1, ...), custom_call_target="tpu_custom_call" | custom-call | bytes 18000000 | tf_op jit(solution)/shard_map/moment_step/pallas_call | solution.py:531
  538.4 26.0 %all-gather.5.cloned.1.call-done.in_ref = bf16[192,48,768]{2,1,0:T(8,128)(2,1)} async-done(((bf16[6,48,768]{2,1,0:T(8,128)(2,1)}), bf16[192,48,768]{2,1,0:T(8,128)(2,1)}) %all-gather.5.cloned.1.call-update) | async-done | bytes 14155792 | tf_op jit(solution)/shard_map/all_gather | solution.py:653
  564.4 8.3 %take_blocks.1 = f32[12,48,768]{2,1,0:T(8,128)} custom-call(s32[12]{0:T(128)} %dynamic_slice.10.from_ref, bf16[192,48,768]{2,1,0:T(8,128)(2,1)} %all-gather.5.cloned.1.call-done.in_ref), custom_call_target="tpu_custom_call" | custom-call | bytes 3000000 | tf_op jit(solution)/shard_map/take_blocks/pallas_call | solution.py:551
  (68 shorter events, 7.9 us)
Async XLA Ops:
  7.2 10.9 %copy-start = (f32[24,48,768]{2,1,0:T(8,128)S(1)}, f32[24,48,768]{2,1,0:T(8,128)}, u32[]{:S(2)}) copy-start(f32[24,48,768]{2,1,0:T(8,128)} %param.19) | copy-start | bytes 10616836
  7.2 182.1 %all-gather.3.cloned.1.call-start = ((), (), s32[]{:S(2)}) async-start(), calls=%async_computation.3 | async-start | bytes 15040512 | tf_op jit(solution)/shard_map/all_gather | solution.py:635
  23.5 7.5 %copy-start.11 = (s32[3,104]{1,0:T(4,128)S(1)}, s32[3,104]{1,0:T(4,128)}, u32[]{:S(2)}) copy-start(s32[3,104]{1,0:T(4,128)} %param.13) | copy-start | bytes 3748
  23.5 7.5 %copy-start.13 = (s32[3]{0:T(128)S(1)}, s32[3]{0:T(128)}, u32[]{:S(2)}) copy-start(s32[3]{0:T(128)} %param.14) | copy-start | bytes 40
  23.5 10.5 %copy-start.10 = (s32[192]{0:T(256)S(1)}, s32[192]{0:T(256)}, u32[]{:S(2)}) copy-start(s32[192]{0:T(256)} %param.18) | copy-start | bytes 2308
  23.5 125.2 %all-to-all-start = ((bf16[16,3,48,768]{3,2,1,0:T(8,128)(2,1)}), bf16[16,3,48,768]{3,2,1,0:T(8,128)(2,1)S(1)}, u32[]{:S(2)}, u32[]{:S(2)}) async-start(bf16[16,3,48,768]{3,2,1,0:T(8,128)(2,1)} %pad_maximum_fusion), calls=%async_computation | async-start | bytes 7077888 | tf_op jit(solution)/shard_map/all_to_all | solution.py:624
  31.0 403.7 %reduce-scatter.2.cloned.1.call-start = ((), (), s32[]{:S(2)}) async-start(), calls=%async_computation.4 | async-start | bytes 14598144 | tf_op jit(solution)/shard_map/reduce_scatter | solution.py:641
  148.7 63.5 %copy-start.2 = (bf16[16,3,48,768]{3,2,1,0:T(8,128)(2,1)}, bf16[16,3,48,768]{3,2,1,0:T(8,128)(2,1)S(1)}, u32[]{:S(2)}) copy-start(bf16[16,3,48,768]{3,2,1,0:T(8,128)(2,1)S(1)} %all-to-all-done.state_ref) | copy-start | bytes 10616836
  273.0 0.6 copy-start.14
  273.0 1.6 copy-start.6
  273.0 291.4 %all-gather.5.cloned.1.call-start = ((), (), s32[]{:S(2)}) async-start(), calls=%async_computation.5 | async-start | bytes 14598144 | tf_op jit(solution)/shard_map/all_gather | solution.py:653
  274.6 1.3 collective-permute-start
  275.9 4.2 collective-permute-start.1
  280.1 4.2 collective-permute-start.2
  284.2 38.9 %collective-permute-start.3 = (f32[12,768]{1,0:T(8,128)S(1)}, f32[12,768]{1,0:T(8,128)S(1)}, u32[]{:S(2)}, u32[]{:S(2)}) collective-permute-start(f32[12,768]{1,0:T(8,128)S(1)} %add.177), channel_id=1, source_target_pairs={{0,8},{1,9},{2,10},{3,11},{4,12},{5,13},{6,14},{7,15},{8,0},{9,1},... | collective-permute-start | bytes 110600 | tf_op jit(solution)/shard_map/ppermute | solution.py:480
  323.2 13.6 %collective-permute-start.4 = (f32[12,768]{1,0:T(8,128)S(1)}, f32[12,768]{1,0:T(8,128)S(1)}, u32[]{:S(2)}, u32[]{:S(2)}) collective-permute-start(f32[12,768]{1,0:T(8,128)S(1)} %add.178), channel_id=1, source_target_pairs={{0,16},{16,0},{1,17},{17,1},{2,18},{18,2},{3,19},{19,3},{4,20},{20... | collective-permute-start | bytes 110600 | tf_op jit(solution)/shard_map/ppermute | solution.py:480
  434.7 5.6 copy-start.3
  440.3 45.2 %copy-start.12 = (s32[192]{0:T(256)S(1)}, s32[192]{0:T(256)}, u32[]{:S(2)}) copy-start(s32[192]{0:T(256)} %fusion.4.place_ref) | copy-start | bytes 2308
  440.3 47.6 %copy-start.7 = (f32[12,768]{1,0:T(8,128)S(1)}, f32[12,768]{1,0:T(8,128)}, u32[]{:S(2)}) copy-start(f32[12,768]{1,0:T(8,128)} %vec_ref.5) | copy-start | bytes 110596
  440.3 47.6 %copy-start.8 = (f32[12,768]{1,0:T(8,128)S(1)}, f32[12,768]{1,0:T(8,128)}, u32[]{:S(2)}) copy-start(f32[12,768]{1,0:T(8,128)} %param.22) | copy-start | bytes 110596
  440.3 47.6 %copy-start.9 = (f32[12,768]{1,0:T(8,128)S(1)}, f32[12,768]{1,0:T(8,128)}, u32[]{:S(2)}) copy-start(f32[12,768]{1,0:T(8,128)} %param.23) | copy-start | bytes 110596
  483.9 36.7 %copy-start.4 = (bf16[16,48,768]{2,1,0:T(8,128)(2,1)}, bf16[16,48,768]{2,1,0:T(8,128)(2,1)S(1)}, u32[]{:S(2)}) copy-start(bf16[16,48,768]{2,1,0:T(8,128)(2,1)S(1)} %all_to_all.10.grad_ref) | copy-start | bytes 3538948
  483.9 36.7 %collective-permute-start.5 = (bf16[16,48,768]{2,1,0:T(8,128)(2,1)S(1)}, bf16[16,48,768]{2,1,0:T(8,128)(2,1)S(1)}, u32[]{:S(2)}, u32[]{:S(2)}) collective-permute-start(bf16[16,48,768]{2,1,0:T(8,128)(2,1)S(1)} %all_to_all.10.grad_ref), channel_id=1, source_target_pairs={{0,16},{16,0},{1,17},{17,1},{2,18},{18,2},{3,19},{19,3},{4,20},{20... | collective-permute-start | bytes 3538952 | tf_op jit(solution)/shard_map/ppermute | solution.py:657
  520.6 1.0 copy-start.5
  564.4 8.3 %copy-start.1 = (f32[24,48,768]{2,1,0:T(8,128)S(1)}, f32[24,48,768]{2,1,0:T(8,128)}, u32[]{:S(2)}) copy-start(f32[24,48,768]{2,1,0:T(8,128)} %param.19) | copy-start | bytes 10616836
Sparse Core Ops, SparseCore 0:
  10.3 178.8 all-gather.2
  273.2 161.4 reduce-scatter.1
  440.3 124.0 all-gather.4

commit v3 on v1

v3 whole, which is shorter than its diff:
```python
import functools

import jax
import jax.numpy as jnp
from jax import lax
from jax.experimental import pallas as pl
from jax.experimental.pallas import tpu as pltpu
from jax.sharding import PartitionSpec as P

WIDTH = 768
HEADS = 12
HD = 64
FF = 3072
PAGE = 512
MASKM = 104
ROWS = 48
STEP = 10
NBLK = 192
PAD = 128
STACK = NBLK * ROWS
UP_ROWS = FF // WIDTH

QUERY_SCALE = 0.125
NORM_EPSILON = 1e-06
INV_ROOT_TWO = 0.7071067811865476
INV_ROOT_TAU = 0.3989422804014327
FIRST_DECAY = 0.5
SECOND_DECAY = 0.5
LEARN_RATE = 0.05
VECTOR_RATE = 0.3
WEIGHT_DECAY = 0.01
ADAM_EPSILON = 1e-08

BF = jnp.bfloat16
F32 = jnp.float32
VMEM_LIMIT = 60 * 1024 * 1024
ANY = pl.BlockSpec(memory_space=pl.ANY)
VM = pl.BlockSpec(memory_space=pltpu.VMEM)


def cost(tflop, mbytes):
    return pl.CostEstimate(
        flops=int(tflop * 1e12), bytes_accessed=int(mbytes * 1e6), transcendentals=0
    )


def mm(a, b):
    return lax.dot_general(a, b, (((1,), (0,)), ((), ())), preferred_element_type=F32)


def mm_last(a, b):
    return lax.dot_general(a, b, (((1,), (1,)), ((), ())), preferred_element_type=F32)


def mm_first(a, b):
    return lax.dot_general(a, b, (((0,), (0,)), ((), ())), preferred_element_type=F32)


def send_blocks(stage_ref, first, count, place_ref, shift, arrays, sem):
    @pl.loop(first, first + count)
    def _(i):
        place, low = place_ref[shift + i], 0
        for array in arrays:
            high = low + array.shape[0]

            @pl.when((place >= low) & (place < high))
            def _(array=array, low=low):
                pltpu.make_async_copy(stage_ref.at[i], array.at[place - low], sem).start()

            low = high


def wait_blocks(stage_ref, first, count, arrays, sem):
    pltpu.make_async_copy(
        stage_ref.at[pl.ds(first, count)], arrays[0].at[pl.ds(0, count)], sem
    ).wait()


def row_sum(x):
    return jnp.sum(x, axis=0, keepdims=True)


def unit_of(x):
    center = x - jnp.mean(x, axis=1, keepdims=True)
    inverse = lax.rsqrt(jnp.mean(center * center, axis=1, keepdims=True) + NORM_EPSILON)
    return center * inverse, inverse


def unit_back(grad_out, gain, unit, inverse):
    grad_unit = grad_out * gain
    centered = grad_unit - jnp.mean(grad_unit, axis=1, keepdims=True)
    return inverse * (centered - unit * jnp.mean(grad_unit * unit, axis=1, keepdims=True))


def gelu_cdf(u):
    return 0.5 * (1.0 + lax.erf(u * INV_ROOT_TWO))


def half_masks():
    lane = lax.broadcasted_iota(jnp.int32, (1, 2 * HD), 1)
    low = jnp.where(lane < HD, 1.0, 0.0)
    return (low.astype(BF), (1.0 - low).astype(BF)), lane < HD


def softmax(scores):
    top = jnp.max(scores, axis=1, keepdims=True)
    exponent = jnp.exp(scores - top)
    total = jnp.sum(exponent, axis=1, keepdims=True)
    return exponent * (1.0 / total)


def one_hot_rows(pos):
    return jnp.where(
        pos == lax.broadcasted_iota(jnp.int32, (PAD, PAGE), 1), 1.0, 0.0
    ).astype(BF)


def project_kernel(counts, rows_ref, pos_ref, tok_ref, vec_ref, *rest):
    pieces, rest = rest[: max(1, len(counts))], rest[max(1, len(counts)) :]
    q_ref, k_ref, v_ref, tm_ref, qm_ref, cm_ref, *stacks, w_ref, sem = rest
    step, last = pl.program_id(0), pl.num_programs(0) - 1

    def cut(first, act):
        at = 0
        for piece, (number, size) in zip(pieces, counts):

            @pl.loop(0, number)
            def _(i, piece=piece, size=size, at=at):
                row = pl.multiple_of(rows_ref[at + i], 16)

                @pl.when((row < 3 * WIDTH) == first)
                def _():
                    source = piece.at[pl.ds(pl.multiple_of(i * size, 16), size)]
                    target = w_ref.at[pl.ds(row, size)]
                    act(pltpu.make_async_copy(source, target, sem.at[1 + at + i]))

            at += number

    @pl.when(step == 0)
    def _():
        if counts:
            cut(True, lambda copy: copy.start())
            cut(False, lambda copy: copy.start())
            cut(True, lambda copy: copy.wait())
        else:
            copy = pltpu.make_async_copy(pieces[0].at[pl.ds(0, 3 * WIDTH)], w_ref, sem.at[0])
            copy.start()
            copy.wait()

    if counts:

        @pl.when(step == 1)
        def _():
            cut(False, lambda copy: copy.wait())
            pltpu.make_async_copy(w_ref, stacks[0], sem.at[0]).start()

    tok = tok_ref[...]
    q = ((mm(tok, w_ref[0:WIDTH]) + vec_ref[0:1]) * QUERY_SCALE).astype(BF)
    k = mm(tok, w_ref[WIDTH : 2 * WIDTH]).astype(BF)
    v = (mm(tok, w_ref[2 * WIDTH : 3 * WIDTH]) + vec_ref[1:2]).astype(BF)
    q_ref[...] = q
    k_ref[...] = k
    v_ref[...] = v
    pick = one_hot_rows(pos_ref[0])
    tm_ref[...] = mm(pick, tok).astype(BF)
    qm = mm(pick, q).astype(BF)
    qm_ref[...] = qm
    masks, low = half_masks()
    for pair in range(HEADS // 2):
        cols = slice(pair * 2 * HD, (pair + 1) * 2 * HD)
        kp, vp, qp = k[:, cols], v[:, cols], qm[:, cols]
        parts = []
        for mask in masks:
            prob = softmax(mm_last(qp * mask, kp)).astype(BF)
            parts.append(mm(prob, vp))
        cm_ref[:, cols] = jnp.where(low, parts[0], parts[1]).astype(BF)

    if counts:

        @pl.when(step == last)
        def _():
            pltpu.make_async_copy(w_ref, stacks[0], sem.at[0]).wait()


def project(tokens, pos, vectors, pieces, rows, counts):
    pages = tokens.shape[0] // PAGE
    tall = jax.ShapeDtypeStruct((pages * PAGE, WIDTH), BF)
    short = jax.ShapeDtypeStruct((pages * PAD, WIDTH), BF)
    page = pl.BlockSpec((PAGE, WIDTH), lambda i, s: (i, 0))
    few = pl.BlockSpec((PAD, WIDTH), lambda i, s: (i, 0))
    stack = [jax.ShapeDtypeStruct((STACK, WIDTH), BF)] if counts else []
    total = sum(number for number, _ in counts)
    return pl.pallas_call(
        functools.partial(project_kernel, counts),
        grid_spec=pltpu.PrefetchScalarGridSpec(
            num_scalar_prefetch=1,
            grid=(pages,),
            in_specs=[
                pl.BlockSpec((1, PAD, 1), lambda i, s: (i, 0, 0)),
                page,
                pl.BlockSpec((12, WIDTH), lambda i, s: (0, 0)),
            ]
            + [ANY] * len(pieces),
            out_specs=[page, page, page, few, few, few] + [ANY] * len(stack),
            scratch_shapes=[
                pltpu.VMEM((STACK if counts else 3 * WIDTH, WIDTH), BF),
                pltpu.SemaphoreType.DMA((1 + total,)),
            ],
        ),
        out_shape=[tall, tall, tall, short, short, short] + stack,
        compiler_params=pltpu.CompilerParams(vmem_limit_bytes=VMEM_LIMIT),
        cost_estimate=cost(0.018, 20),
        name="project",
    )(rows, pos, tokens, vectors, *pieces)


def masked_kernel(
    place_ref,
    tm_ref,
    cm_ref,
    cot_ref,
    vec_ref,
    w_any,
    gr_ref,
    gc_ref,
    gv_ref,
    *rest,
):
    *dws, w_ref, up_ref, act_ref, hid_ref, stage_ref, in_sem, out_sem = rest
    parts = 1 + 2 * UP_ROWS
    loads = [
        pltpu.make_async_copy(
            w_any.at[pl.ds((3 + i) * WIDTH, WIDTH)], w_ref.at[i], in_sem.at[i]
        )
        for i in range(parts)
    ]
    for load in loads:
        load.start()
    per = WIDTH // ROWS

    def send(part, value):
        stage_ref[pl.ds(part * per, per)] = value.astype(BF).reshape(per, ROWS, WIDTH)
        send_blocks(stage_ref, part * per, per, place_ref, 3 * per, dws, out_sem.at[part])

    gain_one, shift_one = vec_ref[8:9], vec_ref[9:10]
    gain_two = vec_ref[10:11]
    cm = cm_ref[...]
    loads[0].wait()
    resid_one = tm_ref[...].astype(F32) + mm(cm, w_ref[0]) + vec_ref[2:3]
    unit_one, inv_one = unit_of(resid_one)
    hidden_one = unit_one * gain_one + shift_one
    hid_ref[...] = hidden_one.astype(BF)
    hid = hid_ref[...]
    for c in range(UP_ROWS):
        cols = slice(c * WIDTH, (c + 1) * WIDTH)
        loads[1 + c].wait()
        up = mm_last(hid, w_ref[1 + c]) + vec_ref[3 + c : 4 + c]
        up_ref[:, cols] = up
        act_ref[:, cols] = (up * gelu_cdf(up)).astype(BF)
    resid_two = hidden_one + vec_ref[7:8]
    for c in range(UP_ROWS):
        cols = slice(c * WIDTH, (c + 1) * WIDTH)
        loads[1 + UP_ROWS + c].wait()
        resid_two = resid_two + mm(act_ref[:, cols], w_ref[1 + UP_ROWS + c])
    unit_two, inv_two = unit_of(resid_two)
    cot = cot_ref[...].astype(F32)
    grad_two = unit_back(cot, gain_two, unit_two, inv_two)
    gv_ref[...] = jnp.zeros_like(gv_ref)
    gv_ref[10:11] = row_sum(cot * unit_two)
    gv_ref[11:12] = row_sum(cot)
    down = grad_two.astype(BF)
    gv_ref[7:8] = row_sum(down.astype(F32))
    grad_hidden = grad_two
    for c in range(UP_ROWS):
        cols = slice(c * WIDTH, (c + 1) * WIDTH)
        send(1 + UP_ROWS + c, mm_first(act_ref[:, cols], down))
        up = up_ref[:, cols]
        slope = gelu_cdf(up) + up * jnp.exp(-0.5 * up * up) * INV_ROOT_TAU
        grad_up = (mm_last(down, w_ref[1 + UP_ROWS + c]) * slope).astype(BF)
        gv_ref[3 + c : 4 + c] = row_sum(grad_up.astype(F32))
        send(1 + c, mm_first(grad_up, hid))
        grad_hidden = grad_hidden + mm(grad_up, w_ref[1 + c])
    gv_ref[8:9] = row_sum(grad_hidden * unit_one)
    gv_ref[9:10] = row_sum(grad_hidden)
    grad_one = unit_back(grad_hidden, gain_one, unit_one, inv_one)
    gr_ref[...] = grad_one
    attn = grad_one.astype(BF)
    gv_ref[2:3] = row_sum(attn.astype(F32))
    send(0, mm_first(cm, attn))
    gc_ref[...] = mm_last(attn, w_ref[0]).astype(BF)
    for part in range(parts):
        wait_blocks(stage_ref, part * per, per, dws, out_sem.at[part])


def masked_part(place, sizes, tm, cm, cot, vectors, stack):
    rows = tm.shape[0]
    parts = 1 + 2 * UP_ROWS
    vm = pl.BlockSpec(memory_space=pltpu.VMEM)
    return pl.pallas_call(
        masked_kernel,
        grid_spec=pltpu.PrefetchScalarGridSpec(
            num_scalar_prefetch=1,
            grid=(),
            in_specs=[vm, vm, vm, vm, ANY],
            out_specs=[vm, vm, vm] + [ANY] * len(sizes),
            scratch_shapes=[
                pltpu.VMEM((parts, WIDTH, WIDTH), BF),
                pltpu.VMEM((rows, FF), F32),
                pltpu.VMEM((rows, FF), BF),
                pltpu.VMEM((rows, WIDTH), BF),
                pltpu.VMEM((parts * WIDTH // ROWS, ROWS, WIDTH), BF),
                pltpu.SemaphoreType.DMA((parts,)),
                pltpu.SemaphoreType.DMA((parts,)),
            ],
        ),
        out_shape=[
            jax.ShapeDtypeStruct((rows, WIDTH), F32),
            jax.ShapeDtypeStruct((rows, WIDTH), BF),
            jax.ShapeDtypeStruct((16, WIDTH), F32),
        ]
        + [jax.ShapeDtypeStruct((size, ROWS, WIDTH), BF) for size in sizes],
        compiler_params=pltpu.CompilerParams(vmem_limit_bytes=VMEM_LIMIT),
        cost_estimate=cost(0.024, 30),
        name="masked",
    )(place, tm, cm, cot, vectors, stack)


def attention_back_kernel(
    place_ref,
    tok_ref,
    k_ref,
    v_ref,
    tm_ref,
    qm_ref,
    gc_ref,
    *rest,
):
    arrays = (len(rest) - 7) // 2
    dq_ref, dk_ref, dv_ref, gv_ref, *dws, sum_ref, stage_ref, out_sem = rest[arrays:]
    page, last = pl.program_id(0), pl.num_programs(0) - 1
    per = WIDTH // ROWS
    masks, low = half_masks()

    @pl.when(page == 0)
    def _():
        sum_ref[...] = jnp.zeros_like(sum_ref)
        gv_ref[...] = jnp.zeros_like(gv_ref)

    for pair in range(HEADS // 2):
        cols = slice(pair * 2 * HD, (pair + 1) * 2 * HD)
        kp, vp, qp, gp = k_ref[:, cols], v_ref[:, cols], qm_ref[:, cols], gc_ref[:, cols]
        grad_v, grad_k, grad_q = None, None, []
        for mask in masks:
            qh, gh = qp * mask, gp * mask
            prob = softmax(mm_last(qh, kp))
            grad_prob = mm_last(gh, vp)
            spread = jnp.sum(prob * grad_prob, axis=1, keepdims=True)
            grad_s = (prob * (grad_prob - spread)).astype(BF)
            one_v = mm_first(prob.astype(BF), gh)
            one_k = mm_first(grad_s, qh)
            grad_v = one_v if grad_v is None else grad_v + one_v
            grad_k = one_k if grad_k is None else grad_k + one_k
            grad_q.append(mm(grad_s, kp))
        dv_ref[:, cols] = grad_v.astype(BF)
        dk_ref[:, cols] = grad_k.astype(BF)
        dq_ref[:, cols] = jnp.where(low, grad_q[0], grad_q[1]).astype(BF) * QUERY_SCALE
    dq, dk, dv = dq_ref[...], dk_ref[...], dv_ref[...]
    gv_ref[0:1] += row_sum(dq.astype(F32))
    gv_ref[1:2] += row_sum(dv.astype(F32))
    tok = tok_ref[...]
    sum_ref[0] += mm_first(tm_ref[...], dq)
    sum_ref[1] += mm_first(tok, dk)
    sum_ref[2] += mm_first(tok, dv)

    @pl.when(page == last)
    def _():
        for i in range(3):
            stage_ref[pl.ds(i * per, per)] = (
                sum_ref[i].astype(BF).reshape(per, ROWS, WIDTH)
            )

            send_blocks(stage_ref, i * per, per, place_ref, 0, dws, out_sem.at[i])
        for i in range(3):
            wait_blocks(stage_ref, i * per, per, dws, out_sem.at[i])


def attention_back(place, tokens, k, v, tm, qm, gc, dws):
    pages = tokens.shape[0] // PAGE
    page = pl.BlockSpec((PAGE, WIDTH), lambda i, s: (i, 0))
    few = pl.BlockSpec((PAD, WIDTH), lambda i, s: (i, 0))
    tall = jax.ShapeDtypeStruct((pages * PAGE, WIDTH), BF)
    return pl.pallas_call(
        attention_back_kernel,
        grid_spec=pltpu.PrefetchScalarGridSpec(
            num_scalar_prefetch=1,
            grid=(pages,),
            in_specs=[page, page, page, few, few, few] + [ANY] * len(dws),
            out_specs=[few, page, page, pl.BlockSpec((8, WIDTH), lambda i, s: (0, 0))]
            + [ANY] * len(dws),
            scratch_shapes=[
                pltpu.VMEM((3, WIDTH, WIDTH), F32),
                pltpu.VMEM((3 * WIDTH // ROWS, ROWS, WIDTH), BF),
                pltpu.SemaphoreType.DMA((3,)),
            ],
        ),
        out_shape=[
            jax.ShapeDtypeStruct((pages * PAD, WIDTH), BF),
            tall,
            tall,
            jax.ShapeDtypeStruct((8, WIDTH), F32),
        ]
        + [jax.ShapeDtypeStruct(dw.shape, BF) for dw in dws],
        input_output_aliases={7 + i: 4 + i for i in range(len(dws))},
        compiler_params=pltpu.CompilerParams(vmem_limit_bytes=VMEM_LIMIT),
        cost_estimate=cost(0.025, 30),
        name="attention_back",
    )(place, tokens, k, v, tm, qm, gc, *dws)


def forward_kernel(tok_ref, q_ref, k_ref, v_ref, vec_ref, w_any, *rest):
    out_ref, w_ref, ctx_ref, sem = rest[-4:]
    parts = 1 + 2 * UP_ROWS
    load = pltpu.make_async_copy(w_any.at[pl.ds(3 * WIDTH, parts * WIDTH)], w_ref, sem)
    load.start()

    masks, low = half_masks()
    for pair in range(HEADS // 2):
        cols = slice(pair * 2 * HD, (pair + 1) * 2 * HD)
        kp, vp, qp = k_ref[:, cols], v_ref[:, cols], q_ref[:, cols]
        halves = []
        for mask in masks:
            prob = softmax(mm_last(qp * mask, kp)).astype(BF)
            halves.append(mm(prob, vp))
        ctx_ref[:, cols] = jnp.where(low, halves[0], halves[1]).astype(BF)

    load.wait()
    resid_one = tok_ref[...].astype(F32) + mm(ctx_ref[...], w_ref[0:WIDTH]) + vec_ref[2:3]
    unit_one, _ = unit_of(resid_one)
    hidden_one = unit_one * vec_ref[8:9] + vec_ref[9:10]
    hid = hidden_one.astype(BF)
    resid_two = hidden_one + vec_ref[7:8]
    for c in range(UP_ROWS):
        at, to = (1 + c) * WIDTH, (1 + UP_ROWS + c) * WIDTH
        up = mm_last(hid, w_ref[at : at + WIDTH]) + vec_ref[3 + c : 4 + c]
        act = (up * gelu_cdf(up)).astype(BF)
        resid_two = resid_two + mm(act, w_ref[to : to + WIDTH])
    unit_two, _ = unit_of(resid_two)
    out_ref[...] = (unit_two * vec_ref[10:11] + vec_ref[11:12]).astype(BF)


def forward_page(index, tokens, q, k, v, vectors, stack, before, *after):
    extra = before + after
    page = pl.BlockSpec((PAGE, WIDTH), lambda i: (index, 0))
    whole = pl.BlockSpec((12, WIDTH), lambda i: (0, 0))
    return pl.pallas_call(
        forward_kernel,
        grid=(1,),
        in_specs=[page, page, page, page, whole, ANY] + [ANY] * len(extra),
        out_specs=page,
        out_shape=jax.ShapeDtypeStruct(tokens.shape, BF),
        scratch_shapes=[
            pltpu.VMEM(((1 + 2 * UP_ROWS) * WIDTH, WIDTH), BF),
            pltpu.VMEM((PAGE, WIDTH), BF),
            pltpu.SemaphoreType.DMA,
        ],
        input_output_aliases={6: 0} if before else {},
        compiler_params=pltpu.CompilerParams(vmem_limit_bytes=VMEM_LIMIT),
        cost_estimate=cost(0.0, 0.001),
        name="forward_page",
    )(tokens, q, k, v, vectors, stack, *extra)


def input_grad_kernel(pos_ref, dq_ref, dk_ref, dv_ref, gr_ref, w_any, *rest):
    out_ref, w_ref, sem = rest[-3:]

    @pl.when(pl.program_id(0) == 0)
    def _():
        copy = pltpu.make_async_copy(w_any.at[pl.ds(0, 3 * WIDTH)], w_ref, sem)
        copy.start()
        copy.wait()

    few = gr_ref[...] + mm_last(dq_ref[...], w_ref[0:WIDTH])
    high = few.astype(BF)
    rest = (few - high.astype(F32)).astype(BF)
    pick = one_hot_rows(pos_ref[0])
    out_ref[...] = (
        mm_last(dk_ref[...], w_ref[WIDTH : 2 * WIDTH])
        + mm_last(dv_ref[...], w_ref[2 * WIDTH : 3 * WIDTH])
        + (mm_first(pick, high) + mm_first(pick, rest))
    )


def input_grad(pos, dq, dk, dv, gr, stack, *after):
    pages = dk.shape[0] // PAGE
    page = pl.BlockSpec((PAGE, WIDTH), lambda i: (i, 0))
    few = pl.BlockSpec((PAD, WIDTH), lambda i: (i, 0))
    return pl.pallas_call(
        input_grad_kernel,
        grid=(pages,),
        in_specs=[pl.BlockSpec((1, PAD, 1), lambda i: (i, 0, 0)), few, page, page, few, ANY]
        + [ANY] * len(after),
        out_specs=page,
        out_shape=jax.ShapeDtypeStruct(dk.shape, F32),
        scratch_shapes=[pltpu.VMEM((3 * WIDTH, WIDTH), BF), pltpu.SemaphoreType.DMA],
        compiler_params=pltpu.CompilerParams(vmem_limit_bytes=VMEM_LIMIT),
        cost_estimate=cost(0.0, 0.001),
        name="input_grad",
    )(pos, dq, dk, dv, gr, stack, *after)


def adam_step(parameter, moment_one, moment_two, gradient, rate):
    moment_one = FIRST_DECAY * moment_one + (1.0 - FIRST_DECAY) * gradient
    moment_two = SECOND_DECAY * moment_two + (1.0 - SECOND_DECAY) * gradient * gradient
    ascent = (
        moment_one
        / (1.0 - FIRST_DECAY**STEP)
        / (jnp.sqrt(moment_two / (1.0 - SECOND_DECAY**STEP)) + ADAM_EPSILON)
    )
    return (parameter - rate * (ascent + WEIGHT_DECAY * parameter), moment_one, moment_two)


ORDER = (2, 1, 3, 0)
SIZES = (96, 24, 48, 24)


def swap_dp(x):
    return lax.ppermute(x, "dp", [(0, 1), (1, 0)])


def swap_y(x):
    return lax.ppermute(x, "fsdp", [(f, f ^ 2) for f in range(16)])


def swap_core(x):
    return lax.ppermute(x, "fsdp", [(f, f ^ 1) for f in range(16)])


def up_z(x, steps):
    return lax.ppermute(x, "fsdp", [(f, (f + 4 * steps) % 16) for f in range(16)])


def apart(group, spot):
    me_d, me_f = lax.axis_index("dp"), lax.axis_index("fsdp")
    steps = (spot // 4 - me_f // 4) % 4
    dy = (spot // 2 % 2 + me_f // 2) % 2
    return steps, (group + me_d) % 2, dy, (spot + me_f) % 2


def relative_place(group, spot, turn):
    steps, dx, dy, core = apart(group, spot)
    half, third = turn // 3, turn % 3
    first = jnp.where(dx == 1, 0, 12) + dy * 3
    second = jnp.where(dy == 1, 6, 18) + dx * 3
    inner = jnp.where(half == 0, first, second) + third
    rank = jnp.where(steps == 2, 0, jnp.where(steps == 0, 3, jnp.where(steps == 1, 1, 2)))
    return core * 96 + rank * 24 + inner


def blocks_spec(shape, first=0):
    return pl.BlockSpec(shape, lambda i: (i + first,) + (0,) * (len(shape) - 1))


def core_sum_kernel(keep_ref, from_ref, *rest):
    for part, out in enumerate(rest[-4:]):
        out[0] = keep_ref[0, part] + from_ref[0, part]


def core_sum(keep, got, first, *after):
    count = got.shape[0] // 24
    whole, six = (1, 4, 6, ROWS, WIDTH), (1, 6, ROWS, WIDTH)
    return pl.pallas_call(
        core_sum_kernel,
        grid=(count,),
        in_specs=[blocks_spec(whole, first), blocks_spec(whole)] + [ANY] * len(after),
        out_specs=[blocks_spec(six)] * 4,
        out_shape=[jax.ShapeDtypeStruct((count,) + six[1:], BF)] * 4,
        compiler_params=pltpu.CompilerParams(vmem_limit_bytes=VMEM_LIMIT),
        cost_estimate=cost(0.0, 0.001),
        name="core_sum",
    )(keep.reshape((4,) + whole[1:]), got.reshape((count,) + whole[1:]), *after)


def first_sum_kernel(a_ref, b_ref, to_a_ref, to_b_ref, *rest):
    keep_a, keep_b, send_a, send_b = rest[-4:]
    half_a, half_b = a_ref[0] + to_a_ref[0], b_ref[0] + to_b_ref[0]
    keep_a[0], keep_b[0], send_a[0], send_b[0] = half_a[:3], half_b[:3], half_a[3:], half_b[3:]


def first_sum(a, b, to_a, to_b, *after, weight=0.001):
    count, six, three = a.shape[0], (1, 6, ROWS, WIDTH), (1, 3, ROWS, WIDTH)
    return pl.pallas_call(
        first_sum_kernel,
        grid=(count,),
        in_specs=[blocks_spec(six)] * 4 + [ANY] * len(after),
        out_specs=[blocks_spec(three)] * 4,
        out_shape=[jax.ShapeDtypeStruct((count,) + three[1:], BF)] * 4,
        compiler_params=pltpu.CompilerParams(vmem_limit_bytes=VMEM_LIMIT),
        cost_estimate=cost(0.0, weight),
        name="first_sum",
    )(a, b, to_a, to_b, *after)


def last_sum_kernel(count, a_ref, b_ref, to_a_ref, to_b_ref, *rest):
    for i, out in enumerate(rest[-count:]):
        out[0:3] = a_ref[i] + to_a_ref[i]
        out[3:6] = b_ref[i] + to_b_ref[i]


def last_sum(a, b, to_a, to_b, *after):
    count = a.shape[0]
    return pl.pallas_call(
        functools.partial(last_sum_kernel, count),
        in_specs=[VM] * 4 + [ANY] * len(after),
        out_specs=[VM] * count,
        out_shape=[jax.ShapeDtypeStruct((6, ROWS, WIDTH), BF)] * count,
        compiler_params=pltpu.CompilerParams(vmem_limit_bytes=VMEM_LIMIT),
        cost_estimate=cost(0.0, 0.001),
        name="last_sum",
    )(a, b, to_a, to_b, *after)


def reduce_blocks(dws, tasks):
    keep = dws[0]
    got = [swap_core(send) for send in dws[1:]]
    xs_far, ys_far, a_far, b_far = core_sum(keep, got[0], 0)
    to_far = swap_dp(xs_far), swap_y(ys_far)
    a_far, b_far, ys_far, xs_far = first_sum(a_far, b_far, *to_far)
    to_far = swap_y(ys_far), swap_dp(xs_far)
    xs_near, ys_near, a_near, b_near = core_sum(keep, got[1], 1, ys_far)
    to_near = swap_dp(xs_near), swap_y(ys_near)
    done = tasks[0](xs_near)
    a_near, b_near, ys_near, xs_near = first_sum(a_near, b_near, *to_near, done)
    to_near = swap_y(ys_near), swap_dp(xs_near)
    (far,) = last_sum(a_far, b_far, *to_far, ys_near)
    xs_own, ys_own, a_own, b_own = core_sum(keep, got[2], 3, far)
    far = up_z(far, 2)
    to_own = swap_dp(xs_own), swap_y(ys_own)
    done = tasks[1](xs_own)
    up, down = last_sum(a_near, b_near, *to_near, done, far)
    near = up_z(up, 1), up_z(down, 3)
    a_own, b_own, ys_own, xs_own = first_sum(a_own, b_own, *to_own, up)
    to_own = swap_y(ys_own), swap_dp(xs_own)
    done = tasks[2](ys_own)
    return (a_own, to_own[0], b_own, to_own[1]), (far,) + near, done


def weight_step_kernel(halves, wholes, *refs):
    half_refs, refs = refs[:halves], refs[halves:]
    whole_refs, refs = refs[:wholes], refs[wholes:]
    state_ref, grad_out, new_out = refs[0], refs[-2], refs[-1]
    for i in range(grad_out.shape[0]):
        parts = [ref[i] for ref in whole_refs]
        if halves:
            first = 2 * (i // 3)
            parts += [ref[0, i % 3] for ref in half_refs[first : first + 2]]
        total = parts[0].astype(F32)
        for part in parts[1:]:
            total = total + part.astype(F32)
        grad = total.astype(BF)
        grad_out[i] = grad
        new, _, _ = adam_step(
            state_ref[i, 0].astype(F32),
            state_ref[i, 1].astype(F32),
            state_ref[i, 2].astype(F32),
            grad.astype(F32),
            LEARN_RATE,
        )
        new_out[i] = new.astype(BF)


def weight_step(halves, wholes, states, *after):
    count = states.shape[0]
    shape = jax.ShapeDtypeStruct((count, ROWS, WIDTH), BF)
    return pl.pallas_call(
        functools.partial(weight_step_kernel, len(halves), len(wholes)),
        in_specs=[VM] * (len(halves) + len(wholes) + 1) + [ANY] * len(after),
        out_specs=[VM] * 2,
        out_shape=[shape, shape],
        compiler_params=pltpu.CompilerParams(vmem_limit_bytes=VMEM_LIMIT),
        cost_estimate=cost(0.0, 0.001),
        name="weight_step",
    )(*halves, *wholes, states, *after)


def moment_step_kernel(info_ref, a_ref, b_ref, first_ref, second_ref, *rest):
    one_ref, two_ref = rest[-2:]
    count = first_ref.shape[0]
    lead, live = info_ref[0] == 0, info_ref[1]
    for i in range(count):
        one, two = a_ref[i // 2].astype(F32), b_ref[i // 2].astype(F32)
        grad = jnp.where(lead if i % 2 == 0 else jnp.logical_not(lead), one, two)
        grad = jnp.where(pl.program_id(0) * count + i < live, grad, 0.0)
        one_ref[i] = FIRST_DECAY * first_ref[i] + (1.0 - FIRST_DECAY) * grad
        two_ref[i] = SECOND_DECAY * second_ref[i] + (1.0 - SECOND_DECAY) * grad * grad


def moment_step(info, a, b, first, second, *after):
    each = 4 if first.shape[0] % 4 == 0 else 2
    grads = pl.BlockSpec((each // 2, ROWS, WIDTH), lambda i, s: (i, 0, 0))
    slots = pl.BlockSpec((each, ROWS, WIDTH), lambda i, s: (i, 0, 0))
    shape = jax.ShapeDtypeStruct(first.shape, F32)
    return pl.pallas_call(
        moment_step_kernel,
        grid_spec=pltpu.PrefetchScalarGridSpec(
            num_scalar_prefetch=1,
            grid=(first.shape[0] // each,),
            in_specs=[grads, grads, slots, slots] + [ANY] * len(after),
            out_specs=[slots, slots],
        ),
        out_shape=[shape, shape],
        compiler_params=pltpu.CompilerParams(vmem_limit_bytes=VMEM_LIMIT),
        cost_estimate=cost(0.0, 0.001),
        name="moment_step",
    )(info, a, b, first, second, *after)


def pick_kernel(sizes, arrays, from_ref, *refs):
    outs, sem = refs[-1 - len(sizes) : -1], refs[-1]
    slot = 0
    for out, size in zip(outs, sizes):

        @pl.loop(0, size)
        def _(i, out=out, slot=slot):
            number, low = from_ref[slot + i], 0
            for array in refs[:arrays]:
                high = low + array.shape[0]

                @pl.when((number >= low) & (number < high))
                def _(array=array, low=low):
                    pltpu.make_async_copy(
                        array.at[number - low], out.at[i], sem.at[slot + i]
                    ).start()

                low = high

        slot += size
    slot = 0
    for out, size in zip(outs, sizes):

        @pl.loop(0, size)
        def _(i, out=out, slot=slot):
            pltpu.make_async_copy(refs[0].at[0], out.at[i], sem.at[slot + i]).wait()

        slot += size


def pick_blocks(source, arrays, sizes, *after):
    arrays = [array.reshape(-1, ROWS, WIDTH) for array in arrays]
    return pl.pallas_call(
        functools.partial(pick_kernel, sizes, len(arrays)),
        grid_spec=pltpu.PrefetchScalarGridSpec(
            num_scalar_prefetch=1,
            grid=(),
            in_specs=[ANY] * (len(arrays) + len(after)),
            out_specs=[VM] * len(sizes),
            scratch_shapes=[pltpu.SemaphoreType.DMA((sum(sizes),))],
        ),
        out_shape=[jax.ShapeDtypeStruct((size, ROWS, WIDTH), BF) for size in sizes],
        compiler_params=pltpu.CompilerParams(vmem_limit_bytes=VMEM_LIMIT),
        cost_estimate=cost(0.0, 0.001),
        name="pick_blocks",
    )(source, *arrays, *after)


def move_kernel(plan, *refs):
    for out, pieces in zip(refs[-len(plan) :], plan):
        at = 0
        for source, low, high in pieces:
            out[at : at + high - low] = refs[source][low:high]
            at += high - low


def move(plan, arrays, *after):
    return pl.pallas_call(
        functools.partial(move_kernel, plan),
        in_specs=[VM] * len(arrays) + [ANY] * len(after),
        out_specs=[VM] * len(plan),
        out_shape=[
            jax.ShapeDtypeStruct((sum(high - low for _, low, high in pieces), ROWS, WIDTH), BF)
            for pieces in plan
        ],
        compiler_params=pltpu.CompilerParams(vmem_limit_bytes=VMEM_LIMIT),
        cost_estimate=cost(0.0, 0.001),
        name="move",
    )(*arrays, *after)


ENDS = (((0, 0, 3),), ((1, 3, 6),))
TWO_ENDS = (((0, 0, 3), (0, 6, 9)), ((1, 3, 6), (1, 9, 12)))


def gather_blocks(mine, tasks):
    up, down = up_z(mine, 1), up_z(mine, 3)
    far = up_z(up, 1)
    own_x, own_y = swap_dp(mine), swap_y(mine)
    done = tasks[0](mine)
    end_x, end_y = move(ENDS, [own_x, own_y], *done)
    own = [mine, own_x, own_y, swap_y(end_x), swap_dp(end_y)]
    (near,) = move((((0, 0, 6), (1, 0, 6)),), [up, down], end_x)
    near_x, near_y = swap_dp(near), swap_y(near)
    done = tasks[1](near)
    done = tasks[2](*done, far)
    far_x, far_y = swap_dp(far), swap_y(far)
    end_x, end_y = move(TWO_ENDS, [near_x, near_y], *done)
    near = [near, near_x, near_y, swap_y(end_x), swap_dp(end_y)]
    end_x, end_y = move(ENDS, [far_x, far_y], end_x)
    far = [far, far_x, far_y, swap_y(end_x), swap_dp(end_y)]
    return own + far + near, end_x


PIECES = ((1, 288), (1, 288), (1, 288), (1, 144), (1, 144))
PIECES += PIECES + tuple((2 * number, rows) for number, rows in PIECES)
PIECES += PIECES


def piece_rows():
    me_d, me_f = lax.axis_index("dp"), lax.axis_index("fsdp")
    rows = []
    for core in (0, 1):
        for steps in ((0,), (2,), (1, 3)):
            for dx, dy, low in ((0, 0, 0), (1, 0, 0), (0, 1, 0), (1, 1, 0), (1, 1, 144)):
                for step in steps:
                    z = (me_f // 4 - step) % 4
                    y, c = (me_f // 2 + dy) % 2, (me_f + core) % 2
                    rows.append((((z * 2 + y) * 2 + c) * 2 + (me_d + dx) % 2) * 288 + low)
    return jnp.stack(rows).astype(jnp.int32)


def gather_stack(weights, early):
    half = weights.shape[0] // 2
    mine = lax.dynamic_slice(weights, (lax.axis_index("dp") * half, 0), (half, WIDTH))
    tasks = [lambda *after: early, lambda *after: after, lambda *after: after]
    arrays, _ = gather_blocks(mine.reshape(-1, ROWS, WIDTH), tasks)
    arrays += [swap_core(array) for array in arrays]
    return [array.reshape(-1, WIDTH) for array in arrays]


def gathered_place(group, spot, turn):
    ahead, dx, dy, core = apart(group, spot)
    steps = (4 - ahead) % 4
    side, pair = dx + 2 * dy, steps // 2
    plain = jnp.where(steps == 2, 24, 0) + side * 6 + turn
    corner = jnp.where(turn < 3, 84 + pair * 3 + turn, 90 + pair * 3 + turn - 3)
    near = jnp.where(side == 3, corner, 48 + side * 12 + pair * 6 + turn)
    steps_odd = steps % 2 == 1
    return jnp.where(steps_odd, near, plain), core == 0


def local(
    groups,
    tokens,
    masked_pos,
    masked_count,
    out_grad,
    weights,
    vectors,
    owner_list,
    master_slots,
    first_slots,
    second_slots,
    vector_first,
    vector_second,
):
    pages = masked_pos.shape[0]
    capacity = master_slots.shape[0]
    held = weights.shape[0] // ROWS
    spread = lax.axis_size("fsdp")
    me_f = lax.axis_index("fsdp")
    ids = groups * spread
    each = NBLK // ids
    lanes = -(-capacity // ids)
    my_group = lax.axis_index("dp") if groups > 1 else 0
    me = me_f * groups + my_group

    blocks = jnp.arange(NBLK, dtype=jnp.int32)
    lower = owner_list[None, :] < owner_list[:, None]
    tied = (owner_list[None, :] == owner_list[:, None]) & (blocks[None, :] < blocks[:, None])
    rank = jnp.sum((lower | tied).astype(jnp.int32), axis=1)
    group, spot, turn = rank % groups, rank % ids // groups, rank // ids
    place = (group * spread + spot) * each + turn
    direct = groups == 2 and spread == 16 and each == 6 and pages == 3
    if direct:
        sizes = SIZES
        put = relative_place(group, spot, turn)
    else:
        sizes, put = (NBLK,), place
    owners = jnp.arange(spread, dtype=jnp.int32)
    start = jnp.sum((owner_list[None, :] < owners[:, None]).astype(jnp.int32), axis=1)
    count = jnp.sum((owner_list[None, :] == owners[:, None]).astype(jnp.int32), axis=1)
    lane = jnp.arange(lanes, dtype=jnp.int32) * ids

    my_start, my_count = start[me_f], count[me_f]
    slot_to = ((owners * groups + my_group - my_start) % ids)[:, None] + lane[None, :]
    slot_to = jnp.minimum(slot_to, capacity - 1).reshape(-1)
    slot_at = ((me - start) % ids)[:, None] + lane[None, :]
    send_to = jnp.clip((start[:, None] + slot_at) // ids, 0, each - 1).reshape(-1)
    my_rank = me + ids * jnp.arange(each, dtype=jnp.int32)
    my_owner = jnp.sum((start + count)[None, :] <= my_rank[:, None], axis=1).astype(jnp.int32)
    my_lane = (my_rank - start[my_owner]) // ids
    state_at = my_owner * lanes + my_lane
    lead = (my_group - my_start) % 2 if groups > 1 else 0
    slots = jnp.arange(capacity // 2, dtype=jnp.int32) * 2

    def grad_at(first):
        which = slots + first
        return ((my_start + which) % ids // groups) * lanes + which // ids

    info = jnp.stack([jnp.asarray(lead, jnp.int32), my_count])

    states = jnp.stack(
        [
            jnp.take(master_slots, slot_to, axis=0, mode="clip").astype(BF),
            jnp.take(first_slots, slot_to, axis=0, mode="clip").astype(BF),
            jnp.take(second_slots, slot_to, axis=0, mode="clip").astype(BF),
        ],
        axis=1,
    )

    live = jnp.arange(MASKM, dtype=jnp.int32)[None, :] < masked_count[:, None]
    pos = jnp.pad(
        jnp.where(live, masked_pos, -1), ((0, 0), (0, PAD - MASKM)), constant_values=-1
    )[:, :, None]
    cot = jnp.pad(
        jnp.where(live[:, :, None], out_grad, jnp.zeros((), BF)), ((0, 0), (0, PAD - MASKM), (0, 0))
    ).reshape(pages * PAD, WIDTH)

    if direct:
        pieces, rows, counts = gather_stack(weights, (states, cot)), piece_rows(), PIECES
        last, states = lax.optimization_barrier((pieces[-1], states))
        pieces = pieces[:-1] + [last]
    else:
        pieces, rows, counts = [lax.all_gather(weights, "fsdp", axis=0, tiled=True)], jnp.zeros((1,), jnp.int32), ()
    states = lax.all_to_all(states, "fsdp", 0, 0, tiled=True)
    q, k, v, tm, qm, cm, *stack = project(tokens, pos, vectors, pieces, rows, counts)
    stack = stack[0] if direct else pieces[0]
    gr, gc, gv, *dws = masked_part(put, sizes, tm, cm, cot, vectors, stack)
    dq, dk, dv, gv_attn, *dws = attention_back(put, tokens, k, v, tm, qm, gc, dws)
    grad_vectors = jnp.concatenate([gv_attn[0:2], gv[2:12]], axis=0)
    dws, states = lax.optimization_barrier((dws, states))
    grad_vectors = jnp.sum(lax.all_gather(grad_vectors, ("dp", "fsdp")), axis=0)
    outs = []

    def page_task(*after):
        outs[:] = [
            forward_page(page_task.next, tokens, q, k, v, vectors, stack, tuple(outs), *after)
        ]
        page_task.next += 1
        return outs[0]

    def grad_task(*after):
        outs.append(input_grad(pos, dq, dk, dv, gr, stack, *after))
        return outs[-1]

    page_task.next = 0
    tasks = [page_task] * pages + [grad_task]
    states = jnp.take(states, state_at, axis=0, mode="clip")
    if direct:
        halves, wholes, done = reduce_blocks(dws, tasks)
    else:
        if groups > 1:
            mine = lax.psum_scatter(dws[0], ("dp", "fsdp"), scatter_dimension=0, tiled=True)
        else:
            mine = lax.psum_scatter(dws[0], "fsdp", scatter_dimension=0, tiled=True)
            mine = lax.psum(mine, "dp")
        for task in tasks:
            done = task()
        halves, wholes = (), (mine,)
    mine, new_mine = weight_step(halves, wholes, states, done, grad_vectors)

    held_first = me_f * held

    def held_table(table, first):
        return lax.dynamic_slice(table, (first,), (held,))

    def exchange(*after):
        (send,) = pick_blocks(send_to, [mine], (spread * lanes,), *after)
        return send, lax.all_to_all(send, "fsdp", 0, 0, tiled=True)

    if direct:
        kept = []

        def send_task(*after):
            send, owned = exchange(*after)
            kept.append(owned)
            return (send,)

        def swap_task(*after):
            (even,) = pick_blocks(grad_at(lead), kept, (capacity // 2,), *after)
            kept[:] = even, swap_dp(even)
            return (even,)

        def last_task(*after):
            return (tasks[pages](*after),)

        arrays, _ = gather_blocks(new_mine, (last_task, send_task, swap_task))
        at, near = gathered_place(group, spot, turn)
        at = jnp.where(near, at, 0)
        sibling = (me_f + 1 - 2 * (me_f % 2)) * held
        table = jnp.concatenate([held_table(at, held_first), held_table(at, sibling)])
        mine, handed = pick_blocks(table, arrays, (held, held))
        new_first, new_second = moment_step(info, *kept, first_slots, second_slots, mine)
        handed = swap_core(handed)
        ours = held_table(near, held_first)
        new_weights = jnp.where(ours[:, None, None], mine, handed).astype(F32)
    else:
        _, owned = exchange()
        axes = ("dp", "fsdp") if groups > 1 else "fsdp"
        new_all = lax.all_gather(new_mine, axes, axis=0, tiled=True)
        (kept,) = pick_blocks(held_table(place, held_first), [new_all], (held,))
        new_weights = kept.astype(F32)
        if groups > 1:
            (even,) = pick_blocks(grad_at(lead), [owned], (capacity // 2,))
            odd = swap_dp(even)
        else:
            even, odd = pick_blocks(
                jnp.concatenate([grad_at(0), grad_at(1)]), [owned], (capacity // 2, capacity // 2)
            )
        new_first, new_second = moment_step(info, even, odd, first_slots, second_slots)
    layer_out, token_grad = outs
    new_weights = new_weights.reshape(held * ROWS, WIDTH)
    new_vectors, new_vector_first, new_vector_second = adam_step(
        vectors, vector_first, vector_second, grad_vectors, VECTOR_RATE
    )
    return (
        layer_out,
        token_grad,
        new_weights,
        new_first,
        new_second,
        new_vectors,
        new_vector_first,
        new_vector_second,
    )


def solution(mesh):
    dp, fsdp = mesh.shape["dp"], mesh.shape["fsdp"]
    groups = 2 if dp == 2 and NBLK % (2 * fsdp) == 0 else 1
    both = ("dp", "fsdp")
    return jax.shard_map(
        functools.partial(local, groups),
        mesh=mesh,
        in_specs=(
            P(both, None),
            P(both, None),
            P(both),
            P(both, None, None),
            P("fsdp", None),
            P(),
            P(),
            P("fsdp", None, None),
            P("fsdp", None, None),
            P("fsdp", None, None),
            P(),
            P(),
        ),
        out_specs=(
            P(both, None),
            P(both, None),
            P("fsdp", None),
            P("fsdp", None, None),
            P("fsdp", None, None),
            P(),
            P(),
            P(),
        ),
        check_vma=False,
    )
```

time: 667 us -> 466 us (0.70)
  waiting for transfers between devices: 428 us -> 119 us
  starting transfers between devices: 12.1 us -> 70.8 us
  Pallas kernels: 164 us -> 206 us
  local copies, waits for them, and re-layouts: 19.9 us -> 29.5 us
    all_gather x3 -> x0, waiting for transfers between devices: 192 us -> none  [the longest x1 110 us: local(): stack = lax.all_gather(weights, 'fsdp', axis=0, tiled=True)]
    reduce_scatter x1 -> x0, waiting for transfers between devices: 161 us -> none  [local(): mine = lax.psum_scatter(dw, ('dp', 'fsdp'), scatter_dimension=0, tiled=True)]
    ppermute x0 -> x65, waiting for transfers between devices: none -> 118 us  [the longest x19 54.8 us: swap_dp(): return lax.ppermute(x, 'dp', [(0, 1), (1, 0)])]
    all_to_all x1, waiting for transfers between devices: 63.9 us -> 0.01 us  [local(): states = lax.all_to_all(states, 'fsdp', 0, 0, tiled=True)]
    ppermute x0 -> x65, starting transfers between devices: none -> 61.9 us  [the longest x19 22.4 us: swap_dp(): return lax.ppermute(x, 'dp', [(0, 1), (1, 0)])]
    pallas_call x4 -> x24, Pallas kernels: 75.4 us -> 124 us  [the longest x3 43.3 us: forward_page(): pl.pallas_call(forward_kernel, grid=(1,), in_specs=[page, page, page, pag...]
    all_to_all x1, waiting for transfers between devices: 9.82 us -> 0.01 us  [exchange(): return (send, lax.all_to_all(send, 'fsdp', 0, 0, tiled=True))]
    unnamed x18 -> x100, local copies, waits for them, and re-layouts: 2.34 us -> 10.3 us
  transfers between devices with their start and end apart: 7 -> 68, of which waited for: 5 -> 19; matrix products, arithmetic and copies ran while one was open for 5% -> 7% of each run, Pallas kernels for 11% -> 42%
where the time goes in v3:
time: 466 us; the launch traced here: 458 us
  Pallas kernels  206 us (44%)
  waiting for transfers between devices  119 us (26%)
  starting transfers between devices  70.8 us (15%)
  local copies, waits for them, and re-layouts  29.5 us (6%)
  other arithmetic  18.2 us (4%)
  between operations  15.6 us (3%)
    ppermute x19, waiting for transfers between devices, swap_dp(): return lax.ppermute(x, 'dp', [(0, 1), (1, 0)])  54.8 us
    pallas_call x3, Pallas kernels, forward_page(): pl.pallas_call(forward_kernel, grid=(1,), in_specs=[page, page, page, pag...  43.3 us
    pallas_call x1, Pallas kernels, attention_back(): pl.pallas_call(attention_back_kernel, grid_spec=pltpu.PrefetchScalarGridS...  30.9 us
    pallas_call x1, Pallas kernels, masked_part(): pl.pallas_call(masked_kernel, grid_spec=pltpu.PrefetchScalarGridSpec(num_...  30.4 us
    ppermute x9, waiting for transfers between devices, up_z(): lax.ppermute(x, 'fsdp', [(f, (f + 4 * steps) % 16) for f in range(16)])  29.4 us
    ppermute x18, waiting for transfers between devices, swap_y(): return lax.ppermute(x, 'fsdp', [(f, f ^ 2) for f in range(16)])  27.1 us
    pallas_call x1, Pallas kernels, project(): pl.pallas_call(functools.partial(project_kernel, counts), grid_spec=pltpu...  25.2 us
    ppermute x19, starting transfers between devices, swap_dp(): return lax.ppermute(x, 'dp', [(0, 1), (1, 0)])  22.4 us
  transfers between devices with their start and end apart: 68, of which 19 were waited for; matrix products, arithmetic and copies ran while one was open for 7% of the time, Pallas kernels for 42%

profile of v3, /device:TPU:0, one launch (start us, length us, event | category | flops | bytes accessed | tf_op | source)
XLA Modules:
  0.0 458.5 jit_solution(1960202881102203632)
XLA Ops:
  19.5 3.7 gather_fusion.2
  23.2 3.7 gather_fusion.1
  30.7 3.2 pad_maximum_fusion.refs_2_
  43.5 22.3 %collective-permute-done.2 = bf16[3,48,768]{2,1,0:T(8,128)(2,1)S(1)} collective-permute-done((bf16[3,48,768]{2,1,0:T(8,128)(2,1)}, bf16[3,48,768]{2,1,0:T(8,128)(2,1)S(1)}, u32[]{:S(2)}, u32[]{:S(2)}) %collective-permute-start.2) | collective-permute-done | bytes 221216 | tf_op jit(solution)/shard_map/ppermute | solution.py:531
  71.9 7.4 %collective-permute-done.6.refs_0_ = bf16[6,48,768]{2,1,0:T(8,128)(2,1)S(1)} collective-permute-done((bf16[6,48,768]{2,1,0:T(8,128)(2,1)S(1)}, bf16[6,48,768]{2,1,0:T(8,128)(2,1)S(1)}, u32[]{:S(2)}, u32[]{:S(2)}) %collective-permute-start.6) | collective-permute-done | bytes 442400 | tf_op jit(solution)/shard_map/ppermute | solution.py:527
  83.9 4.0 collective-permute-done.14
  90.7 5.6 %collective-permute-done.12 = bf16[3,48,768]{2,1,0:T(8,128)(2,1)S(1)} collective-permute-done((bf16[3,48,768]{2,1,0:T(8,128)(2,1)}, bf16[3,48,768]{2,1,0:T(8,128)(2,1)S(1)}, u32[]{:S(2)}, u32[]{:S(2)}) %collective-permute-start.12) | collective-permute-done | bytes 221216 | tf_op jit(solution)/shard_map/ppermute | solution.py:527
  98.6 4.7 %all-to-all-start = ((bf16[16,3,48,768]{3,2,1,0:T(8,128)(2,1)}), bf16[16,3,48,768]{3,2,1,0:T(8,128)(2,1)S(1)}, u32[]{:S(2)}, u32[]{:S(2)}) async-start(bf16[16,3,48,768]{3,2,1,0:T(8,128)(2,1)} %pad_maximum_fusion.refs_2_), calls=%async_computation | async-start | bytes 7077888 | tf_op jit(solution)/shard_map/all_to_all | solution.py:933
  108.0 25.2 %project.1 = (bf16[1536,768]{1,0:T(8,128)(2,1)}, bf16[1536,768]{1,0:T(8,128)(2,1)}, bf16[1536,768]{1,0:T(8,128)(2,1)}, bf16[384,768]{1,0:T(8,128)(2,1)}, bf16[38...) custom-call(s32[40]{0:T(128)} %stack.175.rows_ref, s32[3,128,1]{2,1,0:T(8,128)} %copy.30.pos_ref, ...), custom_call_target="tpu_custom_call" | custom-call | flops 17999998976 | bytes 20000000 | tf_op jit(solution)/shard_map/project/pallas_call | solution.py:193
  133.2 30.4 %masked.1 = (f32[384,768]{1,0:T(8,128)}, bf16[384,768]{1,0:T(8,128)(2,1)}, f32[16,768]{1,0:T(8,128)}, bf16[96,48,768]{2,1,0:T(8,128)(2,1)}, bf16[24,48,768]{2,1,...) custom-call(s32[192]{0:T(256)} %fusion.5.place_ref, ...), custom_call_target="tpu_custom_call" | custom-call | flops 24000000000 | bytes 30000000 | tf_op jit(solution)/shard_map/masked/pallas_call | solution.py:299
  163.6 30.9 %attention_back.1 = (bf16[384,768]{1,0:T(8,128)(2,1)}, bf16[1536,768]{1,0:T(8,128)(2,1)}, bf16[1536,768]{1,0:T(8,128)(2,1)}, f32[8,768]{1,0:T(8,128)}, bf16[96,4...) custom-call(s32[192]{0:T(256)} %fusion.5.place_ref, ...), custom_call_target="tpu_custom_call", output_to_operand_aliasing={{4}: (7, {}), {5}: (8, {}), {6}: (9, {}), {7}: (10, {})} | custom-call | flops 24999999488 | bytes 30000000 | tf_op jit(solution)/shard_map/attention_back/pallas_call | solution.py:392
  197.4 6.2 %collective-permute-done.31 = bf16[24,48,768]{2,1,0:T(8,128)(2,1)} collective-permute-done((bf16[24,48,768]{2,1,0:T(8,128)(2,1)}, bf16[24,48,768]{2,1,0:T(8,128)(2,1)}, u32[]{:S(2)}, u32[]{:S(2)}) %collective-permute-start.31) | collective-permute-done | bytes 1769504 | tf_op jit(solution)/shard_map/ppermute | solution.py:535
  203.7 3.3 core_sum.3
  210.1 9.6 %collective-permute-done.32.to_a_ref = bf16[1,6,48,768]{3,2,1,0:T(8,128)(2,1)S(1)} collective-permute-done((bf16[1,6,48,768]{3,2,1,0:T(8,128)(2,1)}, bf16[1,6,48,768]{3,2,1,0:T(8,128)(2,1)S(1)}, u32[]{:S(2)}, u32[]{:S(2)}) %collective-permute-start.32) | collective-permute-done | bytes 442400 | tf_op jit(solution)/shard_map/ppermute | solution.py:527
  223.2 4.9 %core_sum.4 = (bf16[2,6,48,768]{3,2,1,0:T(8,128)(2,1)}, bf16[2,6,48,768]{3,2,1,0:T(8,128)(2,1)}, bf16[2,6,48,768]{3,2,1,0:T(8,128)(2,1)}, bf16[2,6,48,768]{3,2,1,0:T(8,128)(2,1)}) custom-call(bf16[4,4,6,48,768]{4,3,2,1,0:T(8,128)(2,1)} %bitcast.109, bf16[2,4,6,48,768]{4,3,2,1,0:T(8,128)(2,1)} %bitcast.78.from_ref, ...), custom_call_target="tpu_custom_call" | custom-call | bytes 1000 | tf_op jit(solution)/shard_map/core_sum/pallas_call | solution.py:571
  232.7 14.4 %forward_page.3.rest_0_ = bf16[1536,768]{1,0:T(8,128)(2,1)} custom-call(bf16[1536,768]{1,0:T(8,128)(2,1)} %tok_ref.9, bf16[1536,768]{1,0:T(8,128)(2,1)} %get-tuple-element.88.q_ref, bf16[1536,768]{1,0:T(8,128)(2,1)} %get-tuple-element.89.k_ref, bf16[1536,768]{1,0:T(8,128)(2,1)} %get-tuple-element.90.v_ref, f32[12,768]{1,0:T(8,128)} %vec_ref.9, ...), custom_call_target="tpu_custom_call" | custom-call | bytes 1000 | tf_op jit(solution)/shard_map/forward_page/pallas_call | solution.py:455
  247.2 6.7 %collective-permute-done.37.to_a_ref = bf16[2,6,48,768]{3,2,1,0:T(8,128)(2,1)} collective-permute-done((bf16[2,6,48,768]{3,2,1,0:T(8,128)(2,1)}, bf16[2,6,48,768]{3,2,1,0:T(8,128)(2,1)}, u32[]{:S(2)}, u32[]{:S(2)}) %collective-permute-start.37) | collective-permute-done | bytes 884768 | tf_op jit(solution)/shard_map/ppermute | solution.py:527
  254.7 3.1 first_sum.4
  266.1 3.3 core_sum.5
  271.1 14.4 %forward_page.4.rest_0_ = bf16[1536,768]{1,0:T(8,128)(2,1)} custom-call(bf16[1536,768]{1,0:T(8,128)(2,1)} %tok_ref.9, bf16[1536,768]{1,0:T(8,128)(2,1)} %get-tuple-element.88.q_ref, bf16[1536,768]{1,0:T(8,128)(2,1)} %get-tuple-element.89.k_ref, bf16[1536,768]{1,0:T(8,128)(2,1)} %get-tuple-element.90.v_ref, ...), custom_call_target="tpu_custom_call", output_to_operand_aliasing={{}: (6, {})} | custom-call | bytes 1000 | tf_op jit(solution)/shard_map/forward_page/pallas_call | solution.py:455
  303.4 14.4 %forward_page.5.refs_8_ = bf16[1536,768]{1,0:T(8,128)(2,1)} custom-call(bf16[1536,768]{1,0:T(8,128)(2,1)} %tok_ref.9, bf16[1536,768]{1,0:T(8,128)(2,1)} %get-tuple-element.88.q_ref, bf16[1536,768]{1,0:T(8,128)(2,1)} %get-tuple-element.89.k_ref, bf16[1536,768]{1,0:T(8,128)(2,1)} %get-tuple-element.90.v_ref, ...), custom_call_target="tpu_custom_call", output_to_operand_aliasing={{}: (6, {})} | custom-call | bytes 1000 | tf_op jit(solution)/shard_map/forward_page/pallas_call | solution.py:455
  317.9 4.3 weight_step.1
  323.8 3.8 collective-permute-start.56
  327.6 11.5 %input_grad.1.refs_2_ = f32[1536,768]{1,0:T(8,128)} custom-call(s32[3,128,1]{2,1,0:T(8,128)} %copy.30.pos_ref, bf16[384,768]{1,0:T(8,128)(2,1)} %get-tuple-element.131.dq_ref, bf16[1536,768]{1,0:T(8,128)(2,1)} %get-tuple-element.132.dk_ref, bf16[1536,768]{1,0:T(8,128)(2,1)} %get-tuple-element.133.dv_ref, f32[384,768]{1,0:T(8,128)} %get-tuple-element.134.gr_ref, ...), custom_call_target="tpu_custom_call" | custom-call | bytes 1000 | tf_op jit(solution)/shard_map/input_grad/pallas_call | solution.py:497
  345.6 3.3 pick_blocks.3.refs_1_
  348.9 3.7 all-to-all-start.1
  357.1 29.2 %collective-permute-done.53.refs_2_.refs_5_ = bf16[6,48,768]{2,1,0:T(8,128)(2,1)} collective-permute-done((bf16[6,48,768]{2,1,0:T(8,128)(2,1)S(1)}, bf16[6,48,768]{2,1,0:T(8,128)(2,1)}, u32[]{:S(2)}, u32[]{:S(2)}) %collective-permute-start.53) | collective-permute-done | bytes 442400 | tf_op jit(solution)/shard_map/ppermute | solution.py:539
  407.2 10.2 %collective-permute-done.51.refs_4_ = bf16[3,48,768]{2,1,0:T(8,128)(2,1)S(1)} collective-permute-done((bf16[3,48,768]{2,1,0:T(8,128)(2,1)}, bf16[3,48,768]{2,1,0:T(8,128)(2,1)S(1)}, u32[]{:S(2)}, u32[]{:S(2)}) %collective-permute-start.51) | collective-permute-done | bytes 221216 | tf_op jit(solution)/shard_map/ppermute | solution.py:527
  418.4 3.8 collective-permute-done.60.refs_9_
  423.9 4.4 pick_blocks.5
  431.0 7.5 %collective-permute-done.64.b_ref = bf16[12,48,768]{2,1,0:T(8,128)(2,1)S(1)} collective-permute-done((bf16[12,48,768]{2,1,0:T(8,128)(2,1)S(1)}, bf16[12,48,768]{2,1,0:T(8,128)(2,1)S(1)}, u32[]{:S(2)}, u32[]{:S(2)}) %collective-permute-start.64) | collective-permute-done | bytes 884768 | tf_op jit(solution)/shard_map/ppermute | solution.py:527
  439.4 9.0 %moment_step.1 = (f32[24,48,768]{2,1,0:T(8,128)}, f32[24,48,768]{2,1,0:T(8,128)}) custom-call(s32[2]{0:T(128)} %pad_add_fusion.1.info_ref, bf16[12,48,768]{2,1,0:T(8,128)(2,1)} %pick_blocks.4.refs_2_.a_ref, bf16[12,48,768]{2,1,0:T(8,128)(2,1)} %copy-done.10, f32[24,48,768]{2,1,0:T(8,128)} %first_ref.1, f32[24,48,768]{2,1,0:T(8,128)} %second_ref.1, ...), custom_call_target="tpu_custom_call" | custom-call | bytes 1000 | tf_op jit(solution)/shard_map/moment_step/pallas_call | solution.py:702
  (274 shorter events, 130.8 us)
Async XLA Ops:
  9.2 24.8 %collective-permute-start = (bf16[6,48,768]{2,1,0:T(8,128)(2,1)}, bf16[6,48,768]{2,1,0:T(8,128)(2,1)}, u32[]{:S(2)}, u32[]{:S(2)}) collective-permute-start(bf16[6,48,768]{2,1,0:T(8,128)(2,1)} %bitcast.41), channel_id=1, source_target_pairs={{0,16},{16,0},{1,17},{17,1},{2,18},{18,2},{3,19},{19,3},{4,20},{20... | collective-permute-start | bytes 1327112 | tf_op jit(solution)/shard_map/ppermute | solution.py:527
  12.1 21.9 %collective-permute-start.1 = (bf16[6,48,768]{2,1,0:T(8,128)(2,1)}, bf16[6,48,768]{2,1,0:T(8,128)(2,1)}, u32[]{:S(2)}, u32[]{:S(2)}) collective-permute-start(bf16[6,48,768]{2,1,0:T(8,128)(2,1)} %bitcast.41), channel_id=1, source_target_pairs={{0,2},{1,3},{2,0},{3,1},{4,6},{5,7},{6,4},{7,5},{8,10},{9,11},{10,... | collective-permute-start | bytes 1327112 | tf_op jit(solution)/shard_map/ppermute | solution.py:531
  13.6 22.3 %collective-permute-start.4 = (bf16[6,48,768]{2,1,0:T(8,128)(2,1)}, bf16[6,48,768]{2,1,0:T(8,128)(2,1)}, u32[]{:S(2)}, u32[]{:S(2)}) collective-permute-start(bf16[6,48,768]{2,1,0:T(8,128)(2,1)} %bitcast.41), channel_id=1, source_target_pairs={{0,4},{1,5},{2,6},{3,7},{4,8},{5,9},{6,10},{7,11},{8,12},{9,13},{1... | collective-permute-start | bytes 1327112 | tf_op jit(solution)/shard_map/ppermute | solution.py:539
  38.2 29.6 %collective-permute-start.9 = (bf16[12,48,768]{2,1,0:T(8,128)(2,1)}, bf16[12,48,768]{2,1,0:T(8,128)(2,1)S(1)}, u32[]{:S(2)}, u32[]{:S(2)}) collective-permute-start(bf16[12,48,768]{2,1,0:T(8,128)(2,1)} %move.9.refs_2_), channel_id=1, source_target_pairs={{0,16},{16,0},{1,17},{17,1},{2,18},{18,2},{3,19},{19,3},{4,20},{20... | collective-permute-start | bytes 2654216 | tf_op jit(solution)/shard_map/ppermute | solution.py:527
  38.7 29.1 %collective-permute-start.10 = (bf16[12,48,768]{2,1,0:T(8,128)(2,1)}, bf16[12,48,768]{2,1,0:T(8,128)(2,1)S(1)}, u32[]{:S(2)}, u32[]{:S(2)}) collective-permute-start(bf16[12,48,768]{2,1,0:T(8,128)(2,1)} %move.9.refs_2_), channel_id=1, source_target_pairs={{0,2},{1,3},{2,0},{3,1},{4,6},{5,7},{6,4},{7,5},{8,10},{9,11},{10,... | collective-permute-start | bytes 2654216 | tf_op jit(solution)/shard_map/ppermute | solution.py:531
  39.2 27.0 %collective-permute-start.5 = (bf16[6,48,768]{2,1,0:T(8,128)(2,1)}, bf16[6,48,768]{2,1,0:T(8,128)(2,1)S(1)}, u32[]{:S(2)}, u32[]{:S(2)}) collective-permute-start(bf16[6,48,768]{2,1,0:T(8,128)(2,1)} %collective-permute-done.4.refs_0_), channel_id=1, source_target_pairs={{0,4},{1,5},{2,6},{3,7},{4,8},{5,9},{6,10},{7,11},{8,12},{9,13},{1... | collective-permute-start | bytes 1327112 | tf_op jit(solution)/shard_map/ppermute | solution.py:539
  40.4 25.3 %collective-permute-start.2 = (bf16[3,48,768]{2,1,0:T(8,128)(2,1)}, bf16[3,48,768]{2,1,0:T(8,128)(2,1)S(1)}, u32[]{:S(2)}, u32[]{:S(2)}) collective-permute-start(bf16[3,48,768]{2,1,0:T(8,128)(2,1)} %get-tuple-element.81.refs_2_), channel_id=1, source_target_pairs={{0,2},{1,3},{2,0},{3,1},{4,6},{5,7},{6,4},{7,5},{8,10},{9,11},{10,... | collective-permute-start | bytes 663560 | tf_op jit(solution)/shard_map/ppermute | solution.py:531
  41.9 23.8 %collective-permute-start.3 = (bf16[3,48,768]{2,1,0:T(8,128)(2,1)}, bf16[3,48,768]{2,1,0:T(8,128)(2,1)S(1)}, u32[]{:S(2)}, u32[]{:S(2)}) collective-permute-start(bf16[3,48,768]{2,1,0:T(8,128)(2,1)} %get-tuple-element.82), channel_id=1, source_target_pairs={{0,16},{16,0},{1,17},{17,1},{2,18},{18,2},{3,19},{19,3},{4,20},{20... | collective-permute-start | bytes 663560 | tf_op jit(solution)/shard_map/ppermute | solution.py:527
  67.8 22.2 %collective-permute-start.25 = (bf16[12,48,768]{2,1,0:T(8,128)(2,1)}, bf16[12,48,768]{2,1,0:T(8,128)(2,1)}, u32[]{:S(2)}, u32[]{:S(2)}) collective-permute-start(bf16[12,48,768]{2,1,0:T(8,128)(2,1)} %move.9.refs_2_), channel_id=1, source_target_pairs={{0,1},{1,0},{2,3},{3,2},{4,5},{5,4},{6,7},{7,6},{8,9},{9,8},{10,11... | collective-permute-start | bytes 2654216 | tf_op jit(solution)/shard_map/ppermute | solution.py:535
  98.6 95.9 %all-to-all-start = ((bf16[16,3,48,768]{3,2,1,0:T(8,128)(2,1)}), bf16[16,3,48,768]{3,2,1,0:T(8,128)(2,1)S(1)}, u32[]{:S(2)}, u32[]{:S(2)}) async-start(bf16[16,3,48,768]{3,2,1,0:T(8,128)(2,1)} %pad_maximum_fusion.refs_2_), calls=%async_computation | async-start | bytes 7077888 | tf_op jit(solution)/shard_map/all_to_all | solution.py:933
  103.2 196.3 %all-gather.4.cloned.1.call-start = ((), (), s32[]{:S(2)}) async-start(), calls=%async_computation.2 | async-start | bytes 1622016 | tf_op jit(solution)/shard_map/all_gather | solution.py:940
  194.5 28.7 %collective-permute-start.30 = (bf16[48,48,768]{2,1,0:T(8,128)(2,1)}, bf16[48,48,768]{2,1,0:T(8,128)(2,1)}, u32[]{:S(2)}, u32[]{:S(2)}) collective-permute-start(bf16[48,48,768]{2,1,0:T(8,128)(2,1)} %get-tuple-element.106), channel_id=1, source_target_pairs={{0,1},{1,0},{2,3},{3,2},{4,5},{5,4},{6,7},{7,6},{8,9},{9,8},{10,11... | collective-permute-start | bytes 10616840 | tf_op jit(solution)/shard_map/ppermute | solution.py:535
  195.1 71.0 %collective-permute-start.34 = (bf16[24,48,768]{2,1,0:T(8,128)(2,1)}, bf16[24,48,768]{2,1,0:T(8,128)(2,1)}, u32[]{:S(2)}, u32[]{:S(2)}) collective-permute-start(bf16[24,48,768]{2,1,0:T(8,128)(2,1)} %get-tuple-element.114), channel_id=1, source_target_pairs={{0,1},{1,0},{2,3},{3,2},{4,5},{5,4},{6,7},{7,6},{8,9},{9,8},{10,11... | collective-permute-start | bytes 5308424 | tf_op jit(solution)/shard_map/ppermute | solution.py:535
  228.1 25.8 %collective-permute-start.37 = (bf16[2,6,48,768]{3,2,1,0:T(8,128)(2,1)}, bf16[2,6,48,768]{3,2,1,0:T(8,128)(2,1)}, u32[]{:S(2)}, u32[]{:S(2)}) collective-permute-start(bf16[2,6,48,768]{3,2,1,0:T(8,128)(2,1)} %get-tuple-element.113.rest_0_), channel_id=1, source_target_pairs={{0,16},{16,0},{1,17},{17,1},{2,18},{18,2},{3,19},{19,3},{4,20},{20... | collective-permute-start | bytes 2654216 | tf_op jit(solution)/shard_map/ppermute | solution.py:527
  229.0 25.7 %collective-permute-start.38 = (bf16[2,6,48,768]{3,2,1,0:T(8,128)(2,1)}, bf16[2,6,48,768]{3,2,1,0:T(8,128)(2,1)}, u32[]{:S(2)}, u32[]{:S(2)}) collective-permute-start(bf16[2,6,48,768]{3,2,1,0:T(8,128)(2,1)} %get-tuple-element.120), channel_id=1, source_target_pairs={{0,2},{1,3},{2,0},{3,1},{4,6},{5,7},{6,4},{7,5},{8,10},{9,11},{10,... | collective-permute-start | bytes 2654216 | tf_op jit(solution)/shard_map/ppermute | solution.py:531
  230.9 30.0 %collective-permute-start.35 = (bf16[1,3,48,768]{3,2,1,0:T(8,128)(2,1)}, bf16[1,3,48,768]{3,2,1,0:T(8,128)(2,1)S(1)}, u32[]{:S(2)}, u32[]{:S(2)}) collective-permute-start(bf16[1,3,48,768]{3,2,1,0:T(8,128)(2,1)} %get-tuple-element.112.rest_0_), channel_id=1, source_target_pairs={{0,2},{1,3},{2,0},{3,1},{4,6},{5,7},{6,4},{7,5},{8,10},{9,11},{10,... | collective-permute-start | bytes 663560 | tf_op jit(solution)/shard_map/ppermute | solution.py:531
  231.0 29.8 %collective-permute-start.36 = (bf16[1,3,48,768]{3,2,1,0:T(8,128)(2,1)}, bf16[1,3,48,768]{3,2,1,0:T(8,128)(2,1)S(1)}, u32[]{:S(2)}, u32[]{:S(2)}) collective-permute-start(bf16[1,3,48,768]{3,2,1,0:T(8,128)(2,1)} %get-tuple-element.117), channel_id=1, source_target_pairs={{0,16},{16,0},{1,17},{17,1},{2,18},{18,2},{3,19},{19,3},{4,20},{20... | collective-permute-start | bytes 663560 | tf_op jit(solution)/shard_map/ppermute | solution.py:527
  257.8 27.7 %collective-permute-start.41 = (bf16[2,3,48,768]{3,2,1,0:T(8,128)(2,1)}, bf16[2,3,48,768]{3,2,1,0:T(8,128)(2,1)}, u32[]{:S(2)}, u32[]{:S(2)}) collective-permute-start(bf16[2,3,48,768]{3,2,1,0:T(8,128)(2,1)} %get-tuple-element.121.rest_0_), channel_id=1, source_target_pairs={{0,2},{1,3},{2,0},{3,1},{4,6},{5,7},{6,4},{7,5},{8,10},{9,11},{10,... | collective-permute-start | bytes 1327112 | tf_op jit(solution)/shard_map/ppermute | solution.py:531
  259.8 25.7 %collective-permute-start.42 = (bf16[2,3,48,768]{3,2,1,0:T(8,128)(2,1)}, bf16[2,3,48,768]{3,2,1,0:T(8,128)(2,1)}, u32[]{:S(2)}, u32[]{:S(2)}) collective-permute-start(bf16[2,3,48,768]{3,2,1,0:T(8,128)(2,1)} %get-tuple-element.128), channel_id=1, source_target_pairs={{0,16},{16,0},{1,17},{17,1},{2,18},{18,2},{3,19},{19,3},{4,20},{20... | collective-permute-start | bytes 1327112 | tf_op jit(solution)/shard_map/ppermute | solution.py:527
  263.7 21.9 %collective-permute-start.43 = (bf16[6,48,768]{2,1,0:T(8,128)(2,1)}, bf16[6,48,768]{2,1,0:T(8,128)(2,1)S(1)}, u32[]{:S(2)}, u32[]{:S(2)}) collective-permute-start(bf16[6,48,768]{2,1,0:T(8,128)(2,1)} %last_sum.2.rest_0_), channel_id=1, source_target_pairs={{0,8},{1,9},{2,10},{3,11},{4,12},{5,13},{6,14},{7,15},{8,0},{9,1},... | collective-permute-start | bytes 1327112 | tf_op jit(solution)/shard_map/ppermute | solution.py:539
  269.3 24.6 %collective-permute-start.39 = (bf16[1,6,48,768]{3,2,1,0:T(8,128)(2,1)}, bf16[1,6,48,768]{3,2,1,0:T(8,128)(2,1)}, u32[]{:S(2)}, u32[]{:S(2)}) collective-permute-start(bf16[1,6,48,768]{3,2,1,0:T(8,128)(2,1)} %get-tuple-element.122.rest_1_), channel_id=1, source_target_pairs={{0,16},{16,0},{1,17},{17,1},{2,18},{18,2},{3,19},{19,3},{4,20},{20... | collective-permute-start | bytes 1327112 | tf_op jit(solution)/shard_map/ppermute | solution.py:527
  270.3 23.6 %collective-permute-start.40 = (bf16[1,6,48,768]{3,2,1,0:T(8,128)(2,1)}, bf16[1,6,48,768]{3,2,1,0:T(8,128)(2,1)}, u32[]{:S(2)}, u32[]{:S(2)}) collective-permute-start(bf16[1,6,48,768]{3,2,1,0:T(8,128)(2,1)} %get-tuple-element.125), channel_id=1, source_target_pairs={{0,2},{1,3},{2,0},{3,1},{4,6},{5,7},{6,4},{7,5},{8,10},{9,11},{10,... | collective-permute-start | bytes 1327112 | tf_op jit(solution)/shard_map/ppermute | solution.py:531
  288.8 29.1 %collective-permute-start.46 = (bf16[6,48,768]{2,1,0:T(8,128)(2,1)}, bf16[6,48,768]{2,1,0:T(8,128)(2,1)}, u32[]{:S(2)}, u32[]{:S(2)}) collective-permute-start(bf16[6,48,768]{2,1,0:T(8,128)(2,1)} %get-tuple-element.129.rest_0_), channel_id=1, source_target_pairs={{0,4},{1,5},{2,6},{3,7},{4,8},{5,9},{6,10},{7,11},{8,12},{9,13},{1... | collective-permute-start | bytes 1327112 | tf_op jit(solution)/shard_map/ppermute | solution.py:539
  290.2 27.7 %collective-permute-start.47 = (bf16[6,48,768]{2,1,0:T(8,128)(2,1)}, bf16[6,48,768]{2,1,0:T(8,128)(2,1)}, u32[]{:S(2)}, u32[]{:S(2)}) collective-permute-start(bf16[6,48,768]{2,1,0:T(8,128)(2,1)} %get-tuple-element.138), channel_id=1, source_target_pairs={{0,12},{1,13},{2,14},{3,15},{4,0},{5,1},{6,2},{7,3},{8,4},{9,5},{1... | collective-permute-start | bytes 1327112 | tf_op jit(solution)/shard_map/ppermute | solution.py:539
  296.3 21.6 %collective-permute-start.44 = (bf16[1,3,48,768]{3,2,1,0:T(8,128)(2,1)}, bf16[1,3,48,768]{3,2,1,0:T(8,128)(2,1)}, u32[]{:S(2)}, u32[]{:S(2)}) collective-permute-start(bf16[1,3,48,768]{3,2,1,0:T(8,128)(2,1)} %get-tuple-element.130.rest_1_), channel_id=1, source_target_pairs={{0,2},{1,3},{2,0},{3,1},{4,6},{5,7},{6,4},{7,5},{8,10},{9,11},{10,... | collective-permute-start | bytes 663560 | tf_op jit(solution)/shard_map/ppermute | solution.py:531
  348.9 42.3 %all-to-all-start.1 = ((bf16[16,48,768]{2,1,0:T(8,128)(2,1)}), bf16[16,48,768]{2,1,0:T(8,128)(2,1)S(1)}, u32[]{:S(2)}, u32[]{:S(2)}) async-start(bf16[16,48,768]{2,1,0:T(8,128)(2,1)} %pick_blocks.3.refs_1_), calls=%async_computation.1 | async-start | bytes 2359296 | tf_op jit(solution)/shard_map/all_to_all | solution.py:977
  352.7 42.6 %collective-permute-start.57 = (bf16[12,48,768]{2,1,0:T(8,128)(2,1)S(1)}, bf16[12,48,768]{2,1,0:T(8,128)(2,1)}, u32[]{:S(2)}, u32[]{:S(2)}) collective-permute-start(bf16[12,48,768]{2,1,0:T(8,128)(2,1)S(1)} %copy-done.3), channel_id=1, source_target_pairs={{0,16},{16,0},{1,17},{17,1},{2,18},{18,2},{3,19},{19,3},{4,20},{20... | collective-permute-start | bytes 2654216 | tf_op jit(solution)/shard_map/ppermute | solution.py:527
  353.8 41.5 %collective-permute-start.58 = (bf16[12,48,768]{2,1,0:T(8,128)(2,1)S(1)}, bf16[12,48,768]{2,1,0:T(8,128)(2,1)}, u32[]{:S(2)}, u32[]{:S(2)}) collective-permute-start(bf16[12,48,768]{2,1,0:T(8,128)(2,1)S(1)} %copy-done.3), channel_id=1, source_target_pairs={{0,2},{1,3},{2,0},{3,1},{4,6},{5,7},{6,4},{7,5},{8,10},{9,11},{10,... | collective-permute-start | bytes 2654216 | tf_op jit(solution)/shard_map/ppermute | solution.py:531
  355.6 30.7 %collective-permute-start.53 = (bf16[6,48,768]{2,1,0:T(8,128)(2,1)S(1)}, bf16[6,48,768]{2,1,0:T(8,128)(2,1)}, u32[]{:S(2)}, u32[]{:S(2)}) collective-permute-start(bf16[6,48,768]{2,1,0:T(8,128)(2,1)S(1)} %copy-done.22), channel_id=1, source_target_pairs={{0,4},{1,5},{2,6},{3,7},{4,8},{5,9},{6,10},{7,11},{8,12},{9,13},{1... | collective-permute-start | bytes 1327112 | tf_op jit(solution)/shard_map/ppermute | solution.py:539
  397.8 24.4 %collective-permute-start.61 = (bf16[6,48,768]{2,1,0:T(8,128)(2,1)}, bf16[6,48,768]{2,1,0:T(8,128)(2,1)S(1)}, u32[]{:S(2)}, u32[]{:S(2)}) collective-permute-start(bf16[6,48,768]{2,1,0:T(8,128)(2,1)} %get-tuple-element.146.refs_2_), channel_id=1, source_target_pairs={{0,2},{1,3},{2,0},{3,1},{4,6},{5,7},{6,4},{7,5},{8,10},{9,11},{10,... | collective-permute-start | bytes 1327112 | tf_op jit(solution)/shard_map/ppermute | solution.py:531
  399.3 22.8 %collective-permute-start.62 = (bf16[6,48,768]{2,1,0:T(8,128)(2,1)}, bf16[6,48,768]{2,1,0:T(8,128)(2,1)S(1)}, u32[]{:S(2)}, u32[]{:S(2)}) collective-permute-start(bf16[6,48,768]{2,1,0:T(8,128)(2,1)} %get-tuple-element.149), channel_id=1, source_target_pairs={{0,16},{16,0},{1,17},{17,1},{2,18},{18,2},{3,19},{19,3},{4,20},{20... | collective-permute-start | bytes 1327112 | tf_op jit(solution)/shard_map/ppermute | solution.py:527
  417.4 21.1 %collective-permute-start.64 = (bf16[12,48,768]{2,1,0:T(8,128)(2,1)S(1)}, bf16[12,48,768]{2,1,0:T(8,128)(2,1)S(1)}, u32[]{:S(2)}, u32[]{:S(2)}) collective-permute-start(bf16[12,48,768]{2,1,0:T(8,128)(2,1)S(1)} %copy-done.2), channel_id=1, source_target_pairs={{0,16},{16,0},{1,17},{17,1},{2,18},{18,2},{3,19},{19,3},{4,20},{20... | collective-permute-start | bytes 2654216 | tf_op jit(solution)/shard_map/ppermute | solution.py:527
  (86 other events, 888.1 us)
Sparse Core Ops, SparseCore 0:
  197.5 58.2 all-gather.3

commit v4 on v3

--- a/solution.py
+++ b/solution.py
@@ -16,7 +16,7 @@
 ROWS = 48
 STEP = 10
 NBLK = 192
-PAD = 128
+PAD = 112
 STACK = NBLK * ROWS
 UP_ROWS = FF // WIDTH
 
@@ -70,10 +70,9 @@
             low = high
 
 
-def wait_blocks(stage_ref, first, count, arrays, sem):
-    pltpu.make_async_copy(
-        stage_ref.at[pl.ds(first, count)], arrays[0].at[pl.ds(0, count)], sem
-    ).wait()
+def wait_blocks(stage_ref, first, count, sem):
+    blocks = stage_ref.at[pl.ds(first, count)]
+    pltpu.make_async_copy(blocks, blocks, sem).wait()
 
 
 def row_sum(x):
@@ -100,6 +99,15 @@
     lane = lax.broadcasted_iota(jnp.int32, (1, 2 * HD), 1)
     low = jnp.where(lane < HD, 1.0, 0.0)
     return (low.astype(BF), (1.0 - low).astype(BF)), lane < HD
+
+
+def both_heads(x, masks):
+    return jnp.concatenate([x * masks[0], x * masks[1]], axis=0)
+
+
+def own_lanes(x, low):
+    rows = x.shape[0] // 2
+    return jnp.where(low, x[:rows], x[rows:])
 
 
 def softmax(scores):
@@ -168,12 +176,8 @@
     masks, low = half_masks()
     for pair in range(HEADS // 2):
         cols = slice(pair * 2 * HD, (pair + 1) * 2 * HD)
-        kp, vp, qp = k[:, cols], v[:, cols], qm[:, cols]
-        parts = []
-        for mask in masks:
-            prob = softmax(mm_last(qp * mask, kp)).astype(BF)
-            parts.append(mm(prob, vp))
-        cm_ref[:, cols] = jnp.where(low, parts[0], parts[1]).astype(BF)
+        prob = softmax(mm_last(both_heads(qm[:, cols], masks), k[:, cols])).astype(BF)
+        cm_ref[:, cols] = own_lanes(mm(prob, v[:, cols]), low).astype(BF)
 
     if counts:
 
@@ -238,9 +242,8 @@
         load.start()
     per = WIDTH // ROWS
 
-    def send(part, value):
+    def keep(part, value):
         stage_ref[pl.ds(part * per, per)] = value.astype(BF).reshape(per, ROWS, WIDTH)
-        send_blocks(stage_ref, part * per, per, place_ref, 3 * per, dws, out_sem.at[part])
 
     gain_one, shift_one = vec_ref[8:9], vec_ref[9:10]
     gain_two = vec_ref[10:11]
@@ -255,8 +258,9 @@
         cols = slice(c * WIDTH, (c + 1) * WIDTH)
         loads[1 + c].wait()
         up = mm_last(hid, w_ref[1 + c]) + vec_ref[3 + c : 4 + c]
-        up_ref[:, cols] = up
-        act_ref[:, cols] = (up * gelu_cdf(up)).astype(BF)
+        cdf = gelu_cdf(up)
+        up_ref[:, cols] = cdf + up * jnp.exp(-0.5 * up * up) * INV_ROOT_TAU
+        act_ref[:, cols] = (up * cdf).astype(BF)
     resid_two = hidden_one + vec_ref[7:8]
     for c in range(UP_ROWS):
         cols = slice(c * WIDTH, (c + 1) * WIDTH)
@@ -273,23 +277,23 @@
     grad_hidden = grad_two
     for c in range(UP_ROWS):
         cols = slice(c * WIDTH, (c + 1) * WIDTH)
-        send(1 + UP_ROWS + c, mm_first(act_ref[:, cols], down))
-        up = up_ref[:, cols]
-        slope = gelu_cdf(up) + up * jnp.exp(-0.5 * up * up) * INV_ROOT_TAU
-        grad_up = (mm_last(down, w_ref[1 + UP_ROWS + c]) * slope).astype(BF)
+        keep(1 + UP_ROWS + c, mm_first(act_ref[:, cols], down))
+        grad_up = (mm_last(down, w_ref[1 + UP_ROWS + c]) * up_ref[:, cols]).astype(BF)
         gv_ref[3 + c : 4 + c] = row_sum(grad_up.astype(F32))
-        send(1 + c, mm_first(grad_up, hid))
+        keep(1 + c, mm_first(grad_up, hid))
         grad_hidden = grad_hidden + mm(grad_up, w_ref[1 + c])
+    send_blocks(stage_ref, per, 2 * UP_ROWS * per, place_ref, 3 * per, dws, out_sem.at[1])
     gv_ref[8:9] = row_sum(grad_hidden * unit_one)
     gv_ref[9:10] = row_sum(grad_hidden)
     grad_one = unit_back(grad_hidden, gain_one, unit_one, inv_one)
     gr_ref[...] = grad_one
     attn = grad_one.astype(BF)
     gv_ref[2:3] = row_sum(attn.astype(F32))
-    send(0, mm_first(cm, attn))
+    keep(0, mm_first(cm, attn))
+    send_blocks(stage_ref, 0, per, place_ref, 3 * per, dws, out_sem.at[0])
     gc_ref[...] = mm_last(attn, w_ref[0]).astype(BF)
-    for part in range(parts):
-        wait_blocks(stage_ref, part * per, per, dws, out_sem.at[part])
+    wait_blocks(stage_ref, 0, per, out_sem.at[0])
+    wait_blocks(stage_ref, per, 2 * UP_ROWS * per, out_sem.at[1])
 
 
 def masked_part(place, sizes, tm, cm, cot, vectors, stack):
@@ -310,7 +314,7 @@
                 pltpu.VMEM((rows, WIDTH), BF),
                 pltpu.VMEM((parts * WIDTH // ROWS, ROWS, WIDTH), BF),
                 pltpu.SemaphoreType.DMA((parts,)),
-                pltpu.SemaphoreType.DMA((parts,)),
+                pltpu.SemaphoreType.DMA((2,)),
             ],
         ),
         out_shape=[
@@ -348,22 +352,15 @@
 
     for pair in range(HEADS // 2):
         cols = slice(pair * 2 * HD, (pair + 1) * 2 * HD)
-        kp, vp, qp, gp = k_ref[:, cols], v_ref[:, cols], qm_ref[:, cols], gc_ref[:, cols]
-        grad_v, grad_k, grad_q = None, None, []
-        for mask in masks:
-            qh, gh = qp * mask, gp * mask
-            prob = softmax(mm_last(qh, kp))
-            grad_prob = mm_last(gh, vp)
-            spread = jnp.sum(prob * grad_prob, axis=1, keepdims=True)
-            grad_s = (prob * (grad_prob - spread)).astype(BF)
-            one_v = mm_first(prob.astype(BF), gh)
-            one_k = mm_first(grad_s, qh)
-            grad_v = one_v if grad_v is None else grad_v + one_v
-            grad_k = one_k if grad_k is None else grad_k + one_k
-            grad_q.append(mm(grad_s, kp))
-        dv_ref[:, cols] = grad_v.astype(BF)
-        dk_ref[:, cols] = grad_k.astype(BF)
-        dq_ref[:, cols] = jnp.where(low, grad_q[0], grad_q[1]).astype(BF) * QUERY_SCALE
+        kp, vp = k_ref[:, cols], v_ref[:, cols]
+        qh, gh = both_heads(qm_ref[:, cols], masks), both_heads(gc_ref[:, cols], masks)
+        prob = softmax(mm_last(qh, kp))
+        grad_prob = mm_last(gh, vp)
+        spread = jnp.sum(prob * grad_prob, axis=1, keepdims=True)
+        grad_s = (prob * (grad_prob - spread)).astype(BF)
+        dv_ref[:, cols] = mm_first(prob.astype(BF), gh).astype(BF)
+        dk_ref[:, cols] = mm_first(grad_s, qh).astype(BF)
+        dq_ref[:, cols] = own_lanes(mm(grad_s, kp), low).astype(BF) * QUERY_SCALE
     dq, dk, dv = dq_ref[...], dk_ref[...], dv_ref[...]
     gv_ref[0:1] += row_sum(dq.astype(F32))
     gv_ref[1:2] += row_sum(dv.astype(F32))
@@ -381,7 +378,7 @@
 
             send_blocks(stage_ref, i * per, per, place_ref, 0, dws, out_sem.at[i])
         for i in range(3):
-            wait_blocks(stage_ref, i * per, per, dws, out_sem.at[i])
+            wait_blocks(stage_ref, i * per, per, out_sem.at[i])
 
 
 def attention_back(place, tokens, k, v, tm, qm, gc, dws):
@@ -426,13 +423,8 @@
     masks, low = half_masks()
     for pair in range(HEADS // 2):
         cols = slice(pair * 2 * HD, (pair + 1) * 2 * HD)
-        kp, vp, qp = k_ref[:, cols], v_ref[:, cols], q_ref[:, cols]
-        halves = []
-        for mask in masks:
-            prob = softmax(mm_last(qp * mask, kp)).astype(BF)
-            halves.append(mm(prob, vp))
-        ctx_ref[:, cols] = jnp.where(low, halves[0], halves[1]).astype(BF)
-
+        prob = softmax(mm_last(both_heads(q_ref[:, cols], masks), k_ref[:, cols])).astype(BF)
+        ctx_ref[:, cols] = own_lanes(mm(prob, v_ref[:, cols]), low).astype(BF)
     load.wait()
     resid_one = tok_ref[...].astype(F32) + mm(ctx_ref[...], w_ref[0:WIDTH]) + vec_ref[2:3]
     unit_one, _ = unit_of(resid_one)
@@ -600,23 +592,26 @@
     )(a, b, to_a, to_b, *after)
 
 
-def last_sum_kernel(count, a_ref, b_ref, to_a_ref, to_b_ref, *rest):
+def last_sum_kernel(count, passing, a_ref, b_ref, to_a_ref, to_b_ref, *rest):
     for i, out in enumerate(rest[-count:]):
-        out[0:3] = a_ref[i] + to_a_ref[i]
-        out[3:6] = b_ref[i] + to_b_ref[i]
-
-
-def last_sum(a, b, to_a, to_b, *after):
+        for low, one, two in ((0, a_ref, to_a_ref), (3, b_ref, to_b_ref)):
+            total = one[i].astype(F32) + two[i].astype(F32)
+            if i == 0 and passing:
+                total = total + rest[0][low : low + 3].astype(F32)
+            out[low : low + 3] = total.astype(BF)
+
+
+def last_sum(a, b, to_a, to_b, passing, *after):
     count = a.shape[0]
     return pl.pallas_call(
-        functools.partial(last_sum_kernel, count),
-        in_specs=[VM] * 4 + [ANY] * len(after),
+        functools.partial(last_sum_kernel, count, len(passing)),
+        in_specs=[VM] * (4 + len(passing)) + [ANY] * len(after),
         out_specs=[VM] * count,
         out_shape=[jax.ShapeDtypeStruct((6, ROWS, WIDTH), BF)] * count,
         compiler_params=pltpu.CompilerParams(vmem_limit_bytes=VMEM_LIMIT),
         cost_estimate=cost(0.0, 0.001),
         name="last_sum",
-    )(a, b, to_a, to_b, *after)
+    )(a, b, to_a, to_b, *passing, *after)
 
 
 def reduce_blocks(dws, tasks):
@@ -631,17 +626,16 @@
     done = tasks[0](xs_near)
     a_near, b_near, ys_near, xs_near = first_sum(a_near, b_near, *to_near, done)
     to_near = swap_y(ys_near), swap_dp(xs_near)
-    (far,) = last_sum(a_far, b_far, *to_far, ys_near)
+    (far,) = last_sum(a_far, b_far, *to_far, (), ys_near)
     xs_own, ys_own, a_own, b_own = core_sum(keep, got[2], 3, far)
-    far = up_z(far, 2)
+    far = up_z(far, 1)
     to_own = swap_dp(xs_own), swap_y(ys_own)
-    done = tasks[1](xs_own)
-    up, down = last_sum(a_near, b_near, *to_near, done, far)
+    up, down = last_sum(a_near, b_near, *to_near, (far,), xs_own)
     near = up_z(up, 1), up_z(down, 3)
     a_own, b_own, ys_own, xs_own = first_sum(a_own, b_own, *to_own, up)
     to_own = swap_y(ys_own), swap_dp(xs_own)
-    done = tasks[2](ys_own)
-    return (a_own, to_own[0], b_own, to_own[1]), (far,) + near, done
+    done = tasks[1](ys_own)
+    return (a_own, to_own[0], b_own, to_own[1]), near, done
 
 
 def weight_step_kernel(halves, wholes, *refs):
@@ -682,36 +676,40 @@
     )(*halves, *wholes, states, *after)
 
 
-def moment_step_kernel(info_ref, a_ref, b_ref, first_ref, second_ref, *rest):
+def moment_step_kernel(info_ref, grad_ref, first_ref, second_ref, *rest):
     one_ref, two_ref = rest[-2:]
     count = first_ref.shape[0]
-    lead, live = info_ref[0] == 0, info_ref[1]
     for i in range(count):
-        one, two = a_ref[i // 2].astype(F32), b_ref[i // 2].astype(F32)
-        grad = jnp.where(lead if i % 2 == 0 else jnp.logical_not(lead), one, two)
-        grad = jnp.where(pl.program_id(0) * count + i < live, grad, 0.0)
-        one_ref[i] = FIRST_DECAY * first_ref[i] + (1.0 - FIRST_DECAY) * grad
-        two_ref[i] = SECOND_DECAY * second_ref[i] + (1.0 - SECOND_DECAY) * grad * grad
-
-
-def moment_step(info, a, b, first, second, *after):
-    each = 4 if first.shape[0] % 4 == 0 else 2
-    grads = pl.BlockSpec((each // 2, ROWS, WIDTH), lambda i, s: (i, 0, 0))
-    slots = pl.BlockSpec((each, ROWS, WIDTH), lambda i, s: (i, 0, 0))
-    shape = jax.ShapeDtypeStruct(first.shape, F32)
-    return pl.pallas_call(
-        moment_step_kernel,
-        grid_spec=pltpu.PrefetchScalarGridSpec(
-            num_scalar_prefetch=1,
-            grid=(first.shape[0] // each,),
-            in_specs=[grads, grads, slots, slots] + [ANY] * len(after),
-            out_specs=[slots, slots],
-        ),
-        out_shape=[shape, shape],
-        compiler_params=pltpu.CompilerParams(vmem_limit_bytes=VMEM_LIMIT),
-        cost_estimate=cost(0.0, 0.001),
-        name="moment_step",
-    )(info, a, b, first, second, *after)
+        slot = 2 * (pl.program_id(0) * count + i) + info_ref[0]
+        grad = jnp.where(slot < info_ref[1], grad_ref[i].astype(F32), 0.0)
+        one_ref[i, 0] = FIRST_DECAY * first_ref[i, 0] + (1.0 - FIRST_DECAY) * grad
+        two_ref[i, 0] = SECOND_DECAY * second_ref[i, 0] + (1.0 - SECOND_DECAY) * grad * grad
+
+
+def moment_step(info, grads, first, second, before, *after):
+    half = grads.shape[0]
+    each = 4 if half % 4 == 0 else 2
+    pairs = (half, 2, ROWS, WIDTH)
+    slots = pl.BlockSpec((each, 1, ROWS, WIDTH), lambda i, s: (i, s[0], 0, 0))
+    shape = jax.ShapeDtypeStruct(pairs, F32)
+    extra = before + after
+    return tuple(
+        pl.pallas_call(
+            moment_step_kernel,
+            grid_spec=pltpu.PrefetchScalarGridSpec(
+                num_scalar_prefetch=1,
+                grid=(half // each,),
+                in_specs=[pl.BlockSpec((each, ROWS, WIDTH), lambda i, s: (i, 0, 0)), slots, slots]
+                + [ANY] * len(extra),
+                out_specs=[slots, slots],
+            ),
+            out_shape=[shape, shape],
+            input_output_aliases={4: 0, 5: 1} if before else {},
+            compiler_params=pltpu.CompilerParams(vmem_limit_bytes=VMEM_LIMIT),
+            cost_estimate=cost(0.0, 0.001),
+            name="moment_step",
+        )(info, grads, first.reshape(pairs), second.reshape(pairs), *extra)
+    )
 
 
 def pick_kernel(sizes, arrays, from_ref, *refs):
@@ -799,11 +797,18 @@
     (near,) = move((((0, 0, 6), (1, 0, 6)),), [up, down], end_x)
     near_x, near_y = swap_dp(near), swap_y(near)
     done = tasks[1](near)
-    done = tasks[2](*done, far)
-    far_x, far_y = swap_dp(far), swap_y(far)
-    end_x, end_y = move(TWO_ENDS, [near_x, near_y], *done)
-    near = [near, near_x, near_y, swap_y(end_x), swap_dp(end_y)]
-    end_x, end_y = move(ENDS, [far_x, far_y], end_x)
+    if len(tasks) == 2:
+        far_x, far_y = swap_dp(far), swap_y(far)
+        end_x, end_y = move(TWO_ENDS, [near_x, near_y], *done, far)
+        near = [near, near_x, near_y, swap_y(end_x), swap_dp(end_y)]
+        end_x, end_y = move(ENDS, [far_x, far_y], end_x)
+    else:
+        (far,) = move((((0, 0, 6),),), [far], *done)
+        far_x, far_y = swap_dp(far), swap_y(far)
+        end_x, end_y = move(TWO_ENDS, [near_x, near_y], far, *own[3:])
+        near = [near, near_x, near_y, swap_y(end_x), swap_dp(end_y)]
+        done = tasks[2](end_x)
+        end_x, end_y = move(ENDS, [far_x, far_y], *done)
     far = [far, far_x, far_y, swap_y(end_x), swap_dp(end_y)]
     return own + far + near, end_x
 
@@ -829,7 +834,7 @@
 def gather_stack(weights, early):
     half = weights.shape[0] // 2
     mine = lax.dynamic_slice(weights, (lax.axis_index("dp") * half, 0), (half, WIDTH))
-    tasks = [lambda *after: early, lambda *after: after, lambda *after: after]
+    tasks = [lambda *after: early, lambda *after: after]
     arrays, _ = gather_blocks(mine.reshape(-1, ROWS, WIDTH), tasks)
     arrays += [swap_core(array) for array in arrays]
     return [array.reshape(-1, WIDTH) for array in arrays]
@@ -905,7 +910,7 @@
         which = slots + first
         return ((my_start + which) % ids // groups) * lanes + which // ids
 
-    info = jnp.stack([jnp.asarray(lead, jnp.int32), my_count])
+    info = [jnp.stack([jnp.asarray(side, jnp.int32), my_count]) for side in (lead, 1 - lead)]
 
     states = jnp.stack(
         [
@@ -938,21 +943,19 @@
     grad_vectors = jnp.concatenate([gv_attn[0:2], gv[2:12]], axis=0)
     dws, states = lax.optimization_barrier((dws, states))
     grad_vectors = jnp.sum(lax.all_gather(grad_vectors, ("dp", "fsdp")), axis=0)
-    outs = []
-
-    def page_task(*after):
-        outs[:] = [
-            forward_page(page_task.next, tokens, q, k, v, vectors, stack, tuple(outs), *after)
+    layer_out, token_grad = [], []
+
+    def page_task(page, *after):
+        layer_out[:] = [
+            forward_page(page, tokens, q, k, v, vectors, stack, tuple(layer_out), *after)
         ]
-        page_task.next += 1
-        return outs[0]
+        return layer_out[0]
 
     def grad_task(*after):
-        outs.append(input_grad(pos, dq, dk, dv, gr, stack, *after))
-        return outs[-1]
-
-    page_task.next = 0
-    tasks = [page_task] * pages + [grad_task]
+        token_grad.append(input_grad(pos, dq, dk, dv, gr, stack, *after))
+        return token_grad[0]
+
+    tasks = [functools.partial(page_task, page) for page in range(pages)] + [grad_task]
     states = jnp.take(states, state_at, axis=0, mode="clip")
     if direct:
         halves, wholes, done = reduce_blocks(dws, tasks)
@@ -965,7 +968,7 @@
         for task in tasks:
             done = task()
         halves, wholes = (), (mine,)
-    mine, new_mine = weight_step(halves, wholes, states, done, grad_vectors)
+    mine, new_mine = weight_step(halves, wholes, states, done)
 
     held_first = me_f * held
 
@@ -973,21 +976,22 @@
         return lax.dynamic_slice(table, (first,), (held,))
 
     def exchange(*after):
-        (send,) = pick_blocks(send_to, [mine], (spread * lanes,), *after)
+        (send,) = pick_blocks(send_to, [mine], (spread * lanes,), grad_vectors, *after)
         return send, lax.all_to_all(send, "fsdp", 0, 0, tiled=True)
 
     if direct:
-        kept = []
+        kept, moments = [], []
 
         def send_task(*after):
             send, owned = exchange(*after)
             kept.append(owned)
-            return (send,)
+            return (tasks[2](send),)
 
         def swap_task(*after):
             (even,) = pick_blocks(grad_at(lead), kept, (capacity // 2,), *after)
-            kept[:] = even, swap_dp(even)
-            return (even,)
+            kept[:] = [swap_dp(even)]
+            moments.append(moment_step(info[0], even, first_slots, second_slots, ()))
+            return even, moments[0][0]
 
         def last_task(*after):
             return (tasks[pages](*after),)
@@ -998,7 +1002,9 @@
         sibling = (me_f + 1 - 2 * (me_f % 2)) * held
         table = jnp.concatenate([held_table(at, held_first), held_table(at, sibling)])
         mine, handed = pick_blocks(table, arrays, (held, held))
-        new_first, new_second = moment_step(info, *kept, first_slots, second_slots, mine)
+        new_first, new_second = moment_step(
+            info[1], kept[0], first_slots, second_slots, moments[0], mine
+        )
         handed = swap_core(handed)
         ours = held_table(near, held_first)
         new_weights = jnp.where(ours[:, None, None], mine, handed).astype(F32)
@@ -1015,9 +1021,11 @@
             even, odd = pick_blocks(
                 jnp.concatenate([grad_at(0), grad_at(1)]), [owned], (capacity // 2, capacity // 2)
             )
-        new_first, new_second = moment_step(info, even, odd, first_slots, second_slots)
-    layer_out, token_grad = outs
+        moments = moment_step(info[0], even, first_slots, second_slots, ())
+        new_first, new_second = moment_step(info[1], odd, first_slots, second_slots, moments)
+    (layer_out,), (token_grad,) = layer_out, token_grad
     new_weights = new_weights.reshape(held * ROWS, WIDTH)
+    new_first, new_second = (x.reshape(first_slots.shape) for x in (new_first, new_second))
     new_vectors, new_vector_first, new_vector_second = adam_step(
         vectors, vector_first, vector_second, grad_vectors, VECTOR_RATE
     )

time: 466 us -> 437 us (0.938)
  waiting for transfers between devices: 119 us -> 99.1 us
  Pallas kernels: 206 us -> 193 us
    ppermute x9, waiting for transfers between devices: 29.4 us -> 15.7 us  [up_z(): lax.ppermute(x, 'fsdp', [(f, (f + 4 * steps) % 16) for f in range(16)])]
    ppermute x19, waiting for transfers between devices: 54.8 us -> 43 us  [swap_dp(): return lax.ppermute(x, 'dp', [(0, 1), (1, 0)])]
    pallas_call x1, Pallas kernels: 30.9 us -> 25 us  [attention_back(): pl.pallas_call(attention_back_kernel, grid_spec=pltpu.PrefetchScalarGridS...]
    pallas_call x1, Pallas kernels: 25.2 us -> 20.3 us  [project(): pl.pallas_call(functools.partial(project_kernel, counts), grid_spec=pltpu...]
    pallas_call x1, Pallas kernels: 30.4 us -> 25.6 us  [masked_part(): pl.pallas_call(masked_kernel, grid_spec=pltpu.PrefetchScalarGridSpec(num_...]
    pallas_call x1 -> x2, Pallas kernels: 8.98 us -> 11.6 us  [moment_step(): pl.pallas_call(moment_step_kernel, grid_spec=pltpu.PrefetchScalarGridSpec...]
    pallas_call x8 -> x9, Pallas kernels: 16.9 us -> 18.6 us  [move(): pl.pallas_call(functools.partial(move_kernel, plan), in_specs=[VM] * len(...]
    unnamed x100 -> x96, local copies, waits for them, and re-layouts: 10.3 us -> 10.2 us
  transfers between devices with their start and end apart: 68 -> 68, of which waited for: 19 -> 19; matrix products, arithmetic and copies ran while one was open for 7% -> 8% of each run, Pallas kernels for 42% -> 43%
where the time goes in v4:
time: 437 us; the launch traced here: 429 us
  Pallas kernels  193 us (44%)
  waiting for transfers between devices  99.1 us (23%)
  starting transfers between devices  73.3 us (17%)
  local copies, waits for them, and re-layouts  28.5 us (7%)
  other arithmetic  19.2 us (4%)
  between operations  15.5 us (4%)
    ppermute x19, waiting for transfers between devices, swap_dp(): return lax.ppermute(x, 'dp', [(0, 1), (1, 0)])  43 us
    pallas_call x3, Pallas kernels, forward_page(): pl.pallas_call(forward_kernel, grid=(1,), in_specs=[page, page, page, pag...  42.1 us
    ppermute x18, waiting for transfers between devices, swap_y(): return lax.ppermute(x, 'fsdp', [(f, f ^ 2) for f in range(16)])  31 us
    pallas_call x1, Pallas kernels, masked_part(): pl.pallas_call(masked_kernel, grid_spec=pltpu.PrefetchScalarGridSpec(num_...  25.6 us
    pallas_call x1, Pallas kernels, attention_back(): pl.pallas_call(attention_back_kernel, grid_spec=pltpu.PrefetchScalarGridS...  25 us
    ppermute x19, starting transfers between devices, swap_dp(): return lax.ppermute(x, 'dp', [(0, 1), (1, 0)])  22.2 us
    pallas_call x1, Pallas kernels, project(): pl.pallas_call(functools.partial(project_kernel, counts), grid_spec=pltpu...  20.3 us
    ppermute x18, starting transfers between devices, swap_y(): return lax.ppermute(x, 'fsdp', [(f, f ^ 2) for f in range(16)])  20 us
  transfers between devices with their start and end apart: 68, of which 19 were waited for; matrix products, arithmetic and copies ran while one was open for 8% of the time, Pallas kernels for 43%

profile of v4, /device:TPU:0, one launch (start us, length us, event | category | flops | bytes accessed | tf_op | source)
XLA Modules:
  0.0 428.6 jit_solution(6306622196831271311)
XLA Ops:
  19.4 3.7 gather_fusion.2
  23.1 3.7 gather_fusion.1
  30.6 3.2 pad_maximum_fusion.refs_2_
  43.5 22.3 %collective-permute-done.2 = bf16[3,48,768]{2,1,0:T(8,128)(2,1)S(1)} collective-permute-done((bf16[3,48,768]{2,1,0:T(8,128)(2,1)}, bf16[3,48,768]{2,1,0:T(8,128)(2,1)S(1)}, u32[]{:S(2)}, u32[]{:S(2)}) %collective-permute-start.2) | collective-permute-done | bytes 221216 | tf_op jit(solution)/shard_map/ppermute | solution.py:523
  71.9 7.4 %collective-permute-done.6.refs_0_ = bf16[6,48,768]{2,1,0:T(8,128)(2,1)S(1)} collective-permute-done((bf16[6,48,768]{2,1,0:T(8,128)(2,1)S(1)}, bf16[6,48,768]{2,1,0:T(8,128)(2,1)S(1)}, u32[]{:S(2)}, u32[]{:S(2)}) %collective-permute-start.6) | collective-permute-done | bytes 442400 | tf_op jit(solution)/shard_map/ppermute | solution.py:519
  83.9 4.1 collective-permute-done.14
  90.7 5.6 %collective-permute-done.12 = bf16[3,48,768]{2,1,0:T(8,128)(2,1)S(1)} collective-permute-done((bf16[3,48,768]{2,1,0:T(8,128)(2,1)}, bf16[3,48,768]{2,1,0:T(8,128)(2,1)S(1)}, u32[]{:S(2)}, u32[]{:S(2)}) %collective-permute-start.12) | collective-permute-done | bytes 221216 | tf_op jit(solution)/shard_map/ppermute | solution.py:519
  98.5 4.7 %all-to-all-start = ((bf16[16,3,48,768]{3,2,1,0:T(8,128)(2,1)}), bf16[16,3,48,768]{3,2,1,0:T(8,128)(2,1)S(1)}, u32[]{:S(2)}, u32[]{:S(2)}) async-start(bf16[16,3,48,768]{3,2,1,0:T(8,128)(2,1)} %pad_maximum_fusion.refs_2_), calls=%async_computation | async-start | bytes 7077888 | tf_op jit(solution)/shard_map/all_to_all | solution.py:938
  107.4 20.3 %project.1 = (bf16[1536,768]{1,0:T(8,128)(2,1)}, bf16[1536,768]{1,0:T(8,128)(2,1)}, bf16[1536,768]{1,0:T(8,128)(2,1)}, bf16[336,768]{1,0:T(8,128)(2,1)}, bf16[33...) custom-call(s32[40]{0:T(128)} %stack.181.rows_ref, s32[3,112,1]{2,1,0:T(8,128)} %copy.32.pos_ref, ...), custom_call_target="tpu_custom_call" | custom-call | flops 17999998976 | bytes 20000000 | tf_op jit(solution)/shard_map/project/pallas_call | solution.py:197
  127.7 25.6 %masked.1 = (f32[336,768]{1,0:T(8,128)}, bf16[336,768]{1,0:T(8,128)(2,1)}, f32[16,768]{1,0:T(8,128)}, bf16[96,48,768]{2,1,0:T(8,128)(2,1)}, bf16[24,48,768]{2,1,...) custom-call(s32[192]{0:T(256)} %fusion.5.place_ref, ...), custom_call_target="tpu_custom_call" | custom-call | flops 24000000000 | bytes 30000000 | tf_op jit(solution)/shard_map/masked/pallas_call | solution.py:303
  153.3 25.0 %attention_back.1 = (bf16[336,768]{1,0:T(8,128)(2,1)}, bf16[1536,768]{1,0:T(8,128)(2,1)}, bf16[1536,768]{1,0:T(8,128)(2,1)}, f32[8,768]{1,0:T(8,128)}, bf16[96,4...) custom-call(s32[192]{0:T(256)} %fusion.5.place_ref, ...), custom_call_target="tpu_custom_call", output_to_operand_aliasing={{4}: (7, {}), {5}: (8, {}), {6}: (9, {}), {7}: (10, {})} | custom-call | flops 24999999488 | bytes 30000000 | tf_op jit(solution)/shard_map/attention_back/pallas_call | solution.py:389
  179.1 8.4 %collective-permute-done.31 = bf16[24,48,768]{2,1,0:T(8,128)(2,1)} collective-permute-done((bf16[24,48,768]{2,1,0:T(8,128)(2,1)}, bf16[24,48,768]{2,1,0:T(8,128)(2,1)}, u32[]{:S(2)}, u32[]{:S(2)}) %collective-permute-start.31) | collective-permute-done | bytes 1769504 | tf_op jit(solution)/shard_map/ppermute | solution.py:527
  187.5 3.3 core_sum.3
  195.4 8.0 %collective-permute-done.32.to_a_ref = bf16[1,6,48,768]{3,2,1,0:T(8,128)(2,1)} collective-permute-done((bf16[1,6,48,768]{3,2,1,0:T(8,128)(2,1)}, bf16[1,6,48,768]{3,2,1,0:T(8,128)(2,1)}, u32[]{:S(2)}, u32[]{:S(2)}) %collective-permute-start.32) | collective-permute-done | bytes 442400 | tf_op jit(solution)/shard_map/ppermute | solution.py:519
  207.1 4.9 %core_sum.4 = (bf16[2,6,48,768]{3,2,1,0:T(8,128)(2,1)}, bf16[2,6,48,768]{3,2,1,0:T(8,128)(2,1)}, bf16[2,6,48,768]{3,2,1,0:T(8,128)(2,1)}, bf16[2,6,48,768]{3,2,1,0:T(8,128)(2,1)}) custom-call(bf16[4,4,6,48,768]{4,3,2,1,0:T(8,128)(2,1)} %bitcast.114, bf16[2,4,6,48,768]{4,3,2,1,0:T(8,128)(2,1)} %bitcast.78.from_ref, ...), custom_call_target="tpu_custom_call" | custom-call | bytes 1000 | tf_op jit(solution)/shard_map/core_sum/pallas_call | solution.py:563
  216.7 14.0 %forward_page.3.rest_0_ = bf16[1536,768]{1,0:T(8,128)(2,1)} custom-call(bf16[1536,768]{1,0:T(8,128)(2,1)} %tok_ref.9, bf16[1536,768]{1,0:T(8,128)(2,1)} %get-tuple-element.90.q_ref, bf16[1536,768]{1,0:T(8,128)(2,1)} %get-tuple-element.91.k_ref, bf16[1536,768]{1,0:T(8,128)(2,1)} %get-tuple-element.92.v_ref, f32[12,768]{1,0:T(8,128)} %vec_ref.9, ...), custom_call_target="tpu_custom_call" | custom-call | bytes 1000 | tf_op jit(solution)/shard_map/forward_page/pallas_call | solution.py:447
  230.8 5.7 %collective-permute-done.37.to_a_ref = bf16[2,6,48,768]{3,2,1,0:T(8,128)(2,1)} collective-permute-done((bf16[2,6,48,768]{3,2,1,0:T(8,128)(2,1)}, bf16[2,6,48,768]{3,2,1,0:T(8,128)(2,1)}, u32[]{:S(2)}, u32[]{:S(2)}) %collective-permute-start.37) | collective-permute-done | bytes 884768 | tf_op jit(solution)/shard_map/ppermute | solution.py:519
  244.6 5.4 %collective-permute-start.43 = (bf16[6,48,768]{2,1,0:T(8,128)(2,1)}, bf16[6,48,768]{2,1,0:T(8,128)(2,1)}, u32[]{:S(2)}, u32[]{:S(2)}) collective-permute-start(bf16[6,48,768]{2,1,0:T(8,128)(2,1)} %last_sum.2.rest_0_), channel_id=1, source_target_pairs={{0,4},{1,5},{2,6},{3,7},{4,8},{5,9},{6,10},{7,11},{8,12},{9,13},{1... | collective-permute-start | bytes 1327112 | tf_op jit(solution)/shard_map/ppermute | solution.py:531
  250.0 3.3 core_sum.5
  262.0 3.5 collective-permute-start.47
  273.5 14.0 %forward_page.4.refs_7_.rest_0_ = bf16[1536,768]{1,0:T(8,128)(2,1)} custom-call(bf16[1536,768]{1,0:T(8,128)(2,1)} %tok_ref.9, bf16[1536,768]{1,0:T(8,128)(2,1)} %get-tuple-element.90.q_ref, bf16[1536,768]{1,0:T(8,128)(2,1)} %get-tuple-element.91.k_ref, bf16[1536,768]{1,0:T(8,128)(2,1)} %get-tuple-element.92.v_ref, ...), custom_call_target="tpu_custom_call", output_to_operand_aliasing={{}: (6, {})} | custom-call | bytes 1000 | tf_op jit(solution)/shard_map/forward_page/pallas_call | solution.py:447
  287.6 3.9 weight_step.1
  293.5 3.8 collective-permute-start.49
  299.5 11.4 %input_grad.1.refs_2_ = f32[1536,768]{1,0:T(8,128)} custom-call(s32[3,112,1]{2,1,0:T(8,128)} %copy.32.pos_ref, bf16[336,768]{1,0:T(8,128)(2,1)} %get-tuple-element.142.dq_ref, bf16[1536,768]{1,0:T(8,128)(2,1)} %get-tuple-element.143.dk_ref, bf16[1536,768]{1,0:T(8,128)(2,1)} %get-tuple-element.144.dv_ref, f32[336,768]{1,0:T(8,128)} %get-tuple-element.145.gr_ref, ...), custom_call_target="tpu_custom_call" | custom-call | bytes 1000 | tf_op jit(solution)/shard_map/input_grad/pallas_call | solution.py:489
  317.4 3.3 pick_blocks.3.rest_1_
  320.8 3.7 all-to-all-start.1
  330.7 14.0 %forward_page.5.refs_1_ = bf16[1536,768]{1,0:T(8,128)(2,1)} custom-call(bf16[1536,768]{1,0:T(8,128)(2,1)} %tok_ref.9, bf16[1536,768]{1,0:T(8,128)(2,1)} %get-tuple-element.90.q_ref, bf16[1536,768]{1,0:T(8,128)(2,1)} %get-tuple-element.91.k_ref, bf16[1536,768]{1,0:T(8,128)(2,1)} %get-tuple-element.92.v_ref, ...), custom_call_target="tpu_custom_call", output_to_operand_aliasing={{}: (6, {})} | custom-call | bytes 1000 | tf_op jit(solution)/shard_map/forward_page/pallas_call | solution.py:447
  344.7 13.4 %collective-permute-done.54.refs_0_ = bf16[6,48,768]{2,1,0:T(8,128)(2,1)S(1)} collective-permute-done((bf16[6,48,768]{2,1,0:T(8,128)(2,1)}, bf16[6,48,768]{2,1,0:T(8,128)(2,1)S(1)}, u32[]{:S(2)}, u32[]{:S(2)}) %collective-permute-start.54) | collective-permute-done | bytes 442400 | tf_op jit(solution)/shard_map/ppermute | solution.py:531
  377.7 5.6 %moment_step.2 = (f32[12,2,48,768]{3,2,1,0:T(8,128)}, f32[12,2,48,768]{3,2,1,0:T(8,128)}) custom-call(s32[2]{0:T(128)} %pad_add_fusion.1.info_ref, bf16[12,48,768]{2,1,0:T(8,128)(2,1)} %pick_blocks.4.grad_ref.refs_2_, f32[12,2,48,768]{3,2,1,0:T(8,128)} %bitcast.118, f32[12,2,48,768]{3,2,1,0:T(8,128)} %bitcast.116), custom_call_target="tpu_custom_call" | custom-call | bytes 1000 | tf_op jit(solution)/shard_map/moment_step/pallas_call | solution.py:697
  395.8 4.0 pick_blocks.5
  401.9 9.7 %collective-permute-done.64.grad_ref = bf16[12,48,768]{2,1,0:T(8,128)(2,1)S(1)} collective-permute-done((bf16[12,48,768]{2,1,0:T(8,128)(2,1)S(1)}, bf16[12,48,768]{2,1,0:T(8,128)(2,1)S(1)}, u32[]{:S(2)}, u32[]{:S(2)}) %collective-permute-start.64) | collective-permute-done | bytes 884768 | tf_op jit(solution)/shard_map/ppermute | solution.py:519
  412.6 6.0 %moment_step.3 = (f32[12,2,48,768]{3,2,1,0:T(8,128)}, f32[12,2,48,768]{3,2,1,0:T(8,128)}) custom-call(s32[2]{0:T(128)} %pad_add_fusion.2.info_ref, bf16[12,48,768]{2,1,0:T(8,128)(2,1)} %copy-done.12, f32[12,2,48,768]{3,2,1,0:T(8,128)} %bitcast.119, f32[12,2,48,768]{3,2,1,0:T(8,128)} %bitcast.117, ...), custom_call_target="tpu_custom_call", output_to_operand_aliasing={{0}: (4, {}), {1}: (5, {})} | custom-call | bytes 1000 | tf_op jit(solution)/shard_map/moment_step/pallas_call | solution.py:697
  (273 shorter events, 138.0 us)
Async XLA Ops:
  9.1 24.6 %collective-permute-start = (bf16[6,48,768]{2,1,0:T(8,128)(2,1)}, bf16[6,48,768]{2,1,0:T(8,128)(2,1)}, u32[]{:S(2)}, u32[]{:S(2)}) collective-permute-start(bf16[6,48,768]{2,1,0:T(8,128)(2,1)} %bitcast.41), channel_id=1, source_target_pairs={{0,16},{16,0},{1,17},{17,1},{2,18},{18,2},{3,19},{19,3},{4,20},{20... | collective-permute-start | bytes 1327112 | tf_op jit(solution)/shard_map/ppermute | solution.py:519
  12.1 21.7 %collective-permute-start.1 = (bf16[6,48,768]{2,1,0:T(8,128)(2,1)}, bf16[6,48,768]{2,1,0:T(8,128)(2,1)}, u32[]{:S(2)}, u32[]{:S(2)}) collective-permute-start(bf16[6,48,768]{2,1,0:T(8,128)(2,1)} %bitcast.41), channel_id=1, source_target_pairs={{0,2},{1,3},{2,0},{3,1},{4,6},{5,7},{6,4},{7,5},{8,10},{9,11},{10,... | collective-permute-start | bytes 1327112 | tf_op jit(solution)/shard_map/ppermute | solution.py:523
  13.6 22.1 %collective-permute-start.4 = (bf16[6,48,768]{2,1,0:T(8,128)(2,1)}, bf16[6,48,768]{2,1,0:T(8,128)(2,1)}, u32[]{:S(2)}, u32[]{:S(2)}) collective-permute-start(bf16[6,48,768]{2,1,0:T(8,128)(2,1)} %bitcast.41), channel_id=1, source_target_pairs={{0,4},{1,5},{2,6},{3,7},{4,8},{5,9},{6,10},{7,11},{8,12},{9,13},{1... | collective-permute-start | bytes 1327112 | tf_op jit(solution)/shard_map/ppermute | solution.py:531
  15.2 20.9 %collective-permute-start.8 = (bf16[6,48,768]{2,1,0:T(8,128)(2,1)}, bf16[6,48,768]{2,1,0:T(8,128)(2,1)}, u32[]{:S(2)}, u32[]{:S(2)}) collective-permute-start(bf16[6,48,768]{2,1,0:T(8,128)(2,1)} %bitcast.41), channel_id=1, source_target_pairs={{0,12},{1,13},{2,14},{3,15},{4,0},{5,1},{6,2},{7,3},{8,4},{9,5},{1... | collective-permute-start | bytes 1327112 | tf_op jit(solution)/shard_map/ppermute | solution.py:531
  38.2 29.6 %collective-permute-start.9 = (bf16[12,48,768]{2,1,0:T(8,128)(2,1)}, bf16[12,48,768]{2,1,0:T(8,128)(2,1)S(1)}, u32[]{:S(2)}, u32[]{:S(2)}) collective-permute-start(bf16[12,48,768]{2,1,0:T(8,128)(2,1)} %move.10.refs_2_), channel_id=1, source_target_pairs={{0,16},{16,0},{1,17},{17,1},{2,18},{18,2},{3,19},{19,3},{4,20},{20... | collective-permute-start | bytes 2654216 | tf_op jit(solution)/shard_map/ppermute | solution.py:519
  38.7 29.1 %collective-permute-start.10 = (bf16[12,48,768]{2,1,0:T(8,128)(2,1)}, bf16[12,48,768]{2,1,0:T(8,128)(2,1)S(1)}, u32[]{:S(2)}, u32[]{:S(2)}) collective-permute-start(bf16[12,48,768]{2,1,0:T(8,128)(2,1)} %move.10.refs_2_), channel_id=1, source_target_pairs={{0,2},{1,3},{2,0},{3,1},{4,6},{5,7},{6,4},{7,5},{8,10},{9,11},{10,... | collective-permute-start | bytes 2654216 | tf_op jit(solution)/shard_map/ppermute | solution.py:523
  39.2 27.0 %collective-permute-start.5 = (bf16[6,48,768]{2,1,0:T(8,128)(2,1)}, bf16[6,48,768]{2,1,0:T(8,128)(2,1)S(1)}, u32[]{:S(2)}, u32[]{:S(2)}) collective-permute-start(bf16[6,48,768]{2,1,0:T(8,128)(2,1)} %collective-permute-done.4.refs_0_), channel_id=1, source_target_pairs={{0,4},{1,5},{2,6},{3,7},{4,8},{5,9},{6,10},{7,11},{8,12},{9,13},{1... | collective-permute-start | bytes 1327112 | tf_op jit(solution)/shard_map/ppermute | solution.py:531
  40.4 25.3 %collective-permute-start.2 = (bf16[3,48,768]{2,1,0:T(8,128)(2,1)}, bf16[3,48,768]{2,1,0:T(8,128)(2,1)S(1)}, u32[]{:S(2)}, u32[]{:S(2)}) collective-permute-start(bf16[3,48,768]{2,1,0:T(8,128)(2,1)} %get-tuple-element.83.refs_2_), channel_id=1, source_target_pairs={{0,2},{1,3},{2,0},{3,1},{4,6},{5,7},{6,4},{7,5},{8,10},{9,11},{10,... | collective-permute-start | bytes 663560 | tf_op jit(solution)/shard_map/ppermute | solution.py:523
  41.9 23.8 %collective-permute-start.3 = (bf16[3,48,768]{2,1,0:T(8,128)(2,1)}, bf16[3,48,768]{2,1,0:T(8,128)(2,1)S(1)}, u32[]{:S(2)}, u32[]{:S(2)}) collective-permute-start(bf16[3,48,768]{2,1,0:T(8,128)(2,1)} %get-tuple-element.84), channel_id=1, source_target_pairs={{0,16},{16,0},{1,17},{17,1},{2,18},{18,2},{3,19},{19,3},{4,20},{20... | collective-permute-start | bytes 663560 | tf_op jit(solution)/shard_map/ppermute | solution.py:519
  67.8 22.2 %collective-permute-start.25 = (bf16[12,48,768]{2,1,0:T(8,128)(2,1)}, bf16[12,48,768]{2,1,0:T(8,128)(2,1)}, u32[]{:S(2)}, u32[]{:S(2)}) collective-permute-start(bf16[12,48,768]{2,1,0:T(8,128)(2,1)} %move.10.refs_2_), channel_id=1, source_target_pairs={{0,1},{1,0},{2,3},{3,2},{4,5},{5,4},{6,7},{7,6},{8,9},{9,8},{10,11... | collective-permute-start | bytes 2654216 | tf_op jit(solution)/shard_map/ppermute | solution.py:527
  98.5 79.8 %all-to-all-start = ((bf16[16,3,48,768]{3,2,1,0:T(8,128)(2,1)}), bf16[16,3,48,768]{3,2,1,0:T(8,128)(2,1)S(1)}, u32[]{:S(2)}, u32[]{:S(2)}) async-start(bf16[16,3,48,768]{3,2,1,0:T(8,128)(2,1)} %pad_maximum_fusion.refs_2_), calls=%async_computation | async-start | bytes 7077888 | tf_op jit(solution)/shard_map/all_to_all | solution.py:938
  103.2 194.1 %all-gather.4.cloned.1.call-start = ((), (), s32[]{:S(2)}) async-start(), calls=%async_computation.2 | async-start | bytes 1622016 | tf_op jit(solution)/shard_map/all_gather | solution.py:945
  178.4 28.7 %collective-permute-start.30 = (bf16[48,48,768]{2,1,0:T(8,128)(2,1)}, bf16[48,48,768]{2,1,0:T(8,128)(2,1)}, u32[]{:S(2)}, u32[]{:S(2)}) collective-permute-start(bf16[48,48,768]{2,1,0:T(8,128)(2,1)} %get-tuple-element.108), channel_id=1, source_target_pairs={{0,1},{1,0},{2,3},{3,2},{4,5},{5,4},{6,7},{7,6},{8,9},{9,8},{10,11... | collective-permute-start | bytes 10616840 | tf_op jit(solution)/shard_map/ppermute | solution.py:527
  179.0 71.0 %collective-permute-start.34 = (bf16[24,48,768]{2,1,0:T(8,128)(2,1)}, bf16[24,48,768]{2,1,0:T(8,128)(2,1)}, u32[]{:S(2)}, u32[]{:S(2)}) collective-permute-start(bf16[24,48,768]{2,1,0:T(8,128)(2,1)} %get-tuple-element.116), channel_id=1, source_target_pairs={{0,1},{1,0},{2,3},{3,2},{4,5},{5,4},{6,7},{7,6},{8,9},{9,8},{10,11... | collective-permute-start | bytes 5308424 | tf_op jit(solution)/shard_map/ppermute | solution.py:527
  212.1 24.4 %collective-permute-start.37 = (bf16[2,6,48,768]{3,2,1,0:T(8,128)(2,1)}, bf16[2,6,48,768]{3,2,1,0:T(8,128)(2,1)}, u32[]{:S(2)}, u32[]{:S(2)}) collective-permute-start(bf16[2,6,48,768]{3,2,1,0:T(8,128)(2,1)} %get-tuple-element.115.rest_0_), channel_id=1, source_target_pairs={{0,16},{16,0},{1,17},{17,1},{2,18},{18,2},{3,19},{19,3},{4,20},{20... | collective-permute-start | bytes 2654216 | tf_op jit(solution)/shard_map/ppermute | solution.py:519
  212.7 23.8 %collective-permute-start.38 = (bf16[2,6,48,768]{3,2,1,0:T(8,128)(2,1)}, bf16[2,6,48,768]{3,2,1,0:T(8,128)(2,1)}, u32[]{:S(2)}, u32[]{:S(2)}) collective-permute-start(bf16[2,6,48,768]{3,2,1,0:T(8,128)(2,1)} %get-tuple-element.122), channel_id=1, source_target_pairs={{0,2},{1,3},{2,0},{3,1},{4,6},{5,7},{6,4},{7,5},{8,10},{9,11},{10,... | collective-permute-start | bytes 2654216 | tf_op jit(solution)/shard_map/ppermute | solution.py:523
  214.4 28.1 %collective-permute-start.35 = (bf16[1,3,48,768]{3,2,1,0:T(8,128)(2,1)}, bf16[1,3,48,768]{3,2,1,0:T(8,128)(2,1)}, u32[]{:S(2)}, u32[]{:S(2)}) collective-permute-start(bf16[1,3,48,768]{3,2,1,0:T(8,128)(2,1)} %get-tuple-element.114.rest_0_), channel_id=1, source_target_pairs={{0,2},{1,3},{2,0},{3,1},{4,6},{5,7},{6,4},{7,5},{8,10},{9,11},{10,... | collective-permute-start | bytes 663560 | tf_op jit(solution)/shard_map/ppermute | solution.py:523
  214.7 27.8 %collective-permute-start.36 = (bf16[1,3,48,768]{3,2,1,0:T(8,128)(2,1)}, bf16[1,3,48,768]{3,2,1,0:T(8,128)(2,1)}, u32[]{:S(2)}, u32[]{:S(2)}) collective-permute-start(bf16[1,3,48,768]{3,2,1,0:T(8,128)(2,1)} %get-tuple-element.119), channel_id=1, source_target_pairs={{0,16},{16,0},{1,17},{17,1},{2,18},{18,2},{3,19},{19,3},{4,20},{20... | collective-permute-start | bytes 663560 | tf_op jit(solution)/shard_map/ppermute | solution.py:519
  261.5 26.0 %collective-permute-start.46 = (bf16[6,48,768]{2,1,0:T(8,128)(2,1)}, bf16[6,48,768]{2,1,0:T(8,128)(2,1)}, u32[]{:S(2)}, u32[]{:S(2)}) collective-permute-start(bf16[6,48,768]{2,1,0:T(8,128)(2,1)} %get-tuple-element.131.rest_0_), channel_id=1, source_target_pairs={{0,4},{1,5},{2,6},{3,7},{4,8},{5,9},{6,10},{7,11},{8,12},{9,13},{1... | collective-permute-start | bytes 1327112 | tf_op jit(solution)/shard_map/ppermute | solution.py:531
  262.0 25.6 %collective-permute-start.47 = (bf16[6,48,768]{2,1,0:T(8,128)(2,1)}, bf16[6,48,768]{2,1,0:T(8,128)(2,1)}, u32[]{:S(2)}, u32[]{:S(2)}) collective-permute-start(bf16[6,48,768]{2,1,0:T(8,128)(2,1)} %get-tuple-element.136), channel_id=1, source_target_pairs={{0,12},{1,13},{2,14},{3,15},{4,0},{5,1},{6,2},{7,3},{8,4},{9,5},{1... | collective-permute-start | bytes 1327112 | tf_op jit(solution)/shard_map/ppermute | solution.py:531
  291.5 19.4 %collective-permute-start.50 = (bf16[6,48,768]{2,1,0:T(8,128)(2,1)}, bf16[6,48,768]{2,1,0:T(8,128)(2,1)S(1)}, u32[]{:S(2)}, u32[]{:S(2)}) collective-permute-start(bf16[6,48,768]{2,1,0:T(8,128)(2,1)} %get-tuple-element.141.rest_0_.refs_0_), channel_id=1, source_target_pairs={{0,16},{16,0},{1,17},{17,1},{2,18},{18,2},{3,19},{19,3},{4,20},{20... | collective-permute-start | bytes 1327112 | tf_op jit(solution)/shard_map/ppermute | solution.py:519
  293.5 20.9 %collective-permute-start.48 = (bf16[6,48,768]{2,1,0:T(8,128)(2,1)}, bf16[6,48,768]{2,1,0:T(8,128)(2,1)S(1)}, u32[]{:S(2)}, u32[]{:S(2)}) collective-permute-start(bf16[6,48,768]{2,1,0:T(8,128)(2,1)} %get-tuple-element.141.rest_0_.refs_0_), channel_id=1, source_target_pairs={{0,4},{1,5},{2,6},{3,7},{4,8},{5,9},{6,10},{7,11},{8,12},{9,13},{1... | collective-permute-start | bytes 1327112 | tf_op jit(solution)/shard_map/ppermute | solution.py:531
  293.5 20.9 %collective-permute-start.49 = (bf16[6,48,768]{2,1,0:T(8,128)(2,1)}, bf16[6,48,768]{2,1,0:T(8,128)(2,1)S(1)}, u32[]{:S(2)}, u32[]{:S(2)}) collective-permute-start(bf16[6,48,768]{2,1,0:T(8,128)(2,1)} %get-tuple-element.141.rest_0_.refs_0_), channel_id=1, source_target_pairs={{0,12},{1,13},{2,14},{3,15},{4,0},{5,1},{6,2},{7,3},{8,4},{9,5},{1... | collective-permute-start | bytes 1327112 | tf_op jit(solution)/shard_map/ppermute | solution.py:531
  320.8 52.9 %all-to-all-start.1 = ((bf16[16,48,768]{2,1,0:T(8,128)(2,1)}), bf16[16,48,768]{2,1,0:T(8,128)(2,1)S(1)}, u32[]{:S(2)}, u32[]{:S(2)}) async-start(bf16[16,48,768]{2,1,0:T(8,128)(2,1)} %pick_blocks.3.rest_1_), calls=%async_computation.1 | async-start | bytes 2359296 | tf_op jit(solution)/shard_map/all_to_all | solution.py:980
  324.5 41.0 %collective-permute-start.57 = (bf16[12,48,768]{2,1,0:T(8,128)(2,1)S(1)}, bf16[12,48,768]{2,1,0:T(8,128)(2,1)S(1)}, u32[]{:S(2)}, u32[]{:S(2)}) collective-permute-start(bf16[12,48,768]{2,1,0:T(8,128)(2,1)S(1)} %copy-done.2), channel_id=1, source_target_pairs={{0,16},{16,0},{1,17},{17,1},{2,18},{18,2},{3,19},{19,3},{4,20},{20... | collective-permute-start | bytes 2654216 | tf_op jit(solution)/shard_map/ppermute | solution.py:519
  325.4 40.1 %collective-permute-start.58 = (bf16[12,48,768]{2,1,0:T(8,128)(2,1)S(1)}, bf16[12,48,768]{2,1,0:T(8,128)(2,1)}, u32[]{:S(2)}, u32[]{:S(2)}) collective-permute-start(bf16[12,48,768]{2,1,0:T(8,128)(2,1)S(1)} %copy-done.2), channel_id=1, source_target_pairs={{0,2},{1,3},{2,0},{3,1},{4,6},{5,7},{6,4},{7,5},{8,10},{9,11},{10,... | collective-permute-start | bytes 2654216 | tf_op jit(solution)/shard_map/ppermute | solution.py:523
  327.2 30.9 %collective-permute-start.54 = (bf16[6,48,768]{2,1,0:T(8,128)(2,1)}, bf16[6,48,768]{2,1,0:T(8,128)(2,1)S(1)}, u32[]{:S(2)}, u32[]{:S(2)}) collective-permute-start(bf16[6,48,768]{2,1,0:T(8,128)(2,1)} %copy-done.21), channel_id=1, source_target_pairs={{0,4},{1,5},{2,6},{3,7},{4,8},{5,9},{6,10},{7,11},{8,12},{9,13},{1... | collective-permute-start | bytes 1327112 | tf_op jit(solution)/shard_map/ppermute | solution.py:531
  328.9 35.1 %collective-permute-start.52 = (bf16[3,48,768]{2,1,0:T(8,128)(2,1)}, bf16[3,48,768]{2,1,0:T(8,128)(2,1)}, u32[]{:S(2)}, u32[]{:S(2)}) collective-permute-start(bf16[3,48,768]{2,1,0:T(8,128)(2,1)} %get-tuple-element.146.refs_2_), channel_id=1, source_target_pairs={{0,2},{1,3},{2,0},{3,1},{4,6},{5,7},{6,4},{7,5},{8,10},{9,11},{10,... | collective-permute-start | bytes 663560 | tf_op jit(solution)/shard_map/ppermute | solution.py:523
  329.5 36.1 %collective-permute-start.53 = (bf16[3,48,768]{2,1,0:T(8,128)(2,1)}, bf16[3,48,768]{2,1,0:T(8,128)(2,1)}, u32[]{:S(2)}, u32[]{:S(2)}) collective-permute-start(bf16[3,48,768]{2,1,0:T(8,128)(2,1)} %get-tuple-element.147), channel_id=1, source_target_pairs={{0,16},{16,0},{1,17},{17,1},{2,18},{18,2},{3,19},{19,3},{4,20},{20... | collective-permute-start | bytes 663560 | tf_op jit(solution)/shard_map/ppermute | solution.py:519
  360.6 22.7 %collective-permute-start.55 = (bf16[6,48,768]{2,1,0:T(8,128)(2,1)}, bf16[6,48,768]{2,1,0:T(8,128)(2,1)S(1)}, u32[]{:S(2)}, u32[]{:S(2)}) collective-permute-start(bf16[6,48,768]{2,1,0:T(8,128)(2,1)} %move.15.refs_2_.refs_5_), channel_id=1, source_target_pairs={{0,16},{16,0},{1,17},{17,1},{2,18},{18,2},{3,19},{19,3},{4,20},{20... | collective-permute-start | bytes 1327112 | tf_op jit(solution)/shard_map/ppermute | solution.py:519
  368.9 20.4 %collective-permute-start.61 = (bf16[6,48,768]{2,1,0:T(8,128)(2,1)}, bf16[6,48,768]{2,1,0:T(8,128)(2,1)S(1)}, u32[]{:S(2)}, u32[]{:S(2)}) collective-permute-start(bf16[6,48,768]{2,1,0:T(8,128)(2,1)} %get-tuple-element.148.refs_1_), channel_id=1, source_target_pairs={{0,2},{1,3},{2,0},{3,1},{4,6},{5,7},{6,4},{7,5},{8,10},{9,11},{10,... | collective-permute-start | bytes 1327112 | tf_op jit(solution)/shard_map/ppermute | solution.py:523
  388.4 23.2 %collective-permute-start.64 = (bf16[12,48,768]{2,1,0:T(8,128)(2,1)S(1)}, bf16[12,48,768]{2,1,0:T(8,128)(2,1)S(1)}, u32[]{:S(2)}, u32[]{:S(2)}) collective-permute-start(bf16[12,48,768]{2,1,0:T(8,128)(2,1)S(1)} %copy-done.3), channel_id=1, source_target_pairs={{0,16},{16,0},{1,17},{17,1},{2,18},{18,2},{3,19},{19,3},{4,20},{20... | collective-permute-start | bytes 2654216 | tf_op jit(solution)/shard_map/ppermute | solution.py:519
  (84 other events, 779.2 us)
Sparse Core Ops, SparseCore 0:
  195.6 59.9 all-gather.3

commit v5 on v4

--- a/solution.py
+++ b/solution.py
@@ -174,9 +174,17 @@
     qm = mm(pick, q).astype(BF)
     qm_ref[...] = qm
     masks, low = half_masks()
-    for pair in range(HEADS // 2):
-        cols = slice(pair * 2 * HD, (pair + 1) * 2 * HD)
-        prob = softmax(mm_last(both_heads(qm[:, cols], masks), k[:, cols])).astype(BF)
+    pairs = [slice(pair * 2 * HD, (pair + 1) * 2 * HD) for pair in range(HEADS // 2)]
+
+    def scores_of(cols):
+        return mm_last(both_heads(qm[:, cols], masks), k[:, cols])
+
+    ahead = scores_of(pairs[0])
+    for i, cols in enumerate(pairs):
+        scores = ahead
+        if i + 1 < len(pairs):
+            ahead = scores_of(pairs[i + 1])
+        prob = softmax(scores).astype(BF)
         cm_ref[:, cols] = own_lanes(mm(prob, v[:, cols]), low).astype(BF)
 
     if counts:
@@ -350,17 +358,26 @@
         sum_ref[...] = jnp.zeros_like(sum_ref)
         gv_ref[...] = jnp.zeros_like(gv_ref)
 
-    for pair in range(HEADS // 2):
-        cols = slice(pair * 2 * HD, (pair + 1) * 2 * HD)
-        kp, vp = k_ref[:, cols], v_ref[:, cols]
+    pairs = [slice(pair * 2 * HD, (pair + 1) * 2 * HD) for pair in range(HEADS // 2)]
+
+    def begin(cols):
         qh, gh = both_heads(qm_ref[:, cols], masks), both_heads(gc_ref[:, cols], masks)
-        prob = softmax(mm_last(qh, kp))
-        grad_prob = mm_last(gh, vp)
-        spread = jnp.sum(prob * grad_prob, axis=1, keepdims=True)
+        return qh, gh, mm_last(k_ref[:, cols], qh), mm_last(v_ref[:, cols], gh)
+
+    ahead = begin(pairs[0])
+    for i, cols in enumerate(pairs):
+        qh, gh, scores, grad_prob = ahead
+        if i + 1 < len(pairs):
+            ahead = begin(pairs[i + 1])
+        top = jnp.max(scores, axis=0, keepdims=True)
+        exponent = jnp.exp(scores - top)
+        prob = exponent * (1.0 / jnp.sum(exponent, axis=0, keepdims=True))
+        spread = jnp.sum(prob * grad_prob, axis=0, keepdims=True)
         grad_s = (prob * (grad_prob - spread)).astype(BF)
-        dv_ref[:, cols] = mm_first(prob.astype(BF), gh).astype(BF)
-        dk_ref[:, cols] = mm_first(grad_s, qh).astype(BF)
-        dq_ref[:, cols] = own_lanes(mm(grad_s, kp), low).astype(BF) * QUERY_SCALE
+        dv_ref[:, cols] = mm(prob.astype(BF), gh).astype(BF)
+        dk_ref[:, cols] = mm(grad_s, qh).astype(BF)
+        dq = own_lanes(mm_first(grad_s, k_ref[:, cols]), low)
+        dq_ref[:, cols] = dq.astype(BF) * QUERY_SCALE
     dq, dk, dv = dq_ref[...], dk_ref[...], dv_ref[...]
     gv_ref[0:1] += row_sum(dq.astype(F32))
     gv_ref[1:2] += row_sum(dv.astype(F32))
@@ -614,14 +631,14 @@
     )(a, b, to_a, to_b, *passing, *after)
 
 
-def reduce_blocks(dws, tasks):
+def reduce_blocks(dws, tasks, early):
     keep = dws[0]
     got = [swap_core(send) for send in dws[1:]]
     xs_far, ys_far, a_far, b_far = core_sum(keep, got[0], 0)
     to_far = swap_dp(xs_far), swap_y(ys_far)
     a_far, b_far, ys_far, xs_far = first_sum(a_far, b_far, *to_far)
     to_far = swap_y(ys_far), swap_dp(xs_far)
-    xs_near, ys_near, a_near, b_near = core_sum(keep, got[1], 1, ys_far)
+    xs_near, ys_near, a_near, b_near = core_sum(keep, got[1], 1, ys_far, early)
     to_near = swap_dp(xs_near), swap_y(ys_near)
     done = tasks[0](xs_near)
     a_near, b_near, ys_near, xs_near = first_sum(a_near, b_near, *to_near, done)
@@ -835,9 +852,9 @@
     half = weights.shape[0] // 2
     mine = lax.dynamic_slice(weights, (lax.axis_index("dp") * half, 0), (half, WIDTH))
     tasks = [lambda *after: early, lambda *after: after]
-    arrays, _ = gather_blocks(mine.reshape(-1, ROWS, WIDTH), tasks)
+    arrays, done = gather_blocks(mine.reshape(-1, ROWS, WIDTH), tasks)
     arrays += [swap_core(array) for array in arrays]
-    return [array.reshape(-1, WIDTH) for array in arrays]
+    return [array.reshape(-1, WIDTH) for array in arrays], done
 
 
 def gathered_place(group, spot, turn):
@@ -930,9 +947,9 @@
     ).reshape(pages * PAD, WIDTH)
 
     if direct:
-        pieces, rows, counts = gather_stack(weights, (states, cot)), piece_rows(), PIECES
-        last, states = lax.optimization_barrier((pieces[-1], states))
-        pieces = pieces[:-1] + [last]
+        pieces, done = gather_stack(weights, (states, cot))
+        rows, counts = piece_rows(), PIECES
+        done, states = lax.optimization_barrier((done, states))
     else:
         pieces, rows, counts = [lax.all_gather(weights, "fsdp", axis=0, tiled=True)], jnp.zeros((1,), jnp.int32), ()
     states = lax.all_to_all(states, "fsdp", 0, 0, tiled=True)
@@ -941,8 +958,6 @@
     gr, gc, gv, *dws = masked_part(put, sizes, tm, cm, cot, vectors, stack)
     dq, dk, dv, gv_attn, *dws = attention_back(put, tokens, k, v, tm, qm, gc, dws)
     grad_vectors = jnp.concatenate([gv_attn[0:2], gv[2:12]], axis=0)
-    dws, states = lax.optimization_barrier((dws, states))
-    grad_vectors = jnp.sum(lax.all_gather(grad_vectors, ("dp", "fsdp")), axis=0)
     layer_out, token_grad = [], []
 
     def page_task(page, *after):
@@ -956,9 +971,10 @@
         return token_grad[0]
 
     tasks = [functools.partial(page_task, page) for page in range(pages)] + [grad_task]
+    arrived = states
     states = jnp.take(states, state_at, axis=0, mode="clip")
     if direct:
-        halves, wholes, done = reduce_blocks(dws, tasks)
+        halves, wholes, done = reduce_blocks(dws, tasks, arrived)
     else:
         if groups > 1:
             mine = lax.psum_scatter(dws[0], ("dp", "fsdp"), scatter_dimension=0, tiled=True)
@@ -969,6 +985,8 @@
             done = task()
         halves, wholes = (), (mine,)
     mine, new_mine = weight_step(halves, wholes, states, done)
+    mine, grad_vectors = lax.optimization_barrier((mine, grad_vectors))
+    grad_vectors = jnp.sum(lax.all_gather(grad_vectors, ("dp", "fsdp")), axis=0)
 
     held_first = me_f * held
 
@@ -976,11 +994,11 @@
         return lax.dynamic_slice(table, (first,), (held,))
 
     def exchange(*after):
-        (send,) = pick_blocks(send_to, [mine], (spread * lanes,), grad_vectors, *after)
+        (send,) = pick_blocks(send_to, [mine], (spread * lanes,), *after)
         return send, lax.all_to_all(send, "fsdp", 0, 0, tiled=True)
 
     if direct:
-        kept, moments = [], []
+        kept = []
 
         def send_task(*after):
             send, owned = exchange(*after)
@@ -989,21 +1007,21 @@
 
         def swap_task(*after):
             (even,) = pick_blocks(grad_at(lead), kept, (capacity // 2,), *after)
-            kept[:] = [swap_dp(even)]
-            moments.append(moment_step(info[0], even, first_slots, second_slots, ()))
-            return even, moments[0][0]
+            kept[:] = even, swap_dp(even)
+            return (even,)
 
         def last_task(*after):
             return (tasks[pages](*after),)
 
-        arrays, _ = gather_blocks(new_mine, (last_task, send_task, swap_task))
+        arrays, done = gather_blocks(new_mine, (last_task, send_task, swap_task))
         at, near = gathered_place(group, spot, turn)
         at = jnp.where(near, at, 0)
         sibling = (me_f + 1 - 2 * (me_f % 2)) * held
         table = jnp.concatenate([held_table(at, held_first), held_table(at, sibling)])
-        mine, handed = pick_blocks(table, arrays, (held, held))
+        moments = moment_step(info[0], kept[0], first_slots, second_slots, (), done)
+        mine, handed = pick_blocks(table, arrays, (held, held), moments[0])
         new_first, new_second = moment_step(
-            info[1], kept[0], first_slots, second_slots, moments[0], mine
+            info[1], kept[1], first_slots, second_slots, moments, mine
         )
         handed = swap_core(handed)
         ours = held_table(near, held_first)

time: 437 us -> 426 us (0.975)
  Pallas kernels: 193 us -> 186 us
  starting transfers between devices: 73.3 us -> 66.7 us
  local copies, waits for them, and re-layouts: 28.5 us -> 34 us
    ppermute x18, waiting for transfers between devices: 31 us -> 21.7 us  [swap_y(): return lax.ppermute(x, 'fsdp', [(f, f ^ 2) for f in range(16)])]
    ppermute x9, waiting for transfers between devices: 15.7 us -> 23.3 us  [up_z(): lax.ppermute(x, 'fsdp', [(f, (f + 4 * steps) % 16) for f in range(16)])]
    pallas_call x1, Pallas kernels: 25 us -> 19.9 us  [attention_back(): pl.pallas_call(attention_back_kernel, grid_spec=pltpu.PrefetchScalarGridS...]
    ppermute x9, starting transfers between devices: 19.8 us -> 15 us  [up_z(): lax.ppermute(x, 'fsdp', [(f, (f + 4 * steps) % 16) for f in range(16)])]
    unnamed x96 -> x104, local copies, waits for them, and re-layouts: 10.2 us -> 14 us
  transfers between devices with their start and end apart: 68 -> 68, of which waited for: 19 -> 18; matrix products, arithmetic and copies ran while one was open for 8% -> 8% of each run, Pallas kernels for 43% -> 42%
where the time goes in v5:
time: 426 us; the launch traced here: 417 us
  Pallas kernels  186 us (44%)
  waiting for transfers between devices  97.6 us (23%)
  starting transfers between devices  66.7 us (16%)
  local copies, waits for them, and re-layouts  34 us (8%)
  other arithmetic  17.9 us (4%)
  between operations  15.5 us (4%)
    ppermute x19, waiting for transfers between devices, swap_dp(): return lax.ppermute(x, 'dp', [(0, 1), (1, 0)])  42.8 us
    pallas_call x3, Pallas kernels, forward_page(): pl.pallas_call(forward_kernel, grid=(1,), in_specs=[page, page, page, pag...  42.1 us
    pallas_call x1, Pallas kernels, masked_part(): pl.pallas_call(masked_kernel, grid_spec=pltpu.PrefetchScalarGridSpec(num_...  25.6 us
    ppermute x9, waiting for transfers between devices, up_z(): lax.ppermute(x, 'fsdp', [(f, (f + 4 * steps) % 16) for f in range(16)])  23.3 us
    ppermute x19, starting transfers between devices, swap_dp(): return lax.ppermute(x, 'dp', [(0, 1), (1, 0)])  21.8 us
    ppermute x18, waiting for transfers between devices, swap_y(): return lax.ppermute(x, 'fsdp', [(f, f ^ 2) for f in range(16)])  21.7 us
    pallas_call x1, Pallas kernels, attention_back(): pl.pallas_call(attention_back_kernel, grid_spec=pltpu.PrefetchScalarGridS...  19.9 us
    ppermute x18, starting transfers between devices, swap_y(): return lax.ppermute(x, 'fsdp', [(f, f ^ 2) for f in range(16)])  19.5 us
  transfers between devices with their start and end apart: 68, of which 18 were waited for; matrix products, arithmetic and copies ran while one was open for 8% of the time, Pallas kernels for 42%

profile of v5, /device:TPU:0, one launch (start us, length us, event | category | flops | bytes accessed | tf_op | source)
XLA Modules:
  0.0 417.2 jit_solution(7895901692389262557)
XLA Ops:
  19.6 3.7 gather_fusion.2
  23.3 3.7 gather_fusion.1
  40.6 3.4 collective-permute-done.2
  44.9 5.9 %collective-permute-done.5.refs_3_ = bf16[6,48,768]{2,1,0:T(8,128)(2,1)S(1)} collective-permute-done((bf16[6,48,768]{2,1,0:T(8,128)(2,1)}, bf16[6,48,768]{2,1,0:T(8,128)(2,1)S(1)}, u32[]{:S(2)}, u32[]{:S(2)}) %collective-permute-start.5) | collective-permute-done | bytes 442400 | tf_op jit(solution)/shard_map/ppermute | solution.py:548
  54.8 17.9 %collective-permute-done.6.refs_0_ = bf16[6,48,768]{2,1,0:T(8,128)(2,1)S(1)} collective-permute-done((bf16[6,48,768]{2,1,0:T(8,128)(2,1)S(1)}, bf16[6,48,768]{2,1,0:T(8,128)(2,1)S(1)}, u32[]{:S(2)}, u32[]{:S(2)}) %collective-permute-start.6) | collective-permute-done | bytes 442400 | tf_op jit(solution)/shard_map/ppermute | solution.py:536
  82.9 11.0 %collective-permute-done.11 = bf16[3,48,768]{2,1,0:T(8,128)(2,1)S(1)} collective-permute-done((bf16[3,48,768]{2,1,0:T(8,128)(2,1)}, bf16[3,48,768]{2,1,0:T(8,128)(2,1)S(1)}, u32[]{:S(2)}, u32[]{:S(2)}) %collective-permute-start.11) | collective-permute-done | bytes 221216 | tf_op jit(solution)/shard_map/ppermute | solution.py:540
  100.2 3.8 all-to-all-start
  104.0 18.0 %project.1 = (bf16[1536,768]{1,0:T(8,128)(2,1)}, bf16[1536,768]{1,0:T(8,128)(2,1)}, bf16[1536,768]{1,0:T(8,128)(2,1)}, bf16[336,768]{1,0:T(8,128)(2,1)}, bf16[33...) custom-call(s32[40]{0:T(128)} %stack.181.rows_ref, s32[3,112,1]{2,1,0:T(8,128)} %copy.32.pos_ref, ...), custom_call_target="tpu_custom_call" | custom-call | flops 17999998976 | bytes 20000000 | tf_op jit(solution)/shard_map/project/pallas_call | solution.py:205
  122.0 25.6 %masked.1 = (f32[336,768]{1,0:T(8,128)}, bf16[336,768]{1,0:T(8,128)(2,1)}, f32[16,768]{1,0:T(8,128)}, bf16[96,48,768]{2,1,0:T(8,128)(2,1)}, bf16[24,48,768]{2,1,...) custom-call(s32[192]{0:T(256)} %fusion.5.place_ref, ...), custom_call_target="tpu_custom_call" | custom-call | flops 24000000000 | bytes 30000000 | tf_op jit(solution)/shard_map/masked/pallas_call | solution.py:311
  147.6 19.9 %attention_back.1 = (bf16[336,768]{1,0:T(8,128)(2,1)}, bf16[1536,768]{1,0:T(8,128)(2,1)}, bf16[1536,768]{1,0:T(8,128)(2,1)}, f32[8,768]{1,0:T(8,128)}, bf16[96,4...) custom-call(s32[192]{0:T(256)} %fusion.5.place_ref, ...), custom_call_target="tpu_custom_call", output_to_operand_aliasing={{4}: (7, {}), {5}: (8, {}), {6}: (9, {}), {7}: (10, {})} | custom-call | flops 24999999488 | bytes 30000000 | tf_op jit(solution)/shard_map/attention_back/pallas_call | solution.py:406
  168.4 8.3 %collective-permute-done.31 = bf16[24,48,768]{2,1,0:T(8,128)(2,1)} collective-permute-done((bf16[24,48,768]{2,1,0:T(8,128)(2,1)}, bf16[24,48,768]{2,1,0:T(8,128)(2,1)}, u32[]{:S(2)}, u32[]{:S(2)}) %collective-permute-start.31) | collective-permute-done | bytes 1769504 | tf_op jit(solution)/shard_map/ppermute | solution.py:544
  176.6 3.3 core_sum.3
  182.6 9.9 %collective-permute-done.32.to_a_ref = bf16[1,6,48,768]{3,2,1,0:T(8,128)(2,1)S(1)} collective-permute-done((bf16[1,6,48,768]{3,2,1,0:T(8,128)(2,1)}, bf16[1,6,48,768]{3,2,1,0:T(8,128)(2,1)S(1)}, u32[]{:S(2)}, u32[]{:S(2)}) %collective-permute-start.32) | collective-permute-done | bytes 442400 | tf_op jit(solution)/shard_map/ppermute | solution.py:536
  197.4 4.7 %core_sum.4 = (bf16[2,6,48,768]{3,2,1,0:T(8,128)(2,1)}, bf16[2,6,48,768]{3,2,1,0:T(8,128)(2,1)}, bf16[2,6,48,768]{3,2,1,0:T(8,128)(2,1)}, bf16[2,6,48,768]{3,2,1,0:T(8,128)(2,1)}) custom-call(bf16[4,4,6,48,768]{4,3,2,1,0:T(8,128)(2,1)} %bitcast.113, bf16[2,4,6,48,768]{4,3,2,1,0:T(8,128)(2,1)} %bitcast.78.from_ref, ...), custom_call_target="tpu_custom_call" | custom-call | bytes 1000 | tf_op jit(solution)/shard_map/core_sum/pallas_call | solution.py:580
  206.7 14.0 %forward_page.3.rest_0_ = bf16[1536,768]{1,0:T(8,128)(2,1)} custom-call(bf16[1536,768]{1,0:T(8,128)(2,1)} %tok_ref.9, bf16[1536,768]{1,0:T(8,128)(2,1)} %get-tuple-element.85.q_ref, bf16[1536,768]{1,0:T(8,128)(2,1)} %get-tuple-element.86.k_ref, bf16[1536,768]{1,0:T(8,128)(2,1)} %get-tuple-element.87.v_ref, f32[12,768]{1,0:T(8,128)} %vec_ref.9, ...), custom_call_target="tpu_custom_call" | custom-call | bytes 1000 | tf_op jit(solution)/shard_map/forward_page/pallas_call | solution.py:464
  220.8 4.1 collective-permute-done.37.to_a_ref
  242.0 3.7 collective-permute-done.43.rest_0_
  249.2 4.3 %collective-permute-start.47 = (bf16[6,48,768]{2,1,0:T(8,128)(2,1)}, bf16[6,48,768]{2,1,0:T(8,128)(2,1)S(1)}, u32[]{:S(2)}, u32[]{:S(2)}) collective-permute-start(bf16[6,48,768]{2,1,0:T(8,128)(2,1)} %get-tuple-element.127), channel_id=1, source_target_pairs={{0,12},{1,13},{2,14},{3,15},{4,0},{5,1},{6,2},{7,3},{8,4},{9,5},{1... | collective-permute-start | bytes 1327112 | tf_op jit(solution)/shard_map/ppermute | solution.py:548
  258.8 3.7 gather_fusion.4
  262.6 14.0 %forward_page.4.refs_7_.rest_0_ = bf16[1536,768]{1,0:T(8,128)(2,1)} custom-call(bf16[1536,768]{1,0:T(8,128)(2,1)} %tok_ref.9, bf16[1536,768]{1,0:T(8,128)(2,1)} %get-tuple-element.85.q_ref, bf16[1536,768]{1,0:T(8,128)(2,1)} %get-tuple-element.86.k_ref, bf16[1536,768]{1,0:T(8,128)(2,1)} %get-tuple-element.87.v_ref, ...), custom_call_target="tpu_custom_call", output_to_operand_aliasing={{}: (6, {})} | custom-call | bytes 1000 | tf_op jit(solution)/shard_map/forward_page/pallas_call | solution.py:464
  277.7 4.0 weight_step.1
  284.3 3.8 collective-permute-start.49
  289.5 11.4 %input_grad.1.refs_2_ = f32[1536,768]{1,0:T(8,128)} custom-call(s32[3,112,1]{2,1,0:T(8,128)} %copy.32.pos_ref, bf16[336,768]{1,0:T(8,128)(2,1)} %get-tuple-element.133.dq_ref, bf16[1536,768]{1,0:T(8,128)(2,1)} %get-tuple-element.134.dk_ref, bf16[1536,768]{1,0:T(8,128)(2,1)} %get-tuple-element.135.dv_ref, f32[336,768]{1,0:T(8,128)} %get-tuple-element.136.gr_ref, ...), custom_call_target="tpu_custom_call" | custom-call | bytes 1000 | tf_op jit(solution)/shard_map/input_grad/pallas_call | solution.py:506
  307.5 3.5 pick_blocks.3.rest_1_
  311.0 3.7 all-to-all-start.1
  321.5 14.0 %forward_page.5.refs_1_ = bf16[1536,768]{1,0:T(8,128)(2,1)} custom-call(bf16[1536,768]{1,0:T(8,128)(2,1)} %tok_ref.9, bf16[1536,768]{1,0:T(8,128)(2,1)} %get-tuple-element.85.q_ref, bf16[1536,768]{1,0:T(8,128)(2,1)} %get-tuple-element.86.k_ref, bf16[1536,768]{1,0:T(8,128)(2,1)} %get-tuple-element.87.v_ref, ...), custom_call_target="tpu_custom_call", output_to_operand_aliasing={{}: (6, {})} | custom-call | bytes 1000 | tf_op jit(solution)/shard_map/forward_page/pallas_call | solution.py:464
  335.6 13.7 %collective-permute-done.54.refs_0_ = bf16[6,48,768]{2,1,0:T(8,128)(2,1)S(1)} collective-permute-done((bf16[6,48,768]{2,1,0:T(8,128)(2,1)}, bf16[6,48,768]{2,1,0:T(8,128)(2,1)S(1)}, u32[]{:S(2)}, u32[]{:S(2)}) %collective-permute-start.54) | collective-permute-done | bytes 442400 | tf_op jit(solution)/shard_map/ppermute | solution.py:548
  374.7 5.7 %moment_step.2 = (f32[12,2,48,768]{3,2,1,0:T(8,128)}, f32[12,2,48,768]{3,2,1,0:T(8,128)}) custom-call(s32[2]{0:T(128)} %pad_add_fusion.1.info_ref, bf16[12,48,768]{2,1,0:T(8,128)(2,1)} %pick_blocks.4.refs_2_.grad_ref, f32[12,2,48,768]{3,2,1,0:T(8,128)} %bitcast.117, f32[12,2,48,768]{3,2,1,0:T(8,128)} %bitcast.115, bf16[3,48,768]{2,1,0:T(8,128)(2,1)} %get-tuple-element.140.rest_0_), custom_call_target="tpu_custom_call" | custom-call | bytes 1000 | tf_op jit(solution)/shard_map/moment_step/pallas_call | solution.py:714
  380.4 3.4 collective-permute-done.59.refs_8_
  384.6 4.2 %pick_blocks.5 = (bf16[12,48,768]{2,1,0:T(8,128)(2,1)}, bf16[12,48,768]{2,1,0:T(8,128)(2,1)}) custom-call(s32[24]{0:T(128)} %pad_add_fusion.from_ref, bf16[6,48,768]{2,1,0:T(8,128)(2,1)} %get-tuple-element.132.rest_0_.refs_0_, bf16[6,48,768]{2,1,0:T(8,128)(2,1)} %copy-done.8, bf16[6,48,768]{2,1,0:T(8,128)(2,1)} %copy-done.9, ...), custom_call_target="tpu_custom_call" | custom-call | bytes 1000 | tf_op jit(solution)/shard_map/pick_blocks/pallas_call | solution.py:764
  392.6 8.7 %collective-permute-done.64.grad_ref = bf16[12,48,768]{2,1,0:T(8,128)(2,1)} collective-permute-done((bf16[12,48,768]{2,1,0:T(8,128)(2,1)}, bf16[12,48,768]{2,1,0:T(8,128)(2,1)}, u32[]{:S(2)}, u32[]{:S(2)}) %collective-permute-start.64) | collective-permute-done | bytes 884768 | tf_op jit(solution)/shard_map/ppermute | solution.py:536
  401.2 6.0 %moment_step.3 = (f32[12,2,48,768]{3,2,1,0:T(8,128)}, f32[12,2,48,768]{3,2,1,0:T(8,128)}) custom-call(s32[2]{0:T(128)} %pad_add_fusion.2.info_ref, bf16[12,48,768]{2,1,0:T(8,128)(2,1)} %collective-permute-done.64.grad_ref, f32[12,2,48,768]{3,2,1,0:T(8,128)} %bitcast.118, f32[12,2,48,768]{3,2,1,0:T(8,128)} %bitcast.116, ...), custom_call_target="tpu_custom_call", output_to_operand_aliasing={{0}: (4, {}), {1}: (5, {})} | custom-call | bytes 1000 | tf_op jit(solution)/shard_map/moment_step/pallas_call | solution.py:714
  (281 shorter events, 136.8 us)
Async XLA Ops:
  9.1 24.9 %collective-permute-start = (bf16[6,48,768]{2,1,0:T(8,128)(2,1)}, bf16[6,48,768]{2,1,0:T(8,128)(2,1)}, u32[]{:S(2)}, u32[]{:S(2)}) collective-permute-start(bf16[6,48,768]{2,1,0:T(8,128)(2,1)} %bitcast.41), channel_id=1, source_target_pairs={{0,16},{16,0},{1,17},{17,1},{2,18},{18,2},{3,19},{19,3},{4,20},{20... | collective-permute-start | bytes 1327112 | tf_op jit(solution)/shard_map/ppermute | solution.py:536
  12.1 21.9 %collective-permute-start.1 = (bf16[6,48,768]{2,1,0:T(8,128)(2,1)}, bf16[6,48,768]{2,1,0:T(8,128)(2,1)}, u32[]{:S(2)}, u32[]{:S(2)}) collective-permute-start(bf16[6,48,768]{2,1,0:T(8,128)(2,1)} %bitcast.41), channel_id=1, source_target_pairs={{0,2},{1,3},{2,0},{3,1},{4,6},{5,7},{6,4},{7,5},{8,10},{9,11},{10,... | collective-permute-start | bytes 1327112 | tf_op jit(solution)/shard_map/ppermute | solution.py:540
  13.6 23.2 %collective-permute-start.4 = (bf16[6,48,768]{2,1,0:T(8,128)(2,1)}, bf16[6,48,768]{2,1,0:T(8,128)(2,1)}, u32[]{:S(2)}, u32[]{:S(2)}) collective-permute-start(bf16[6,48,768]{2,1,0:T(8,128)(2,1)} %bitcast.41), channel_id=1, source_target_pairs={{0,4},{1,5},{2,6},{3,7},{4,8},{5,9},{6,10},{7,11},{8,12},{9,13},{1... | collective-permute-start | bytes 1327112 | tf_op jit(solution)/shard_map/ppermute | solution.py:548
  15.2 21.6 %collective-permute-start.8 = (bf16[6,48,768]{2,1,0:T(8,128)(2,1)}, bf16[6,48,768]{2,1,0:T(8,128)(2,1)}, u32[]{:S(2)}, u32[]{:S(2)}) collective-permute-start(bf16[6,48,768]{2,1,0:T(8,128)(2,1)} %bitcast.41), channel_id=1, source_target_pairs={{0,12},{1,13},{2,14},{3,15},{4,0},{5,1},{6,2},{7,3},{8,4},{9,5},{1... | collective-permute-start | bytes 1327112 | tf_op jit(solution)/shard_map/ppermute | solution.py:548
  17.4 23.2 %collective-permute-start.15 = (bf16[6,48,768]{2,1,0:T(8,128)(2,1)}, bf16[6,48,768]{2,1,0:T(8,128)(2,1)}, u32[]{:S(2)}, u32[]{:S(2)}) collective-permute-start(bf16[6,48,768]{2,1,0:T(8,128)(2,1)} %bitcast.41), channel_id=1, source_target_pairs={{0,1},{1,0},{2,3},{3,2},{4,5},{5,4},{6,7},{7,6},{8,9},{9,8},{10,11... | collective-permute-start | bytes 1327112 | tf_op jit(solution)/shard_map/ppermute | solution.py:544
  38.9 33.8 %collective-permute-start.9 = (bf16[12,48,768]{2,1,0:T(8,128)(2,1)}, bf16[12,48,768]{2,1,0:T(8,128)(2,1)S(1)}, u32[]{:S(2)}, u32[]{:S(2)}) collective-permute-start(bf16[12,48,768]{2,1,0:T(8,128)(2,1)} %move.10.refs_2_), channel_id=1, source_target_pairs={{0,16},{16,0},{1,17},{17,1},{2,18},{18,2},{3,19},{19,3},{4,20},{20... | collective-permute-start | bytes 2654216 | tf_op jit(solution)/shard_map/ppermute | solution.py:536
  44.0 29.2 %collective-permute-start.10 = (bf16[12,48,768]{2,1,0:T(8,128)(2,1)}, bf16[12,48,768]{2,1,0:T(8,128)(2,1)S(1)}, u32[]{:S(2)}, u32[]{:S(2)}) collective-permute-start(bf16[12,48,768]{2,1,0:T(8,128)(2,1)} %move.10.refs_2_), channel_id=1, source_target_pairs={{0,2},{1,3},{2,0},{3,1},{4,6},{5,7},{6,4},{7,5},{8,10},{9,11},{10,... | collective-permute-start | bytes 2654216 | tf_op jit(solution)/shard_map/ppermute | solution.py:540
  50.8 21.9 %collective-permute-start.6 = (bf16[6,48,768]{2,1,0:T(8,128)(2,1)S(1)}, bf16[6,48,768]{2,1,0:T(8,128)(2,1)S(1)}, u32[]{:S(2)}, u32[]{:S(2)}) collective-permute-start(bf16[6,48,768]{2,1,0:T(8,128)(2,1)S(1)} %collective-permute-done.5.refs_3_), channel_id=1, source_target_pairs={{0,16},{16,0},{1,17},{17,1},{2,18},{18,2},{3,19},{19,3},{4,20},{20... | collective-permute-start | bytes 1327112 | tf_op jit(solution)/shard_map/ppermute | solution.py:536
  52.5 30.3 %collective-permute-start.25 = (bf16[12,48,768]{2,1,0:T(8,128)(2,1)}, bf16[12,48,768]{2,1,0:T(8,128)(2,1)}, u32[]{:S(2)}, u32[]{:S(2)}) collective-permute-start(bf16[12,48,768]{2,1,0:T(8,128)(2,1)} %move.10.refs_2_), channel_id=1, source_target_pairs={{0,1},{1,0},{2,3},{3,2},{4,5},{5,4},{6,7},{7,6},{8,9},{9,8},{10,11... | collective-permute-start | bytes 2654216 | tf_op jit(solution)/shard_map/ppermute | solution.py:544
  53.3 23.2 %collective-permute-start.7 = (bf16[6,48,768]{2,1,0:T(8,128)(2,1)S(1)}, bf16[6,48,768]{2,1,0:T(8,128)(2,1)S(1)}, u32[]{:S(2)}, u32[]{:S(2)}) collective-permute-start(bf16[6,48,768]{2,1,0:T(8,128)(2,1)S(1)} %collective-permute-done.5.refs_3_), channel_id=1, source_target_pairs={{0,2},{1,3},{2,0},{3,1},{4,6},{5,7},{6,4},{7,5},{8,10},{9,11},{10,... | collective-permute-start | bytes 1327112 | tf_op jit(solution)/shard_map/ppermute | solution.py:540
  100.2 95.4 %all-to-all-start = ((bf16[16,3,48,768]{3,2,1,0:T(8,128)(2,1)}), bf16[16,3,48,768]{3,2,1,0:T(8,128)(2,1)S(1)}, u32[]{:S(2)}, u32[]{:S(2)}) async-start(bf16[16,3,48,768]{3,2,1,0:T(8,128)(2,1)} %pad_maximum_fusion.refs_2_), calls=%async_computation | async-start | bytes 7077888 | tf_op jit(solution)/shard_map/all_to_all | solution.py:955
  167.5 28.1 %collective-permute-start.30 = (bf16[48,48,768]{2,1,0:T(8,128)(2,1)}, bf16[48,48,768]{2,1,0:T(8,128)(2,1)}, u32[]{:S(2)}, u32[]{:S(2)}) collective-permute-start(bf16[48,48,768]{2,1,0:T(8,128)(2,1)} %get-tuple-element.98), channel_id=1, source_target_pairs={{0,1},{1,0},{2,3},{3,2},{4,5},{5,4},{6,7},{7,6},{8,9},{9,8},{10,11... | collective-permute-start | bytes 10616840 | tf_op jit(solution)/shard_map/ppermute | solution.py:544
  168.1 68.9 %collective-permute-start.34 = (bf16[24,48,768]{2,1,0:T(8,128)(2,1)}, bf16[24,48,768]{2,1,0:T(8,128)(2,1)}, u32[]{:S(2)}, u32[]{:S(2)}) collective-permute-start(bf16[24,48,768]{2,1,0:T(8,128)(2,1)} %get-tuple-element.107), channel_id=1, source_target_pairs={{0,1},{1,0},{2,3},{3,2},{4,5},{5,4},{6,7},{7,6},{8,9},{9,8},{10,11... | collective-permute-start | bytes 5308424 | tf_op jit(solution)/shard_map/ppermute | solution.py:544
  202.1 22.8 %collective-permute-start.37 = (bf16[2,6,48,768]{3,2,1,0:T(8,128)(2,1)}, bf16[2,6,48,768]{3,2,1,0:T(8,128)(2,1)S(1)}, u32[]{:S(2)}, u32[]{:S(2)}) collective-permute-start(bf16[2,6,48,768]{3,2,1,0:T(8,128)(2,1)} %get-tuple-element.106.rest_0_), channel_id=1, source_target_pairs={{0,16},{16,0},{1,17},{17,1},{2,18},{18,2},{3,19},{19,3},{4,20},{20... | collective-permute-start | bytes 2654216 | tf_op jit(solution)/shard_map/ppermute | solution.py:536
  203.2 22.8 %collective-permute-start.38 = (bf16[2,6,48,768]{3,2,1,0:T(8,128)(2,1)}, bf16[2,6,48,768]{3,2,1,0:T(8,128)(2,1)S(1)}, u32[]{:S(2)}, u32[]{:S(2)}) collective-permute-start(bf16[2,6,48,768]{3,2,1,0:T(8,128)(2,1)} %get-tuple-element.113), channel_id=1, source_target_pairs={{0,2},{1,3},{2,0},{3,1},{4,6},{5,7},{6,4},{7,5},{8,10},{9,11},{10,... | collective-permute-start | bytes 2654216 | tf_op jit(solution)/shard_map/ppermute | solution.py:540
  204.9 27.6 %collective-permute-start.35 = (bf16[1,3,48,768]{3,2,1,0:T(8,128)(2,1)}, bf16[1,3,48,768]{3,2,1,0:T(8,128)(2,1)S(1)}, u32[]{:S(2)}, u32[]{:S(2)}) collective-permute-start(bf16[1,3,48,768]{3,2,1,0:T(8,128)(2,1)} %get-tuple-element.104.rest_0_), channel_id=1, source_target_pairs={{0,2},{1,3},{2,0},{3,1},{4,6},{5,7},{6,4},{7,5},{8,10},{9,11},{10,... | collective-permute-start | bytes 663560 | tf_op jit(solution)/shard_map/ppermute | solution.py:540
  205.3 27.3 %collective-permute-start.36 = (bf16[1,3,48,768]{3,2,1,0:T(8,128)(2,1)}, bf16[1,3,48,768]{3,2,1,0:T(8,128)(2,1)S(1)}, u32[]{:S(2)}, u32[]{:S(2)}) collective-permute-start(bf16[1,3,48,768]{3,2,1,0:T(8,128)(2,1)} %get-tuple-element.110), channel_id=1, source_target_pairs={{0,16},{16,0},{1,17},{17,1},{2,18},{18,2},{3,19},{19,3},{4,20},{20... | collective-permute-start | bytes 663560 | tf_op jit(solution)/shard_map/ppermute | solution.py:536
  249.2 27.5 %collective-permute-start.46 = (bf16[6,48,768]{2,1,0:T(8,128)(2,1)}, bf16[6,48,768]{2,1,0:T(8,128)(2,1)S(1)}, u32[]{:S(2)}, u32[]{:S(2)}) collective-permute-start(bf16[6,48,768]{2,1,0:T(8,128)(2,1)} %get-tuple-element.122.rest_0_), channel_id=1, source_target_pairs={{0,4},{1,5},{2,6},{3,7},{4,8},{5,9},{6,10},{7,11},{8,12},{9,13},{1... | collective-permute-start | bytes 1327112 | tf_op jit(solution)/shard_map/ppermute | solution.py:548
  249.2 27.5 %collective-permute-start.47 = (bf16[6,48,768]{2,1,0:T(8,128)(2,1)}, bf16[6,48,768]{2,1,0:T(8,128)(2,1)S(1)}, u32[]{:S(2)}, u32[]{:S(2)}) collective-permute-start(bf16[6,48,768]{2,1,0:T(8,128)(2,1)} %get-tuple-element.127), channel_id=1, source_target_pairs={{0,12},{1,13},{2,14},{3,15},{4,0},{5,1},{6,2},{7,3},{8,4},{9,5},{1... | collective-permute-start | bytes 1327112 | tf_op jit(solution)/shard_map/ppermute | solution.py:548
  257.4 19.3 %collective-permute-start.44 = (bf16[1,3,48,768]{3,2,1,0:T(8,128)(2,1)}, bf16[1,3,48,768]{3,2,1,0:T(8,128)(2,1)S(1)}, u32[]{:S(2)}, u32[]{:S(2)}) collective-permute-start(bf16[1,3,48,768]{3,2,1,0:T(8,128)(2,1)} %get-tuple-element.123.rest_1_), channel_id=1, source_target_pairs={{0,2},{1,3},{2,0},{3,1},{4,6},{5,7},{6,4},{7,5},{8,10},{9,11},{10,... | collective-permute-start | bytes 663560 | tf_op jit(solution)/shard_map/ppermute | solution.py:540
  281.6 19.3 %collective-permute-start.50 = (bf16[6,48,768]{2,1,0:T(8,128)(2,1)}, bf16[6,48,768]{2,1,0:T(8,128)(2,1)S(1)}, u32[]{:S(2)}, u32[]{:S(2)}) collective-permute-start(bf16[6,48,768]{2,1,0:T(8,128)(2,1)} %get-tuple-element.132.rest_0_.refs_0_), channel_id=1, source_target_pairs={{0,16},{16,0},{1,17},{17,1},{2,18},{18,2},{3,19},{19,3},{4,20},{20... | collective-permute-start | bytes 1327112 | tf_op jit(solution)/shard_map/ppermute | solution.py:536
  284.2 20.1 %collective-permute-start.48 = (bf16[6,48,768]{2,1,0:T(8,128)(2,1)}, bf16[6,48,768]{2,1,0:T(8,128)(2,1)S(1)}, u32[]{:S(2)}, u32[]{:S(2)}) collective-permute-start(bf16[6,48,768]{2,1,0:T(8,128)(2,1)} %get-tuple-element.132.rest_0_.refs_0_), channel_id=1, source_target_pairs={{0,4},{1,5},{2,6},{3,7},{4,8},{5,9},{6,10},{7,11},{8,12},{9,13},{1... | collective-permute-start | bytes 1327112 | tf_op jit(solution)/shard_map/ppermute | solution.py:548
  284.3 20.1 %collective-permute-start.49 = (bf16[6,48,768]{2,1,0:T(8,128)(2,1)}, bf16[6,48,768]{2,1,0:T(8,128)(2,1)S(1)}, u32[]{:S(2)}, u32[]{:S(2)}) collective-permute-start(bf16[6,48,768]{2,1,0:T(8,128)(2,1)} %get-tuple-element.132.rest_0_.refs_0_), channel_id=1, source_target_pairs={{0,12},{1,13},{2,14},{3,15},{4,0},{5,1},{6,2},{7,3},{8,4},{9,5},{1... | collective-permute-start | bytes 1327112 | tf_op jit(solution)/shard_map/ppermute | solution.py:548
  311.0 52.5 %all-to-all-start.1 = ((bf16[16,48,768]{2,1,0:T(8,128)(2,1)}), bf16[16,48,768]{2,1,0:T(8,128)(2,1)S(1)}, u32[]{:S(2)}, u32[]{:S(2)}) async-start(bf16[16,48,768]{2,1,0:T(8,128)(2,1)} %pick_blocks.3.rest_1_), calls=%async_computation.1 | async-start | bytes 2359296 | tf_op jit(solution)/shard_map/all_to_all | solution.py:998
  314.7 75.7 %all-gather.4.cloned.1.call-start = ((), (), s32[]{:S(2)}) async-start(), calls=%async_computation.2 | async-start | bytes 1622016 | tf_op jit(solution)/shard_map/all_gather | solution.py:989
  315.4 40.8 %collective-permute-start.57 = (bf16[12,48,768]{2,1,0:T(8,128)(2,1)S(1)}, bf16[12,48,768]{2,1,0:T(8,128)(2,1)S(1)}, u32[]{:S(2)}, u32[]{:S(2)}) collective-permute-start(bf16[12,48,768]{2,1,0:T(8,128)(2,1)S(1)} %copy-done.3), channel_id=1, source_target_pairs={{0,16},{16,0},{1,17},{17,1},{2,18},{18,2},{3,19},{19,3},{4,20},{20... | collective-permute-start | bytes 2654216 | tf_op jit(solution)/shard_map/ppermute | solution.py:536
  316.5 39.8 %collective-permute-start.58 = (bf16[12,48,768]{2,1,0:T(8,128)(2,1)S(1)}, bf16[12,48,768]{2,1,0:T(8,128)(2,1)}, u32[]{:S(2)}, u32[]{:S(2)}) collective-permute-start(bf16[12,48,768]{2,1,0:T(8,128)(2,1)S(1)} %copy-done.3), channel_id=1, source_target_pairs={{0,2},{1,3},{2,0},{3,1},{4,6},{5,7},{6,4},{7,5},{8,10},{9,11},{10,... | collective-permute-start | bytes 2654216 | tf_op jit(solution)/shard_map/ppermute | solution.py:540
  318.3 31.0 %collective-permute-start.54 = (bf16[6,48,768]{2,1,0:T(8,128)(2,1)}, bf16[6,48,768]{2,1,0:T(8,128)(2,1)S(1)}, u32[]{:S(2)}, u32[]{:S(2)}) collective-permute-start(bf16[6,48,768]{2,1,0:T(8,128)(2,1)} %copy-done.20), channel_id=1, source_target_pairs={{0,4},{1,5},{2,6},{3,7},{4,8},{5,9},{6,10},{7,11},{8,12},{9,13},{1... | collective-permute-start | bytes 1327112 | tf_op jit(solution)/shard_map/ppermute | solution.py:548
  319.9 34.6 %collective-permute-start.52 = (bf16[3,48,768]{2,1,0:T(8,128)(2,1)}, bf16[3,48,768]{2,1,0:T(8,128)(2,1)}, u32[]{:S(2)}, u32[]{:S(2)}) collective-permute-start(bf16[3,48,768]{2,1,0:T(8,128)(2,1)} %get-tuple-element.137.refs_2_), channel_id=1, source_target_pairs={{0,2},{1,3},{2,0},{3,1},{4,6},{5,7},{6,4},{7,5},{8,10},{9,11},{10,... | collective-permute-start | bytes 663560 | tf_op jit(solution)/shard_map/ppermute | solution.py:540
  320.5 35.7 %collective-permute-start.53 = (bf16[3,48,768]{2,1,0:T(8,128)(2,1)}, bf16[3,48,768]{2,1,0:T(8,128)(2,1)}, u32[]{:S(2)}, u32[]{:S(2)}) collective-permute-start(bf16[3,48,768]{2,1,0:T(8,128)(2,1)} %get-tuple-element.138), channel_id=1, source_target_pairs={{0,16},{16,0},{1,17},{17,1},{2,18},{18,2},{3,19},{19,3},{4,20},{20... | collective-permute-start | bytes 663560 | tf_op jit(solution)/shard_map/ppermute | solution.py:536
  359.6 20.8 %collective-permute-start.61 = (bf16[6,48,768]{2,1,0:T(8,128)(2,1)}, bf16[6,48,768]{2,1,0:T(8,128)(2,1)S(1)}, u32[]{:S(2)}, u32[]{:S(2)}) collective-permute-start(bf16[6,48,768]{2,1,0:T(8,128)(2,1)} %get-tuple-element.139.refs_1_), channel_id=1, source_target_pairs={{0,2},{1,3},{2,0},{3,1},{4,6},{5,7},{6,4},{7,5},{8,10},{9,11},{10,... | collective-permute-start | bytes 1327112 | tf_op jit(solution)/shard_map/ppermute | solution.py:540
  373.7 27.5 %collective-permute-start.64 = (bf16[12,48,768]{2,1,0:T(8,128)(2,1)}, bf16[12,48,768]{2,1,0:T(8,128)(2,1)}, u32[]{:S(2)}, u32[]{:S(2)}) collective-permute-start(bf16[12,48,768]{2,1,0:T(8,128)(2,1)} %pick_blocks.4.refs_2_.grad_ref), channel_id=1, source_target_pairs={{0,16},{16,0},{1,17},{17,1},{2,18},{18,2},{3,19},{19,3},{4,20},{20... | collective-permute-start | bytes 2654216 | tf_op jit(solution)/shard_map/ppermute | solution.py:536
  (88 other events, 789.3 us)
Sparse Core Ops, SparseCore 0:
  319.0 68.6 all-gather.3

commit v6 on v5

--- a/solution.py
+++ b/solution.py
@@ -438,9 +438,17 @@
     load.start()
 
     masks, low = half_masks()
-    for pair in range(HEADS // 2):
-        cols = slice(pair * 2 * HD, (pair + 1) * 2 * HD)
-        prob = softmax(mm_last(both_heads(q_ref[:, cols], masks), k_ref[:, cols])).astype(BF)
+    pairs = [slice(pair * 2 * HD, (pair + 1) * 2 * HD) for pair in range(HEADS // 2)]
+
+    def scores_of(cols):
+        return mm_last(both_heads(q_ref[:, cols], masks), k_ref[:, cols])
+
+    ahead = scores_of(pairs[0])
+    for i, cols in enumerate(pairs):
+        scores = ahead
+        if i + 1 < len(pairs):
+            ahead = scores_of(pairs[i + 1])
+        prob = softmax(scores).astype(BF)
         ctx_ref[:, cols] = own_lanes(mm(prob, v_ref[:, cols]), low).astype(BF)
     load.wait()
     resid_one = tok_ref[...].astype(F32) + mm(ctx_ref[...], w_ref[0:WIDTH]) + vec_ref[2:3]
@@ -529,7 +537,7 @@
 
 
 ORDER = (2, 1, 3, 0)
-SIZES = (96, 24, 48, 24)
+SIZES = (96, 24, 24, 24, 24)
 
 
 def swap_dp(x):
@@ -569,24 +577,29 @@
     return pl.BlockSpec(shape, lambda i: (i + first,) + (0,) * (len(shape) - 1))
 
 
-def core_sum_kernel(keep_ref, from_ref, *rest):
-    for part, out in enumerate(rest[-4:]):
-        out[0] = keep_ref[0, part] + from_ref[0, part]
+def core_sum_kernel(count, keep_ref, *rest):
+    for i in range(count):
+
+        @pl.when(pl.program_id(0) == i)
+        def _(i=i):
+            for part, out in enumerate(rest[-4:]):
+                out[0] = keep_ref[0, part] + rest[i][0, part]
 
 
 def core_sum(keep, got, first, *after):
-    count = got.shape[0] // 24
+    count = len(got)
     whole, six = (1, 4, 6, ROWS, WIDTH), (1, 6, ROWS, WIDTH)
+    part = pl.BlockSpec(whole, lambda i: (0, 0, 0, 0, 0))
     return pl.pallas_call(
-        core_sum_kernel,
+        functools.partial(core_sum_kernel, count),
         grid=(count,),
-        in_specs=[blocks_spec(whole, first), blocks_spec(whole)] + [ANY] * len(after),
+        in_specs=[blocks_spec(whole, first)] + [part] * count + [ANY] * len(after),
         out_specs=[blocks_spec(six)] * 4,
         out_shape=[jax.ShapeDtypeStruct((count,) + six[1:], BF)] * 4,
         compiler_params=pltpu.CompilerParams(vmem_limit_bytes=VMEM_LIMIT),
         cost_estimate=cost(0.0, 0.001),
         name="core_sum",
-    )(keep.reshape((4,) + whole[1:]), got.reshape((count,) + whole[1:]), *after)
+    )(keep.reshape((4,) + whole[1:]), *[x.reshape(whole) for x in got], *after)
 
 
 def first_sum_kernel(a_ref, b_ref, to_a_ref, to_b_ref, *rest):
@@ -634,17 +647,17 @@
 def reduce_blocks(dws, tasks, early):
     keep = dws[0]
     got = [swap_core(send) for send in dws[1:]]
-    xs_far, ys_far, a_far, b_far = core_sum(keep, got[0], 0)
+    xs_far, ys_far, a_far, b_far = core_sum(keep, got[:1], 0)
     to_far = swap_dp(xs_far), swap_y(ys_far)
     a_far, b_far, ys_far, xs_far = first_sum(a_far, b_far, *to_far)
     to_far = swap_y(ys_far), swap_dp(xs_far)
-    xs_near, ys_near, a_near, b_near = core_sum(keep, got[1], 1, ys_far, early)
+    xs_near, ys_near, a_near, b_near = core_sum(keep, got[1:3], 1, ys_far, early)
     to_near = swap_dp(xs_near), swap_y(ys_near)
     done = tasks[0](xs_near)
     a_near, b_near, ys_near, xs_near = first_sum(a_near, b_near, *to_near, done)
     to_near = swap_y(ys_near), swap_dp(xs_near)
     (far,) = last_sum(a_far, b_far, *to_far, (), ys_near)
-    xs_own, ys_own, a_own, b_own = core_sum(keep, got[2], 3, far)
+    xs_own, ys_own, a_own, b_own = core_sum(keep, got[3:], 3, far)
     far = up_z(far, 1)
     to_own = swap_dp(xs_own), swap_y(ys_own)
     up, down = last_sum(a_near, b_near, *to_near, (far,), xs_own)
@@ -655,11 +668,18 @@
     return (a_own, to_own[0], b_own, to_own[1]), near, done
 
 
-def weight_step_kernel(halves, wholes, *refs):
+def weight_step_kernel(halves, wholes, from_ref, *refs):
     half_refs, refs = refs[:halves], refs[halves:]
     whole_refs, refs = refs[:wholes], refs[wholes:]
-    state_ref, grad_out, new_out = refs[0], refs[-2], refs[-1]
-    for i in range(grad_out.shape[0]):
+    states, (grad_out, new_out, state_ref, sem) = refs[0], refs[-4:]
+    count = grad_out.shape[0]
+    loads = [
+        pltpu.make_async_copy(states.at[from_ref[i]], state_ref.at[i], sem.at[i])
+        for i in range(count)
+    ]
+    for load in loads:
+        load.start()
+    for i in range(count):
         parts = [ref[i] for ref in whole_refs]
         if halves:
             first = 2 * (i // 3)
@@ -667,30 +687,39 @@
         total = parts[0].astype(F32)
         for part in parts[1:]:
             total = total + part.astype(F32)
-        grad = total.astype(BF)
-        grad_out[i] = grad
+        grad_out[i] = total.astype(BF)
+    for i in range(count):
+        loads[i].wait()
         new, _, _ = adam_step(
             state_ref[i, 0].astype(F32),
             state_ref[i, 1].astype(F32),
             state_ref[i, 2].astype(F32),
-            grad.astype(F32),
+            grad_out[i].astype(F32),
             LEARN_RATE,
         )
         new_out[i] = new.astype(BF)
 
 
-def weight_step(halves, wholes, states, *after):
-    count = states.shape[0]
+def weight_step(source, halves, wholes, states, *after):
+    count = source.shape[0]
     shape = jax.ShapeDtypeStruct((count, ROWS, WIDTH), BF)
     return pl.pallas_call(
         functools.partial(weight_step_kernel, len(halves), len(wholes)),
-        in_specs=[VM] * (len(halves) + len(wholes) + 1) + [ANY] * len(after),
-        out_specs=[VM] * 2,
+        grid_spec=pltpu.PrefetchScalarGridSpec(
+            num_scalar_prefetch=1,
+            grid=(),
+            in_specs=[VM] * (len(halves) + len(wholes)) + [ANY] * (1 + len(after)),
+            out_specs=[VM] * 2,
+            scratch_shapes=[
+                pltpu.VMEM((count, 3, ROWS, WIDTH), BF),
+                pltpu.SemaphoreType.DMA((count,)),
+            ],
+        ),
         out_shape=[shape, shape],
         compiler_params=pltpu.CompilerParams(vmem_limit_bytes=VMEM_LIMIT),
         cost_estimate=cost(0.0, 0.001),
         name="weight_step",
-    )(*halves, *wholes, states, *after)
+    )(source, *halves, *wholes, states, *after)
 
 
 def moment_step_kernel(info_ref, grad_ref, first_ref, second_ref, *rest):
@@ -971,10 +1000,8 @@
         return token_grad[0]
 
     tasks = [functools.partial(page_task, page) for page in range(pages)] + [grad_task]
-    arrived = states
-    states = jnp.take(states, state_at, axis=0, mode="clip")
     if direct:
-        halves, wholes, done = reduce_blocks(dws, tasks, arrived)
+        halves, wholes, done = reduce_blocks(dws, tasks, states)
     else:
         if groups > 1:
             mine = lax.psum_scatter(dws[0], ("dp", "fsdp"), scatter_dimension=0, tiled=True)
@@ -984,7 +1011,7 @@
         for task in tasks:
             done = task()
         halves, wholes = (), (mine,)
-    mine, new_mine = weight_step(halves, wholes, states, done)
+    mine, new_mine = weight_step(state_at, halves, wholes, states, done)
     mine, grad_vectors = lax.optimization_barrier((mine, grad_vectors))
     grad_vectors = jnp.sum(lax.all_gather(grad_vectors, ("dp", "fsdp")), axis=0)
 

time: 426 us -> 424 us (level)
  starting transfers between devices: 66.7 us -> 72.2 us
  local copies, waits for them, and re-layouts: 34 us -> 29.2 us
  waiting for transfers between devices: 97.6 us -> 93.1 us
    ppermute x18, waiting for transfers between devices: 21.7 us -> 28 us  [swap_y(): return lax.ppermute(x, 'fsdp', [(f, f ^ 2) for f in range(16)])]
    ppermute x19 -> x20, waiting for transfers between devices: 9.14 us -> 3.09 us  [swap_core(): return lax.ppermute(x, 'fsdp', [(f, f ^ 1) for f in range(16)])]
  transfers between devices with their start and end apart: 68 -> 69, of which waited for: 18 -> 19; matrix products, arithmetic and copies ran while one was open for 8% -> 7% of each run, Pallas kernels for 42% -> 42%
where the time goes in v6:
time: 424 us; the launch traced here: 416 us
  Pallas kernels  187 us (44%)
  waiting for transfers between devices  93.1 us (22%)
  starting transfers between devices  72.2 us (17%)
  local copies, waits for them, and re-layouts  29.2 us (7%)
  other arithmetic  19 us (4%)
  between operations  15.5 us (4%)
    pallas_call x3, Pallas kernels, forward_page(): pl.pallas_call(forward_kernel, grid=(1,), in_specs=[page, page, page, pag...  42 us
    ppermute x19, waiting for transfers between devices, swap_dp(): return lax.ppermute(x, 'dp', [(0, 1), (1, 0)])  39.5 us
    ppermute x18, waiting for transfers between devices, swap_y(): return lax.ppermute(x, 'fsdp', [(f, f ^ 2) for f in range(16)])  28 us
    pallas_call x1, Pallas kernels, masked_part(): pl.pallas_call(masked_kernel, grid_spec=pltpu.PrefetchScalarGridSpec(num_...  26.1 us
    ppermute x9, waiting for transfers between devices, up_z(): lax.ppermute(x, 'fsdp', [(f, (f + 4 * steps) % 16) for f in range(16)])  21.8 us
    ppermute x18, starting transfers between devices, swap_y(): return lax.ppermute(x, 'fsdp', [(f, f ^ 2) for f in range(16)])  20.3 us
    pallas_call x1, Pallas kernels, attention_back(): pl.pallas_call(attention_back_kernel, grid_spec=pltpu.PrefetchScalarGridS...  20 us
    ppermute x19, starting transfers between devices, swap_dp(): return lax.ppermute(x, 'dp', [(0, 1), (1, 0)])  19.8 us
  transfers between devices with their start and end apart: 69, of which 19 were waited for; matrix products, arithmetic and copies ran while one was open for 7% of the time, Pallas kernels for 42%

profile of v6, /device:TPU:0, one launch (start us, length us, event | category | flops | bytes accessed | tf_op | source)
XLA Modules:
  0.0 415.7 jit_solution(1043267052620034851)
XLA Ops:
  9.6 4.6 %collective-permute-start.8 = (bf16[6,48,768]{2,1,0:T(8,128)(2,1)}, bf16[6,48,768]{2,1,0:T(8,128)(2,1)}, u32[]{:S(2)}, u32[]{:S(2)}) collective-permute-start(bf16[6,48,768]{2,1,0:T(8,128)(2,1)} %bitcast.41), channel_id=1, source_target_pairs={{0,12},{1,13},{2,14},{3,15},{4,0},{5,1},{6,2},{7,3},{8,4},{9,5},{1... | collective-permute-start | bytes 1327112 | tf_op jit(solution)/shard_map/ppermute | solution.py:556
  20.0 3.7 gather_fusion.2
  23.7 3.7 gather_fusion.1
  31.2 3.2 pad_maximum_fusion.refs_2_
  40.1 3.5 collective-permute-done.3
  45.3 5.3 %collective-permute-done.5.refs_3_ = bf16[6,48,768]{2,1,0:T(8,128)(2,1)S(1)} collective-permute-done((bf16[6,48,768]{2,1,0:T(8,128)(2,1)}, bf16[6,48,768]{2,1,0:T(8,128)(2,1)S(1)}, u32[]{:S(2)}, u32[]{:S(2)}) %collective-permute-start.5) | collective-permute-done | bytes 442400 | tf_op jit(solution)/shard_map/ppermute | solution.py:556
  53.6 20.0 %collective-permute-done.7.refs_1_ = bf16[6,48,768]{2,1,0:T(8,128)(2,1)S(1)} collective-permute-done((bf16[6,48,768]{2,1,0:T(8,128)(2,1)S(1)}, bf16[6,48,768]{2,1,0:T(8,128)(2,1)S(1)}, u32[]{:S(2)}, u32[]{:S(2)}) %collective-permute-start.7) | collective-permute-done | bytes 442400 | tf_op jit(solution)/shard_map/ppermute | solution.py:548
  83.1 4.4 %collective-permute-done.12 = bf16[3,48,768]{2,1,0:T(8,128)(2,1)} collective-permute-done((bf16[3,48,768]{2,1,0:T(8,128)(2,1)}, bf16[3,48,768]{2,1,0:T(8,128)(2,1)}, u32[]{:S(2)}, u32[]{:S(2)}) %collective-permute-start.12) | collective-permute-done | bytes 221216 | tf_op jit(solution)/shard_map/ppermute | solution.py:544
  90.9 5.5 %collective-permute-done.14 = bf16[6,48,768]{2,1,0:T(8,128)(2,1)} collective-permute-done((bf16[6,48,768]{2,1,0:T(8,128)(2,1)}, bf16[6,48,768]{2,1,0:T(8,128)(2,1)}, u32[]{:S(2)}, u32[]{:S(2)}) %collective-permute-start.14) | collective-permute-done | bytes 442400 | tf_op jit(solution)/shard_map/ppermute | solution.py:544
  98.5 4.9 %all-to-all-start = ((bf16[16,3,48,768]{3,2,1,0:T(8,128)(2,1)}), bf16[16,3,48,768]{3,2,1,0:T(8,128)(2,1)S(1)}, u32[]{:S(2)}, u32[]{:S(2)}) async-start(bf16[16,3,48,768]{3,2,1,0:T(8,128)(2,1)} %pad_maximum_fusion.refs_2_), calls=%async_computation | async-start | bytes 7077888 | tf_op jit(solution)/shard_map/all_to_all | solution.py:984
  103.5 18.0 %project.1 = (bf16[1536,768]{1,0:T(8,128)(2,1)}, bf16[1536,768]{1,0:T(8,128)(2,1)}, bf16[1536,768]{1,0:T(8,128)(2,1)}, bf16[336,768]{1,0:T(8,128)(2,1)}, bf16[33...) custom-call(s32[40]{0:T(128)} %stack.181.rows_ref, s32[3,112,1]{2,1,0:T(8,128)} %copy.33.pos_ref, ...), custom_call_target="tpu_custom_call" | custom-call | flops 17999998976 | bytes 20000000 | tf_op jit(solution)/shard_map/project/pallas_call | solution.py:205
  121.5 26.1 %masked.1 = (f32[336,768]{1,0:T(8,128)}, bf16[336,768]{1,0:T(8,128)(2,1)}, f32[16,768]{1,0:T(8,128)}, bf16[96,48,768]{2,1,0:T(8,128)(2,1)}, bf16[24,48,768]{2,1,...) custom-call(s32[192]{0:T(256)} %fusion.5.place_ref, ...), custom_call_target="tpu_custom_call" | custom-call | flops 24000000000 | bytes 30000000 | tf_op jit(solution)/shard_map/masked/pallas_call | solution.py:311
  147.6 20.0 %attention_back.1 = (bf16[336,768]{1,0:T(8,128)(2,1)}, bf16[1536,768]{1,0:T(8,128)(2,1)}, bf16[1536,768]{1,0:T(8,128)(2,1)}, f32[8,768]{1,0:T(8,128)}, bf16[96,4...) custom-call(s32[192]{0:T(256)} %fusion.5.place_ref, ...), custom_call_target="tpu_custom_call", output_to_operand_aliasing={{4}: (7, {}), {5}: (8, {}), {6}: (9, {}), {7}: (10, {}), {8... | custom-call | flops 24999999488 | bytes 30000000 | tf_op jit(solution)/shard_map/attention_back/pallas_call | solution.py:406
  171.8 3.3 core_sum.3
  178.4 9.3 %collective-permute-done.33.to_a_ref = bf16[1,6,48,768]{3,2,1,0:T(8,128)(2,1)S(1)} collective-permute-done((bf16[1,6,48,768]{3,2,1,0:T(8,128)(2,1)}, bf16[1,6,48,768]{3,2,1,0:T(8,128)(2,1)S(1)}, u32[]{:S(2)}, u32[]{:S(2)}) %collective-permute-start.33) | collective-permute-done | bytes 442400 | tf_op jit(solution)/shard_map/ppermute | solution.py:544
  193.2 4.7 %core_sum.4 = (bf16[2,6,48,768]{3,2,1,0:T(8,128)(2,1)}, bf16[2,6,48,768]{3,2,1,0:T(8,128)(2,1)}, bf16[2,6,48,768]{3,2,1,0:T(8,128)(2,1)}, bf16[2,6,48,768]{3,2,1,0:T(8,128)(2,1)}) custom-call(bf16[4,4,6,48,768]{4,3,2,1,0:T(8,128)(2,1)} %bitcast.105, bf16[1,4,6,48,768]{4,3,2,1,0:T(8,128)(2,1)} %bitcast.78.rest_0_, ...), custom_call_target="tpu_custom_call" | custom-call | bytes 1000 | tf_op jit(solution)/shard_map/core_sum/pallas_call | solution.py:593
  202.1 14.0 %forward_page.3.rest_0_ = bf16[1536,768]{1,0:T(8,128)(2,1)} custom-call(bf16[1536,768]{1,0:T(8,128)(2,1)} %tok_ref.9, bf16[1536,768]{1,0:T(8,128)(2,1)} %get-tuple-element.87.q_ref, bf16[1536,768]{1,0:T(8,128)(2,1)} %get-tuple-element.88.k_ref, bf16[1536,768]{1,0:T(8,128)(2,1)} %get-tuple-element.89.v_ref, f32[12,768]{1,0:T(8,128)} %vec_ref.9, ...), custom_call_target="tpu_custom_call" | custom-call | bytes 1000 | tf_op jit(solution)/shard_map/forward_page/pallas_call | solution.py:472
  216.1 4.7 %collective-permute-done.39.to_b_ref = bf16[2,6,48,768]{3,2,1,0:T(8,128)(2,1)S(1)} collective-permute-done((bf16[2,6,48,768]{3,2,1,0:T(8,128)(2,1)}, bf16[2,6,48,768]{3,2,1,0:T(8,128)(2,1)S(1)}, u32[]{:S(2)}, u32[]{:S(2)}) %collective-permute-start.39) | collective-permute-done | bytes 884768 | tf_op jit(solution)/shard_map/ppermute | solution.py:548
  230.6 4.8 %collective-permute-start.44 = (bf16[6,48,768]{2,1,0:T(8,128)(2,1)}, bf16[6,48,768]{2,1,0:T(8,128)(2,1)S(1)}, u32[]{:S(2)}, u32[]{:S(2)}) collective-permute-start(bf16[6,48,768]{2,1,0:T(8,128)(2,1)} %last_sum.2.rest_1_), channel_id=1, source_target_pairs={{0,4},{1,5},{2,6},{3,7},{4,8},{5,9},{6,10},{7,11},{8,12},{9,13},{1... | collective-permute-start | bytes 1327112 | tf_op jit(solution)/shard_map/ppermute | solution.py:556
  235.9 3.2 core_sum.5
  256.6 14.0 %forward_page.4.refs_7_.rest_0_ = bf16[1536,768]{1,0:T(8,128)(2,1)} custom-call(bf16[1536,768]{1,0:T(8,128)(2,1)} %tok_ref.9, bf16[1536,768]{1,0:T(8,128)(2,1)} %get-tuple-element.87.q_ref, bf16[1536,768]{1,0:T(8,128)(2,1)} %get-tuple-element.88.k_ref, bf16[1536,768]{1,0:T(8,128)(2,1)} %get-tuple-element.89.v_ref, ...), custom_call_target="tpu_custom_call", output_to_operand_aliasing={{}: (6, {})} | custom-call | bytes 1000 | tf_op jit(solution)/shard_map/forward_page/pallas_call | solution.py:472
  271.7 5.0 %weight_step.1 = (bf16[6,48,768]{2,1,0:T(8,128)(2,1)}, bf16[6,48,768]{2,1,0:T(8,128)(2,1)}) custom-call(s32[6]{0:T(128)} %fusion.27.from_ref, bf16[1,3,48,768]{3,2,1,0:T(8,128)(2,1)} %get-tuple-element.128.refs_0_, bf16[1,3,48,768]{3,2,1,0:T(8,128)(2,1)} %copy-done.37, bf16[1,3,48,768]{3,2,1,0:T(8,128)(2,1)} %get-tuple-element.129.refs_2_, ...), custom_call_target="tpu_custom_call" | custom-call | bytes 1000 | tf_op jit(solution)/shard_map/weight_step/pallas_call | solution.py:706
  279.1 3.5 collective-permute-start.50
  284.0 11.4 %input_grad.1.refs_2_ = f32[1536,768]{1,0:T(8,128)} custom-call(s32[3,112,1]{2,1,0:T(8,128)} %copy.33.pos_ref, bf16[336,768]{1,0:T(8,128)(2,1)} %get-tuple-element.137.dq_ref, bf16[1536,768]{1,0:T(8,128)(2,1)} %get-tuple-element.138.dk_ref, bf16[1536,768]{1,0:T(8,128)(2,1)} %get-tuple-element.139.dv_ref, f32[336,768]{1,0:T(8,128)} %get-tuple-element.140.gr_ref, ...), custom_call_target="tpu_custom_call" | custom-call | bytes 1000 | tf_op jit(solution)/shard_map/input_grad/pallas_call | solution.py:514
  305.2 6.0 %all-to-all-start.1 = ((bf16[16,48,768]{2,1,0:T(8,128)(2,1)}), bf16[16,48,768]{2,1,0:T(8,128)(2,1)S(1)}, u32[]{:S(2)}, u32[]{:S(2)}) async-start(bf16[16,48,768]{2,1,0:T(8,128)(2,1)} %pick_blocks.3.rest_1_), calls=%async_computation.1 | async-start | bytes 2359296 | tf_op jit(solution)/shard_map/all_to_all | solution.py:1025
  318.2 14.0 %forward_page.5.refs_1_ = bf16[1536,768]{1,0:T(8,128)(2,1)} custom-call(bf16[1536,768]{1,0:T(8,128)(2,1)} %tok_ref.9, bf16[1536,768]{1,0:T(8,128)(2,1)} %get-tuple-element.87.q_ref, bf16[1536,768]{1,0:T(8,128)(2,1)} %get-tuple-element.88.k_ref, bf16[1536,768]{1,0:T(8,128)(2,1)} %get-tuple-element.89.v_ref, ...), custom_call_target="tpu_custom_call", output_to_operand_aliasing={{}: (6, {})} | custom-call | bytes 1000 | tf_op jit(solution)/shard_map/forward_page/pallas_call | solution.py:472
  332.2 13.7 %collective-permute-done.55.refs_0_ = bf16[6,48,768]{2,1,0:T(8,128)(2,1)S(1)} collective-permute-done((bf16[6,48,768]{2,1,0:T(8,128)(2,1)}, bf16[6,48,768]{2,1,0:T(8,128)(2,1)S(1)}, u32[]{:S(2)}, u32[]{:S(2)}) %collective-permute-start.55) | collective-permute-done | bytes 442400 | tf_op jit(solution)/shard_map/ppermute | solution.py:556
  371.1 5.7 %moment_step.2 = (f32[12,2,48,768]{3,2,1,0:T(8,128)}, f32[12,2,48,768]{3,2,1,0:T(8,128)}) custom-call(s32[2]{0:T(128)} %pad_add_fusion.1.info_ref, bf16[12,48,768]{2,1,0:T(8,128)(2,1)} %pick_blocks.4.refs_2_.grad_ref, f32[12,2,48,768]{3,2,1,0:T(8,128)} %bitcast.109, f32[12,2,48,768]{3,2,1,0:T(8,128)} %bitcast.107, bf16[3,48,768]{2,1,0:T(8,128)(2,1)} %get-tuple-element.144.rest_0_), custom_call_target="tpu_custom_call" | custom-call | bytes 1000 | tf_op jit(solution)/shard_map/moment_step/pallas_call | solution.py:743
  376.8 4.2 %collective-permute-done.61.refs_9_ = bf16[3,48,768]{2,1,0:T(8,128)(2,1)S(1)} collective-permute-done((bf16[3,48,768]{2,1,0:T(8,128)(2,1)}, bf16[3,48,768]{2,1,0:T(8,128)(2,1)S(1)}, u32[]{:S(2)}, u32[]{:S(2)}) %collective-permute-start.61) | collective-permute-done | bytes 221216 | tf_op jit(solution)/shard_map/ppermute | solution.py:544
  381.8 4.4 %pick_blocks.5 = (bf16[12,48,768]{2,1,0:T(8,128)(2,1)}, bf16[12,48,768]{2,1,0:T(8,128)(2,1)}) custom-call(s32[24]{0:T(128)} %pad_add_fusion.from_ref, bf16[6,48,768]{2,1,0:T(8,128)(2,1)} %get-tuple-element.136.rest_0_.refs_0_, bf16[6,48,768]{2,1,0:T(8,128)(2,1)} %copy-done.10, bf16[6,48,768]{2,1,0:T(8,128)(2,1)} %copy-done.9, ...), custom_call_target="tpu_custom_call" | custom-call | bytes 1000 | tf_op jit(solution)/shard_map/pick_blocks/pallas_call | solution.py:793
  389.8 9.1 %collective-permute-done.65.grad_ref = bf16[12,48,768]{2,1,0:T(8,128)(2,1)S(1)} collective-permute-done((bf16[12,48,768]{2,1,0:T(8,128)(2,1)S(1)}, bf16[12,48,768]{2,1,0:T(8,128)(2,1)S(1)}, u32[]{:S(2)}, u32[]{:S(2)}) %collective-permute-start.65) | collective-permute-done | bytes 884768 | tf_op jit(solution)/shard_map/ppermute | solution.py:544
  399.9 5.6 %moment_step.3 = (f32[12,2,48,768]{3,2,1,0:T(8,128)}, f32[12,2,48,768]{3,2,1,0:T(8,128)}) custom-call(s32[2]{0:T(128)} %pad_add_fusion.2.info_ref, bf16[12,48,768]{2,1,0:T(8,128)(2,1)} %copy-done.11, f32[12,2,48,768]{3,2,1,0:T(8,128)} %bitcast.110, f32[12,2,48,768]{3,2,1,0:T(8,128)} %bitcast.108, ...), custom_call_target="tpu_custom_call", output_to_operand_aliasing={{0}: (4, {}), {1}: (5, {})} | custom-call | bytes 1000 | tf_op jit(solution)/shard_map/moment_step/pallas_call | solution.py:743
  (281 shorter events, 136.6 us)
Async XLA Ops:
  9.1 28.2 %collective-permute-start.15 = (bf16[6,48,768]{2,1,0:T(8,128)(2,1)}, bf16[6,48,768]{2,1,0:T(8,128)(2,1)}, u32[]{:S(2)}, u32[]{:S(2)}) collective-permute-start(bf16[6,48,768]{2,1,0:T(8,128)(2,1)} %bitcast.41), channel_id=1, source_target_pairs={{0,1},{1,0},{2,3},{3,2},{4,5},{5,4},{6,7},{7,6},{8,9},{9,8},{10,11... | collective-permute-start | bytes 1327112 | tf_op jit(solution)/shard_map/ppermute | solution.py:552
  9.6 27.8 %collective-permute-start.8 = (bf16[6,48,768]{2,1,0:T(8,128)(2,1)}, bf16[6,48,768]{2,1,0:T(8,128)(2,1)}, u32[]{:S(2)}, u32[]{:S(2)}) collective-permute-start(bf16[6,48,768]{2,1,0:T(8,128)(2,1)} %bitcast.41), channel_id=1, source_target_pairs={{0,12},{1,13},{2,14},{3,15},{4,0},{5,1},{6,2},{7,3},{8,4},{9,5},{1... | collective-permute-start | bytes 1327112 | tf_op jit(solution)/shard_map/ppermute | solution.py:556
  14.2 23.1 %collective-permute-start.4 = (bf16[6,48,768]{2,1,0:T(8,128)(2,1)}, bf16[6,48,768]{2,1,0:T(8,128)(2,1)}, u32[]{:S(2)}, u32[]{:S(2)}) collective-permute-start(bf16[6,48,768]{2,1,0:T(8,128)(2,1)} %bitcast.41), channel_id=1, source_target_pairs={{0,4},{1,5},{2,6},{3,7},{4,8},{5,9},{6,10},{7,11},{8,12},{9,13},{1... | collective-permute-start | bytes 1327112 | tf_op jit(solution)/shard_map/ppermute | solution.py:556
  14.2 20.2 %collective-permute-start.1 = (bf16[6,48,768]{2,1,0:T(8,128)(2,1)}, bf16[6,48,768]{2,1,0:T(8,128)(2,1)}, u32[]{:S(2)}, u32[]{:S(2)}) collective-permute-start(bf16[6,48,768]{2,1,0:T(8,128)(2,1)} %bitcast.41), channel_id=1, source_target_pairs={{0,2},{1,3},{2,0},{3,1},{4,6},{5,7},{6,4},{7,5},{8,10},{9,11},{10,... | collective-permute-start | bytes 1327112 | tf_op jit(solution)/shard_map/ppermute | solution.py:548
  43.5 30.5 %collective-permute-start.10 = (bf16[12,48,768]{2,1,0:T(8,128)(2,1)}, bf16[12,48,768]{2,1,0:T(8,128)(2,1)}, u32[]{:S(2)}, u32[]{:S(2)}) collective-permute-start(bf16[12,48,768]{2,1,0:T(8,128)(2,1)} %move.10.refs_2_), channel_id=1, source_target_pairs={{0,2},{1,3},{2,0},{3,1},{4,6},{5,7},{6,4},{7,5},{8,10},{9,11},{10,... | collective-permute-start | bytes 2654216 | tf_op jit(solution)/shard_map/ppermute | solution.py:548
  44.0 30.3 %collective-permute-start.9 = (bf16[12,48,768]{2,1,0:T(8,128)(2,1)}, bf16[12,48,768]{2,1,0:T(8,128)(2,1)}, u32[]{:S(2)}, u32[]{:S(2)}) collective-permute-start(bf16[12,48,768]{2,1,0:T(8,128)(2,1)} %move.10.refs_2_), channel_id=1, source_target_pairs={{0,16},{16,0},{1,17},{17,1},{2,18},{18,2},{3,19},{19,3},{4,20},{20... | collective-permute-start | bytes 2654216 | tf_op jit(solution)/shard_map/ppermute | solution.py:544
  50.5 23.0 %collective-permute-start.7 = (bf16[6,48,768]{2,1,0:T(8,128)(2,1)S(1)}, bf16[6,48,768]{2,1,0:T(8,128)(2,1)S(1)}, u32[]{:S(2)}, u32[]{:S(2)}) collective-permute-start(bf16[6,48,768]{2,1,0:T(8,128)(2,1)S(1)} %collective-permute-done.5.refs_3_), channel_id=1, source_target_pairs={{0,2},{1,3},{2,0},{3,1},{4,6},{5,7},{6,4},{7,5},{8,10},{9,11},{10,... | collective-permute-start | bytes 1327112 | tf_op jit(solution)/shard_map/ppermute | solution.py:548
  52.1 21.7 %collective-permute-start.6 = (bf16[6,48,768]{2,1,0:T(8,128)(2,1)S(1)}, bf16[6,48,768]{2,1,0:T(8,128)(2,1)S(1)}, u32[]{:S(2)}, u32[]{:S(2)}) collective-permute-start(bf16[6,48,768]{2,1,0:T(8,128)(2,1)S(1)} %collective-permute-done.5.refs_3_), channel_id=1, source_target_pairs={{0,16},{16,0},{1,17},{17,1},{2,18},{18,2},{3,19},{19,3},{4,20},{20... | collective-permute-start | bytes 1327112 | tf_op jit(solution)/shard_map/ppermute | solution.py:544
  53.6 28.5 %collective-permute-start.25 = (bf16[12,48,768]{2,1,0:T(8,128)(2,1)}, bf16[12,48,768]{2,1,0:T(8,128)(2,1)S(1)}, u32[]{:S(2)}, u32[]{:S(2)}) collective-permute-start(bf16[12,48,768]{2,1,0:T(8,128)(2,1)} %move.10.refs_2_), channel_id=1, source_target_pairs={{0,1},{1,0},{2,3},{3,2},{4,5},{5,4},{6,7},{7,6},{8,9},{9,8},{10,11... | collective-permute-start | bytes 2654216 | tf_op jit(solution)/shard_map/ppermute | solution.py:552
  98.5 92.9 %all-to-all-start = ((bf16[16,3,48,768]{3,2,1,0:T(8,128)(2,1)}), bf16[16,3,48,768]{3,2,1,0:T(8,128)(2,1)S(1)}, u32[]{:S(2)}, u32[]{:S(2)}) async-start(bf16[16,3,48,768]{3,2,1,0:T(8,128)(2,1)} %pad_maximum_fusion.refs_2_), calls=%async_computation | async-start | bytes 7077888 | tf_op jit(solution)/shard_map/all_to_all | solution.py:984
  168.1 23.3 %collective-permute-start.30 = (bf16[24,48,768]{2,1,0:T(8,128)(2,1)}, bf16[24,48,768]{2,1,0:T(8,128)(2,1)}, u32[]{:S(2)}, u32[]{:S(2)}) collective-permute-start(bf16[24,48,768]{2,1,0:T(8,128)(2,1)} %get-tuple-element.101), channel_id=1, source_target_pairs={{0,1},{1,0},{2,3},{3,2},{4,5},{5,4},{6,7},{7,6},{8,9},{9,8},{10,11... | collective-permute-start | bytes 5308424 | tf_op jit(solution)/shard_map/ppermute | solution.py:552
  168.2 23.2 %collective-permute-start.31 = (bf16[24,48,768]{2,1,0:T(8,128)(2,1)}, bf16[24,48,768]{2,1,0:T(8,128)(2,1)}, u32[]{:S(2)}, u32[]{:S(2)}) collective-permute-start(bf16[24,48,768]{2,1,0:T(8,128)(2,1)} %get-tuple-element.102), channel_id=1, source_target_pairs={{0,1},{1,0},{2,3},{3,2},{4,5},{5,4},{6,7},{7,6},{8,9},{9,8},{10,11... | collective-permute-start | bytes 5308424 | tf_op jit(solution)/shard_map/ppermute | solution.py:552
  168.6 67.2 %collective-permute-start.35 = (bf16[24,48,768]{2,1,0:T(8,128)(2,1)}, bf16[24,48,768]{2,1,0:T(8,128)(2,1)}, u32[]{:S(2)}, u32[]{:S(2)}) collective-permute-start(bf16[24,48,768]{2,1,0:T(8,128)(2,1)} %get-tuple-element.111), channel_id=1, source_target_pairs={{0,1},{1,0},{2,3},{3,2},{4,5},{5,4},{6,7},{7,6},{8,9},{9,8},{10,11... | collective-permute-start | bytes 5308424 | tf_op jit(solution)/shard_map/ppermute | solution.py:552
  197.9 22.9 %collective-permute-start.39 = (bf16[2,6,48,768]{3,2,1,0:T(8,128)(2,1)}, bf16[2,6,48,768]{3,2,1,0:T(8,128)(2,1)S(1)}, u32[]{:S(2)}, u32[]{:S(2)}) collective-permute-start(bf16[2,6,48,768]{3,2,1,0:T(8,128)(2,1)} %get-tuple-element.117), channel_id=1, source_target_pairs={{0,2},{1,3},{2,0},{3,1},{4,6},{5,7},{6,4},{7,5},{8,10},{9,11},{10,... | collective-permute-start | bytes 2654216 | tf_op jit(solution)/shard_map/ppermute | solution.py:548
  199.7 22.8 %collective-permute-start.38 = (bf16[2,6,48,768]{3,2,1,0:T(8,128)(2,1)}, bf16[2,6,48,768]{3,2,1,0:T(8,128)(2,1)S(1)}, u32[]{:S(2)}, u32[]{:S(2)}) collective-permute-start(bf16[2,6,48,768]{3,2,1,0:T(8,128)(2,1)} %get-tuple-element.110.rest_0_), channel_id=1, source_target_pairs={{0,16},{16,0},{1,17},{17,1},{2,18},{18,2},{3,19},{19,3},{4,20},{20... | collective-permute-start | bytes 2654216 | tf_op jit(solution)/shard_map/ppermute | solution.py:544
  200.6 27.0 %collective-permute-start.37 = (bf16[1,3,48,768]{3,2,1,0:T(8,128)(2,1)}, bf16[1,3,48,768]{3,2,1,0:T(8,128)(2,1)S(1)}, u32[]{:S(2)}, u32[]{:S(2)}) collective-permute-start(bf16[1,3,48,768]{3,2,1,0:T(8,128)(2,1)} %get-tuple-element.114), channel_id=1, source_target_pairs={{0,16},{16,0},{1,17},{17,1},{2,18},{18,2},{3,19},{19,3},{4,20},{20... | collective-permute-start | bytes 663560 | tf_op jit(solution)/shard_map/ppermute | solution.py:544
  201.7 26.0 %collective-permute-start.36 = (bf16[1,3,48,768]{3,2,1,0:T(8,128)(2,1)}, bf16[1,3,48,768]{3,2,1,0:T(8,128)(2,1)S(1)}, u32[]{:S(2)}, u32[]{:S(2)}) collective-permute-start(bf16[1,3,48,768]{3,2,1,0:T(8,128)(2,1)} %get-tuple-element.108.rest_2_), channel_id=1, source_target_pairs={{0,2},{1,3},{2,0},{3,1},{4,6},{5,7},{6,4},{7,5},{8,10},{9,11},{10,... | collective-permute-start | bytes 663560 | tf_op jit(solution)/shard_map/ppermute | solution.py:548
  247.9 22.7 %collective-permute-start.48 = (bf16[6,48,768]{2,1,0:T(8,128)(2,1)}, bf16[6,48,768]{2,1,0:T(8,128)(2,1)S(1)}, u32[]{:S(2)}, u32[]{:S(2)}) collective-permute-start(bf16[6,48,768]{2,1,0:T(8,128)(2,1)} %get-tuple-element.131), channel_id=1, source_target_pairs={{0,12},{1,13},{2,14},{3,15},{4,0},{5,1},{6,2},{7,3},{8,4},{9,5},{1... | collective-permute-start | bytes 1327112 | tf_op jit(solution)/shard_map/ppermute | solution.py:556
  249.7 21.0 %collective-permute-start.47 = (bf16[6,48,768]{2,1,0:T(8,128)(2,1)}, bf16[6,48,768]{2,1,0:T(8,128)(2,1)S(1)}, u32[]{:S(2)}, u32[]{:S(2)}) collective-permute-start(bf16[6,48,768]{2,1,0:T(8,128)(2,1)} %get-tuple-element.126.rest_0_), channel_id=1, source_target_pairs={{0,4},{1,5},{2,6},{3,7},{4,8},{5,9},{6,10},{7,11},{8,12},{9,13},{1... | collective-permute-start | bytes 1327112 | tf_op jit(solution)/shard_map/ppermute | solution.py:556
  276.6 18.8 %collective-permute-start.52 = (bf16[6,48,768]{2,1,0:T(8,128)(2,1)}, bf16[6,48,768]{2,1,0:T(8,128)(2,1)S(1)}, u32[]{:S(2)}, u32[]{:S(2)}) collective-permute-start(bf16[6,48,768]{2,1,0:T(8,128)(2,1)} %get-tuple-element.136.rest_0_.refs_0_), channel_id=1, source_target_pairs={{0,2},{1,3},{2,0},{3,1},{4,6},{5,7},{6,4},{7,5},{8,10},{9,11},{10,... | collective-permute-start | bytes 1327112 | tf_op jit(solution)/shard_map/ppermute | solution.py:548
  279.1 19.9 %collective-permute-start.50 = (bf16[6,48,768]{2,1,0:T(8,128)(2,1)}, bf16[6,48,768]{2,1,0:T(8,128)(2,1)S(1)}, u32[]{:S(2)}, u32[]{:S(2)}) collective-permute-start(bf16[6,48,768]{2,1,0:T(8,128)(2,1)} %get-tuple-element.136.rest_0_.refs_0_), channel_id=1, source_target_pairs={{0,12},{1,13},{2,14},{3,15},{4,0},{5,1},{6,2},{7,3},{8,4},{9,5},{1... | collective-permute-start | bytes 1327112 | tf_op jit(solution)/shard_map/ppermute | solution.py:556
  305.2 53.2 %all-to-all-start.1 = ((bf16[16,48,768]{2,1,0:T(8,128)(2,1)}), bf16[16,48,768]{2,1,0:T(8,128)(2,1)S(1)}, u32[]{:S(2)}, u32[]{:S(2)}) async-start(bf16[16,48,768]{2,1,0:T(8,128)(2,1)} %pick_blocks.3.rest_1_), calls=%async_computation.1 | async-start | bytes 2359296 | tf_op jit(solution)/shard_map/all_to_all | solution.py:1025
  311.2 76.4 %all-gather.4.cloned.1.call-start = ((), (), s32[]{:S(2)}) async-start(), calls=%async_computation.2 | async-start | bytes 1622016 | tf_op jit(solution)/shard_map/all_gather | solution.py:1016
  312.0 39.8 %collective-permute-start.59 = (bf16[12,48,768]{2,1,0:T(8,128)(2,1)S(1)}, bf16[12,48,768]{2,1,0:T(8,128)(2,1)S(1)}, u32[]{:S(2)}, u32[]{:S(2)}) collective-permute-start(bf16[12,48,768]{2,1,0:T(8,128)(2,1)S(1)} %copy-done.4), channel_id=1, source_target_pairs={{0,2},{1,3},{2,0},{3,1},{4,6},{5,7},{6,4},{7,5},{8,10},{9,11},{10,... | collective-permute-start | bytes 2654216 | tf_op jit(solution)/shard_map/ppermute | solution.py:548
  314.0 37.9 %collective-permute-start.58 = (bf16[12,48,768]{2,1,0:T(8,128)(2,1)S(1)}, bf16[12,48,768]{2,1,0:T(8,128)(2,1)}, u32[]{:S(2)}, u32[]{:S(2)}) collective-permute-start(bf16[12,48,768]{2,1,0:T(8,128)(2,1)S(1)} %copy-done.4), channel_id=1, source_target_pairs={{0,16},{16,0},{1,17},{17,1},{2,18},{18,2},{3,19},{19,3},{4,20},{20... | collective-permute-start | bytes 2654216 | tf_op jit(solution)/shard_map/ppermute | solution.py:544
  314.5 31.4 %collective-permute-start.55 = (bf16[6,48,768]{2,1,0:T(8,128)(2,1)}, bf16[6,48,768]{2,1,0:T(8,128)(2,1)S(1)}, u32[]{:S(2)}, u32[]{:S(2)}) collective-permute-start(bf16[6,48,768]{2,1,0:T(8,128)(2,1)} %copy-done.21), channel_id=1, source_target_pairs={{0,4},{1,5},{2,6},{3,7},{4,8},{5,9},{6,10},{7,11},{8,12},{9,13},{1... | collective-permute-start | bytes 1327112 | tf_op jit(solution)/shard_map/ppermute | solution.py:556
  316.1 33.9 %collective-permute-start.54 = (bf16[3,48,768]{2,1,0:T(8,128)(2,1)}, bf16[3,48,768]{2,1,0:T(8,128)(2,1)}, u32[]{:S(2)}, u32[]{:S(2)}) collective-permute-start(bf16[3,48,768]{2,1,0:T(8,128)(2,1)} %get-tuple-element.142), channel_id=1, source_target_pairs={{0,16},{16,0},{1,17},{17,1},{2,18},{18,2},{3,19},{19,3},{4,20},{20... | collective-permute-start | bytes 663560 | tf_op jit(solution)/shard_map/ppermute | solution.py:544
  317.6 34.2 %collective-permute-start.53 = (bf16[3,48,768]{2,1,0:T(8,128)(2,1)}, bf16[3,48,768]{2,1,0:T(8,128)(2,1)}, u32[]{:S(2)}, u32[]{:S(2)}) collective-permute-start(bf16[3,48,768]{2,1,0:T(8,128)(2,1)} %get-tuple-element.141.refs_2_), channel_id=1, source_target_pairs={{0,2},{1,3},{2,0},{3,1},{4,6},{5,7},{6,4},{7,5},{8,10},{9,11},{10,... | collective-permute-start | bytes 663560 | tf_op jit(solution)/shard_map/ppermute | solution.py:548
  355.1 21.6 %collective-permute-start.63 = (bf16[6,48,768]{2,1,0:T(8,128)(2,1)}, bf16[6,48,768]{2,1,0:T(8,128)(2,1)S(1)}, u32[]{:S(2)}, u32[]{:S(2)}) collective-permute-start(bf16[6,48,768]{2,1,0:T(8,128)(2,1)} %get-tuple-element.146), channel_id=1, source_target_pairs={{0,16},{16,0},{1,17},{17,1},{2,18},{18,2},{3,19},{19,3},{4,20},{20... | collective-permute-start | bytes 1327112 | tf_op jit(solution)/shard_map/ppermute | solution.py:544
  356.6 20.1 %collective-permute-start.62 = (bf16[6,48,768]{2,1,0:T(8,128)(2,1)}, bf16[6,48,768]{2,1,0:T(8,128)(2,1)S(1)}, u32[]{:S(2)}, u32[]{:S(2)}) collective-permute-start(bf16[6,48,768]{2,1,0:T(8,128)(2,1)} %get-tuple-element.143.refs_1_), channel_id=1, source_target_pairs={{0,2},{1,3},{2,0},{3,1},{4,6},{5,7},{6,4},{7,5},{8,10},{9,11},{10,... | collective-permute-start | bytes 1327112 | tf_op jit(solution)/shard_map/ppermute | solution.py:548
  369.6 29.3 %collective-permute-start.65 = (bf16[12,48,768]{2,1,0:T(8,128)(2,1)S(1)}, bf16[12,48,768]{2,1,0:T(8,128)(2,1)S(1)}, u32[]{:S(2)}, u32[]{:S(2)}) collective-permute-start(bf16[12,48,768]{2,1,0:T(8,128)(2,1)S(1)} %copy-done.3), channel_id=1, source_target_pairs={{0,16},{16,0},{1,17},{17,1},{2,18},{18,2},{3,19},{19,3},{4,20},{20... | collective-permute-start | bytes 2654216 | tf_op jit(solution)/shard_map/ppermute | solution.py:544
  386.2 19.3 %collective-permute-start.64 = (bf16[12,48,768]{2,1,0:T(8,128)(2,1)}, bf16[12,48,768]{2,1,0:T(8,128)(2,1)}, u32[]{:S(2)}, u32[]{:S(2)}) collective-permute-start(bf16[12,48,768]{2,1,0:T(8,128)(2,1)} %get-tuple-element.149), channel_id=1, source_target_pairs={{0,1},{1,0},{2,3},{3,2},{4,5},{5,4},{6,7},{7,6},{8,9},{9,8},{10,11... | collective-permute-start | bytes 2654216 | tf_op jit(solution)/shard_map/ppermute | solution.py:552
  (89 other events, 839.1 us)
Sparse Core Ops, SparseCore 0:
  315.5 68.5 all-gather.3

commit v7 on v6

--- a/solution.py
+++ b/solution.py
@@ -1030,17 +1030,14 @@
         def send_task(*after):
             send, owned = exchange(*after)
             kept.append(owned)
-            return (tasks[2](send),)
+            return (tasks[pages](tasks[2](send)),)
 
         def swap_task(*after):
             (even,) = pick_blocks(grad_at(lead), kept, (capacity // 2,), *after)
             kept[:] = even, swap_dp(even)
             return (even,)
 
-        def last_task(*after):
-            return (tasks[pages](*after),)
-
-        arrays, done = gather_blocks(new_mine, (last_task, send_task, swap_task))
+        arrays, done = gather_blocks(new_mine, (lambda *after: (), send_task, swap_task))
         at, near = gathered_place(group, spot, turn)
         at = jnp.where(near, at, 0)
         sibling = (me_f + 1 - 2 * (me_f % 2)) * held

time: 424 us -> 420 us (level)
    unnamed x104 -> x106, local copies, waits for them, and re-layouts: 13.1 us -> 12.3 us
  transfers between devices with their start and end apart: 69 -> 69, of which waited for: 19 -> 22; matrix products, arithmetic and copies ran while one was open for 7% -> 7% of each run, Pallas kernels for 42% -> 43%
where the time goes in v7:
time: 420 us; the launch traced here: 412 us
  Pallas kernels  187 us (45%)
  waiting for transfers between devices  91.9 us (22%)
  starting transfers between devices  69.8 us (17%)
  local copies, waits for them, and re-layouts  28.4 us (7%)
  other arithmetic  19.2 us (5%)
  between operations  15.6 us (4%)
    pallas_call x3, Pallas kernels, forward_page(): pl.pallas_call(forward_kernel, grid=(1,), in_specs=[page, page, page, pag...  42 us
    ppermute x19, waiting for transfers between devices, swap_dp(): return lax.ppermute(x, 'dp', [(0, 1), (1, 0)])  40.1 us
    ppermute x18, waiting for transfers between devices, swap_y(): return lax.ppermute(x, 'fsdp', [(f, f ^ 2) for f in range(16)])  28.8 us
    pallas_call x1, Pallas kernels, masked_part(): pl.pallas_call(masked_kernel, grid_spec=pltpu.PrefetchScalarGridSpec(num_...  26.5 us
    ppermute x18, starting transfers between devices, swap_y(): return lax.ppermute(x, 'fsdp', [(f, f ^ 2) for f in range(16)])  20.2 us
    pallas_call x1, Pallas kernels, attention_back(): pl.pallas_call(attention_back_kernel, grid_spec=pltpu.PrefetchScalarGridS...  20 us
    ppermute x19, starting transfers between devices, swap_dp(): return lax.ppermute(x, 'dp', [(0, 1), (1, 0)])  19.8 us
    ppermute x9, waiting for transfers between devices, up_z(): lax.ppermute(x, 'fsdp', [(f, (f + 4 * steps) % 16) for f in range(16)])  19.2 us
  transfers between devices with their start and end apart: 69, of which 22 were waited for; matrix products, arithmetic and copies ran while one was open for 7% of the time, Pallas kernels for 43%

profile of v7, /device:TPU:0, one launch (start us, length us, event | category | flops | bytes accessed | tf_op | source)
XLA Modules:
  0.0 412.1 jit_solution(5625781106634151081)
XLA Ops:
  9.6 4.6 %collective-permute-start.8 = (bf16[6,48,768]{2,1,0:T(8,128)(2,1)}, bf16[6,48,768]{2,1,0:T(8,128)(2,1)}, u32[]{:S(2)}, u32[]{:S(2)}) collective-permute-start(bf16[6,48,768]{2,1,0:T(8,128)(2,1)} %bitcast.41), channel_id=1, source_target_pairs={{0,12},{1,13},{2,14},{3,15},{4,0},{5,1},{6,2},{7,3},{8,4},{9,5},{1... | collective-permute-start | bytes 1327112 | tf_op jit(solution)/shard_map/ppermute | solution.py:556
  20.1 3.7 gather_fusion.2
  23.8 3.7 gather_fusion.1
  40.1 3.5 collective-permute-done.3
  45.3 5.3 %collective-permute-done.5.refs_3_ = bf16[6,48,768]{2,1,0:T(8,128)(2,1)S(1)} collective-permute-done((bf16[6,48,768]{2,1,0:T(8,128)(2,1)}, bf16[6,48,768]{2,1,0:T(8,128)(2,1)S(1)}, u32[]{:S(2)}, u32[]{:S(2)}) %collective-permute-start.5) | collective-permute-done | bytes 442400 | tf_op jit(solution)/shard_map/ppermute | solution.py:556
  53.6 20.0 %collective-permute-done.7.refs_1_ = bf16[6,48,768]{2,1,0:T(8,128)(2,1)S(1)} collective-permute-done((bf16[6,48,768]{2,1,0:T(8,128)(2,1)S(1)}, bf16[6,48,768]{2,1,0:T(8,128)(2,1)S(1)}, u32[]{:S(2)}, u32[]{:S(2)}) %collective-permute-start.7) | collective-permute-done | bytes 442400 | tf_op jit(solution)/shard_map/ppermute | solution.py:548
  83.2 4.4 %collective-permute-done.12 = bf16[3,48,768]{2,1,0:T(8,128)(2,1)} collective-permute-done((bf16[3,48,768]{2,1,0:T(8,128)(2,1)}, bf16[3,48,768]{2,1,0:T(8,128)(2,1)}, u32[]{:S(2)}, u32[]{:S(2)}) %collective-permute-start.12) | collective-permute-done | bytes 221216 | tf_op jit(solution)/shard_map/ppermute | solution.py:544
  91.0 5.4 %collective-permute-done.14 = bf16[6,48,768]{2,1,0:T(8,128)(2,1)} collective-permute-done((bf16[6,48,768]{2,1,0:T(8,128)(2,1)}, bf16[6,48,768]{2,1,0:T(8,128)(2,1)}, u32[]{:S(2)}, u32[]{:S(2)}) %collective-permute-start.14) | collective-permute-done | bytes 442400 | tf_op jit(solution)/shard_map/ppermute | solution.py:544
  98.6 4.9 %all-to-all-start = ((bf16[16,3,48,768]{3,2,1,0:T(8,128)(2,1)}), bf16[16,3,48,768]{3,2,1,0:T(8,128)(2,1)S(1)}, u32[]{:S(2)}, u32[]{:S(2)}) async-start(bf16[16,3,48,768]{3,2,1,0:T(8,128)(2,1)} %pad_maximum_fusion.refs_2_), calls=%async_computation | async-start | bytes 7077888 | tf_op jit(solution)/shard_map/all_to_all | solution.py:984
  103.6 17.8 %project.1 = (bf16[1536,768]{1,0:T(8,128)(2,1)}, bf16[1536,768]{1,0:T(8,128)(2,1)}, bf16[1536,768]{1,0:T(8,128)(2,1)}, bf16[336,768]{1,0:T(8,128)(2,1)}, bf16[33...) custom-call(s32[40]{0:T(128)} %stack.181.rows_ref, s32[3,112,1]{2,1,0:T(8,128)} %copy.33.pos_ref, ...), custom_call_target="tpu_custom_call" | custom-call | flops 17999998976 | bytes 20000000 | tf_op jit(solution)/shard_map/project/pallas_call | solution.py:205
  121.4 26.5 %masked.1 = (f32[336,768]{1,0:T(8,128)}, bf16[336,768]{1,0:T(8,128)(2,1)}, f32[16,768]{1,0:T(8,128)}, bf16[96,48,768]{2,1,0:T(8,128)(2,1)}, bf16[24,48,768]{2,1,...) custom-call(s32[192]{0:T(256)} %fusion.5.place_ref, ...), custom_call_target="tpu_custom_call" | custom-call | flops 24000000000 | bytes 30000000 | tf_op jit(solution)/shard_map/masked/pallas_call | solution.py:311
  147.9 20.0 %attention_back.1 = (bf16[336,768]{1,0:T(8,128)(2,1)}, bf16[1536,768]{1,0:T(8,128)(2,1)}, bf16[1536,768]{1,0:T(8,128)(2,1)}, f32[8,768]{1,0:T(8,128)}, bf16[96,4...) custom-call(s32[192]{0:T(256)} %fusion.5.place_ref, ...), custom_call_target="tpu_custom_call", output_to_operand_aliasing={{4}: (7, {}), {5}: (8, {}), {6}: (9, {}), {7}: (10, {}), {8... | custom-call | flops 24999999488 | bytes 30000000 | tf_op jit(solution)/shard_map/attention_back/pallas_call | solution.py:406
  172.0 3.3 core_sum.3
  178.7 9.3 %collective-permute-done.33.to_a_ref = bf16[1,6,48,768]{3,2,1,0:T(8,128)(2,1)S(1)} collective-permute-done((bf16[1,6,48,768]{3,2,1,0:T(8,128)(2,1)}, bf16[1,6,48,768]{3,2,1,0:T(8,128)(2,1)S(1)}, u32[]{:S(2)}, u32[]{:S(2)}) %collective-permute-start.33) | collective-permute-done | bytes 442400 | tf_op jit(solution)/shard_map/ppermute | solution.py:544
  193.5 4.7 %core_sum.4 = (bf16[2,6,48,768]{3,2,1,0:T(8,128)(2,1)}, bf16[2,6,48,768]{3,2,1,0:T(8,128)(2,1)}, bf16[2,6,48,768]{3,2,1,0:T(8,128)(2,1)}, bf16[2,6,48,768]{3,2,1,0:T(8,128)(2,1)}) custom-call(bf16[4,4,6,48,768]{4,3,2,1,0:T(8,128)(2,1)} %bitcast.105, bf16[1,4,6,48,768]{4,3,2,1,0:T(8,128)(2,1)} %bitcast.78.rest_0_, ...), custom_call_target="tpu_custom_call" | custom-call | bytes 1000 | tf_op jit(solution)/shard_map/core_sum/pallas_call | solution.py:593
  202.3 14.0 %forward_page.3.rest_0_ = bf16[1536,768]{1,0:T(8,128)(2,1)} custom-call(bf16[1536,768]{1,0:T(8,128)(2,1)} %tok_ref.9, bf16[1536,768]{1,0:T(8,128)(2,1)} %get-tuple-element.87.q_ref, bf16[1536,768]{1,0:T(8,128)(2,1)} %get-tuple-element.88.k_ref, bf16[1536,768]{1,0:T(8,128)(2,1)} %get-tuple-element.89.v_ref, f32[12,768]{1,0:T(8,128)} %vec_ref.9, ...), custom_call_target="tpu_custom_call" | custom-call | bytes 1000 | tf_op jit(solution)/shard_map/forward_page/pallas_call | solution.py:472
  216.3 4.7 %collective-permute-done.39.to_b_ref = bf16[2,6,48,768]{3,2,1,0:T(8,128)(2,1)S(1)} collective-permute-done((bf16[2,6,48,768]{3,2,1,0:T(8,128)(2,1)}, bf16[2,6,48,768]{3,2,1,0:T(8,128)(2,1)S(1)}, u32[]{:S(2)}, u32[]{:S(2)}) %collective-permute-start.39) | collective-permute-done | bytes 884768 | tf_op jit(solution)/shard_map/ppermute | solution.py:548
  230.8 4.6 %collective-permute-start.44 = (bf16[6,48,768]{2,1,0:T(8,128)(2,1)}, bf16[6,48,768]{2,1,0:T(8,128)(2,1)S(1)}, u32[]{:S(2)}, u32[]{:S(2)}) collective-permute-start(bf16[6,48,768]{2,1,0:T(8,128)(2,1)} %last_sum.2.rest_1_), channel_id=1, source_target_pairs={{0,4},{1,5},{2,6},{3,7},{4,8},{5,9},{6,10},{7,11},{8,12},{9,13},{1... | collective-permute-start | bytes 1327112 | tf_op jit(solution)/shard_map/ppermute | solution.py:556
  235.9 3.3 core_sum.5
  256.4 14.0 %forward_page.4.refs_7_.rest_0_ = bf16[1536,768]{1,0:T(8,128)(2,1)} custom-call(bf16[1536,768]{1,0:T(8,128)(2,1)} %tok_ref.9, bf16[1536,768]{1,0:T(8,128)(2,1)} %get-tuple-element.87.q_ref, bf16[1536,768]{1,0:T(8,128)(2,1)} %get-tuple-element.88.k_ref, bf16[1536,768]{1,0:T(8,128)(2,1)} %get-tuple-element.89.v_ref, ...), custom_call_target="tpu_custom_call", output_to_operand_aliasing={{}: (6, {})} | custom-call | bytes 1000 | tf_op jit(solution)/shard_map/forward_page/pallas_call | solution.py:472
  271.5 5.0 %weight_step.1 = (bf16[6,48,768]{2,1,0:T(8,128)(2,1)}, bf16[6,48,768]{2,1,0:T(8,128)(2,1)}) custom-call(s32[6]{0:T(128)} %fusion.27.from_ref, bf16[1,3,48,768]{3,2,1,0:T(8,128)(2,1)} %get-tuple-element.128.refs_0_, bf16[1,3,48,768]{3,2,1,0:T(8,128)(2,1)} %copy-done.38, bf16[1,3,48,768]{3,2,1,0:T(8,128)(2,1)} %get-tuple-element.129.refs_2_, ...), custom_call_target="tpu_custom_call" | custom-call | bytes 1000 | tf_op jit(solution)/shard_map/weight_step/pallas_call | solution.py:706
  278.9 3.5 collective-permute-start.50
  288.6 3.6 collective-permute-done.50.refs_1_
  292.2 5.3 %collective-permute-done.49.refs_0_ = bf16[6,48,768]{2,1,0:T(8,128)(2,1)S(1)} collective-permute-done((bf16[6,48,768]{2,1,0:T(8,128)(2,1)}, bf16[6,48,768]{2,1,0:T(8,128)(2,1)S(1)}, u32[]{:S(2)}, u32[]{:S(2)}) %collective-permute-start.49) | collective-permute-done | bytes 442400 | tf_op jit(solution)/shard_map/ppermute | solution.py:556
  303.8 3.8 all-to-all-start.1
  314.3 14.0 %forward_page.5.rest_0_ = bf16[1536,768]{1,0:T(8,128)(2,1)} custom-call(bf16[1536,768]{1,0:T(8,128)(2,1)} %tok_ref.9, bf16[1536,768]{1,0:T(8,128)(2,1)} %get-tuple-element.87.q_ref, bf16[1536,768]{1,0:T(8,128)(2,1)} %get-tuple-element.88.k_ref, bf16[1536,768]{1,0:T(8,128)(2,1)} %get-tuple-element.89.v_ref, ...), custom_call_target="tpu_custom_call", output_to_operand_aliasing={{}: (6, {})} | custom-call | bytes 1000 | tf_op jit(solution)/shard_map/forward_page/pallas_call | solution.py:472
  328.3 11.7 %input_grad.1.refs_1_ = f32[1536,768]{1,0:T(8,128)} custom-call(s32[3,112,1]{2,1,0:T(8,128)} %copy.33.pos_ref, bf16[336,768]{1,0:T(8,128)(2,1)} %get-tuple-element.138.dq_ref, bf16[1536,768]{1,0:T(8,128)(2,1)} %get-tuple-element.139.dk_ref, bf16[1536,768]{1,0:T(8,128)(2,1)} %get-tuple-element.140.dv_ref, f32[336,768]{1,0:T(8,128)} %get-tuple-element.141.gr_ref, ...), custom_call_target="tpu_custom_call" | custom-call | bytes 1000 | tf_op jit(solution)/shard_map/input_grad/pallas_call | solution.py:514
  367.5 5.7 %moment_step.2 = (f32[12,2,48,768]{3,2,1,0:T(8,128)}, f32[12,2,48,768]{3,2,1,0:T(8,128)}) custom-call(s32[2]{0:T(128)} %pad_add_fusion.1.info_ref, bf16[12,48,768]{2,1,0:T(8,128)(2,1)} %pick_blocks.4.refs_2_.grad_ref, f32[12,2,48,768]{3,2,1,0:T(8,128)} %bitcast.109, f32[12,2,48,768]{3,2,1,0:T(8,128)} %bitcast.107, bf16[3,48,768]{2,1,0:T(8,128)(2,1)} %get-tuple-element.144.rest_0_), custom_call_target="tpu_custom_call" | custom-call | bytes 1000 | tf_op jit(solution)/shard_map/moment_step/pallas_call | solution.py:743
  373.2 4.2 %collective-permute-done.61.refs_9_ = bf16[3,48,768]{2,1,0:T(8,128)(2,1)S(1)} collective-permute-done((bf16[3,48,768]{2,1,0:T(8,128)(2,1)}, bf16[3,48,768]{2,1,0:T(8,128)(2,1)S(1)}, u32[]{:S(2)}, u32[]{:S(2)}) %collective-permute-start.61) | collective-permute-done | bytes 221216 | tf_op jit(solution)/shard_map/ppermute | solution.py:544
  378.1 4.5 %pick_blocks.5 = (bf16[12,48,768]{2,1,0:T(8,128)(2,1)}, bf16[12,48,768]{2,1,0:T(8,128)(2,1)}) custom-call(s32[24]{0:T(128)} %pad_add_fusion.from_ref, bf16[6,48,768]{2,1,0:T(8,128)(2,1)} %get-tuple-element.136.refs_0_, bf16[6,48,768]{2,1,0:T(8,128)(2,1)} %copy-done.10, bf16[6,48,768]{2,1,0:T(8,128)(2,1)} %copy-done.9, ...), custom_call_target="tpu_custom_call" | custom-call | bytes 1000 | tf_op jit(solution)/shard_map/pick_blocks/pallas_call | solution.py:793
  386.3 9.0 %collective-permute-done.65.grad_ref = bf16[12,48,768]{2,1,0:T(8,128)(2,1)S(1)} collective-permute-done((bf16[12,48,768]{2,1,0:T(8,128)(2,1)S(1)}, bf16[12,48,768]{2,1,0:T(8,128)(2,1)S(1)}, u32[]{:S(2)}, u32[]{:S(2)}) %collective-permute-start.65) | collective-permute-done | bytes 884768 | tf_op jit(solution)/shard_map/ppermute | solution.py:544
  396.2 5.6 %moment_step.3 = (f32[12,2,48,768]{3,2,1,0:T(8,128)}, f32[12,2,48,768]{3,2,1,0:T(8,128)}) custom-call(s32[2]{0:T(128)} %pad_add_fusion.2.info_ref, bf16[12,48,768]{2,1,0:T(8,128)(2,1)} %copy-done.11, f32[12,2,48,768]{3,2,1,0:T(8,128)} %bitcast.110, f32[12,2,48,768]{3,2,1,0:T(8,128)} %bitcast.108, ...), custom_call_target="tpu_custom_call", output_to_operand_aliasing={{0}: (4, {}), {1}: (5, {})} | custom-call | bytes 1000 | tf_op jit(solution)/shard_map/moment_step/pallas_call | solution.py:743
  (283 shorter events, 143.1 us)
Async XLA Ops:
  9.1 28.3 %collective-permute-start.15 = (bf16[6,48,768]{2,1,0:T(8,128)(2,1)}, bf16[6,48,768]{2,1,0:T(8,128)(2,1)}, u32[]{:S(2)}, u32[]{:S(2)}) collective-permute-start(bf16[6,48,768]{2,1,0:T(8,128)(2,1)} %bitcast.41), channel_id=1, source_target_pairs={{0,1},{1,0},{2,3},{3,2},{4,5},{5,4},{6,7},{7,6},{8,9},{9,8},{10,11... | collective-permute-start | bytes 1327112 | tf_op jit(solution)/shard_map/ppermute | solution.py:552
  9.6 27.9 %collective-permute-start.8 = (bf16[6,48,768]{2,1,0:T(8,128)(2,1)}, bf16[6,48,768]{2,1,0:T(8,128)(2,1)}, u32[]{:S(2)}, u32[]{:S(2)}) collective-permute-start(bf16[6,48,768]{2,1,0:T(8,128)(2,1)} %bitcast.41), channel_id=1, source_target_pairs={{0,12},{1,13},{2,14},{3,15},{4,0},{5,1},{6,2},{7,3},{8,4},{9,5},{1... | collective-permute-start | bytes 1327112 | tf_op jit(solution)/shard_map/ppermute | solution.py:556
  14.2 23.2 %collective-permute-start.4 = (bf16[6,48,768]{2,1,0:T(8,128)(2,1)}, bf16[6,48,768]{2,1,0:T(8,128)(2,1)}, u32[]{:S(2)}, u32[]{:S(2)}) collective-permute-start(bf16[6,48,768]{2,1,0:T(8,128)(2,1)} %bitcast.41), channel_id=1, source_target_pairs={{0,4},{1,5},{2,6},{3,7},{4,8},{5,9},{6,10},{7,11},{8,12},{9,13},{1... | collective-permute-start | bytes 1327112 | tf_op jit(solution)/shard_map/ppermute | solution.py:556
  14.2 20.2 %collective-permute-start.1 = (bf16[6,48,768]{2,1,0:T(8,128)(2,1)}, bf16[6,48,768]{2,1,0:T(8,128)(2,1)}, u32[]{:S(2)}, u32[]{:S(2)}) collective-permute-start(bf16[6,48,768]{2,1,0:T(8,128)(2,1)} %bitcast.41), channel_id=1, source_target_pairs={{0,2},{1,3},{2,0},{3,1},{4,6},{5,7},{6,4},{7,5},{8,10},{9,11},{10,... | collective-permute-start | bytes 1327112 | tf_op jit(solution)/shard_map/ppermute | solution.py:548
  15.7 18.7 %collective-permute-start = (bf16[6,48,768]{2,1,0:T(8,128)(2,1)}, bf16[6,48,768]{2,1,0:T(8,128)(2,1)}, u32[]{:S(2)}, u32[]{:S(2)}) collective-permute-start(bf16[6,48,768]{2,1,0:T(8,128)(2,1)} %bitcast.41), channel_id=1, source_target_pairs={{0,16},{16,0},{1,17},{17,1},{2,18},{18,2},{3,19},{19,3},{4,20},{20... | collective-permute-start | bytes 1327112 | tf_op jit(solution)/shard_map/ppermute | solution.py:544
  43.6 30.5 %collective-permute-start.10 = (bf16[12,48,768]{2,1,0:T(8,128)(2,1)}, bf16[12,48,768]{2,1,0:T(8,128)(2,1)}, u32[]{:S(2)}, u32[]{:S(2)}) collective-permute-start(bf16[12,48,768]{2,1,0:T(8,128)(2,1)} %move.10.refs_2_), channel_id=1, source_target_pairs={{0,2},{1,3},{2,0},{3,1},{4,6},{5,7},{6,4},{7,5},{8,10},{9,11},{10,... | collective-permute-start | bytes 2654216 | tf_op jit(solution)/shard_map/ppermute | solution.py:548
  44.1 30.3 %collective-permute-start.9 = (bf16[12,48,768]{2,1,0:T(8,128)(2,1)}, bf16[12,48,768]{2,1,0:T(8,128)(2,1)}, u32[]{:S(2)}, u32[]{:S(2)}) collective-permute-start(bf16[12,48,768]{2,1,0:T(8,128)(2,1)} %move.10.refs_2_), channel_id=1, source_target_pairs={{0,16},{16,0},{1,17},{17,1},{2,18},{18,2},{3,19},{19,3},{4,20},{20... | collective-permute-start | bytes 2654216 | tf_op jit(solution)/shard_map/ppermute | solution.py:544
  50.6 23.0 %collective-permute-start.7 = (bf16[6,48,768]{2,1,0:T(8,128)(2,1)S(1)}, bf16[6,48,768]{2,1,0:T(8,128)(2,1)S(1)}, u32[]{:S(2)}, u32[]{:S(2)}) collective-permute-start(bf16[6,48,768]{2,1,0:T(8,128)(2,1)S(1)} %collective-permute-done.5.refs_3_), channel_id=1, source_target_pairs={{0,2},{1,3},{2,0},{3,1},{4,6},{5,7},{6,4},{7,5},{8,10},{9,11},{10,... | collective-permute-start | bytes 1327112 | tf_op jit(solution)/shard_map/ppermute | solution.py:548
  52.1 21.7 %collective-permute-start.6 = (bf16[6,48,768]{2,1,0:T(8,128)(2,1)S(1)}, bf16[6,48,768]{2,1,0:T(8,128)(2,1)S(1)}, u32[]{:S(2)}, u32[]{:S(2)}) collective-permute-start(bf16[6,48,768]{2,1,0:T(8,128)(2,1)S(1)} %collective-permute-done.5.refs_3_), channel_id=1, source_target_pairs={{0,16},{16,0},{1,17},{17,1},{2,18},{18,2},{3,19},{19,3},{4,20},{20... | collective-permute-start | bytes 1327112 | tf_op jit(solution)/shard_map/ppermute | solution.py:544
  53.6 28.5 %collective-permute-start.25 = (bf16[12,48,768]{2,1,0:T(8,128)(2,1)}, bf16[12,48,768]{2,1,0:T(8,128)(2,1)S(1)}, u32[]{:S(2)}, u32[]{:S(2)}) collective-permute-start(bf16[12,48,768]{2,1,0:T(8,128)(2,1)} %move.10.refs_2_), channel_id=1, source_target_pairs={{0,1},{1,0},{2,3},{3,2},{4,5},{5,4},{6,7},{7,6},{8,9},{9,8},{10,11... | collective-permute-start | bytes 2654216 | tf_op jit(solution)/shard_map/ppermute | solution.py:552
  98.6 93.1 %all-to-all-start = ((bf16[16,3,48,768]{3,2,1,0:T(8,128)(2,1)}), bf16[16,3,48,768]{3,2,1,0:T(8,128)(2,1)S(1)}, u32[]{:S(2)}, u32[]{:S(2)}) async-start(bf16[16,3,48,768]{3,2,1,0:T(8,128)(2,1)} %pad_maximum_fusion.refs_2_), calls=%async_computation | async-start | bytes 7077888 | tf_op jit(solution)/shard_map/all_to_all | solution.py:984
  168.4 23.3 %collective-permute-start.30 = (bf16[24,48,768]{2,1,0:T(8,128)(2,1)}, bf16[24,48,768]{2,1,0:T(8,128)(2,1)}, u32[]{:S(2)}, u32[]{:S(2)}) collective-permute-start(bf16[24,48,768]{2,1,0:T(8,128)(2,1)} %get-tuple-element.101), channel_id=1, source_target_pairs={{0,1},{1,0},{2,3},{3,2},{4,5},{5,4},{6,7},{7,6},{8,9},{9,8},{10,11... | collective-permute-start | bytes 5308424 | tf_op jit(solution)/shard_map/ppermute | solution.py:552
  168.5 23.2 %collective-permute-start.31 = (bf16[24,48,768]{2,1,0:T(8,128)(2,1)}, bf16[24,48,768]{2,1,0:T(8,128)(2,1)}, u32[]{:S(2)}, u32[]{:S(2)}) collective-permute-start(bf16[24,48,768]{2,1,0:T(8,128)(2,1)} %get-tuple-element.102), channel_id=1, source_target_pairs={{0,1},{1,0},{2,3},{3,2},{4,5},{5,4},{6,7},{7,6},{8,9},{9,8},{10,11... | collective-permute-start | bytes 5308424 | tf_op jit(solution)/shard_map/ppermute | solution.py:552
  168.9 67.0 %collective-permute-start.35 = (bf16[24,48,768]{2,1,0:T(8,128)(2,1)}, bf16[24,48,768]{2,1,0:T(8,128)(2,1)}, u32[]{:S(2)}, u32[]{:S(2)}) collective-permute-start(bf16[24,48,768]{2,1,0:T(8,128)(2,1)} %get-tuple-element.111), channel_id=1, source_target_pairs={{0,1},{1,0},{2,3},{3,2},{4,5},{5,4},{6,7},{7,6},{8,9},{9,8},{10,11... | collective-permute-start | bytes 5308424 | tf_op jit(solution)/shard_map/ppermute | solution.py:552
  198.2 22.9 %collective-permute-start.39 = (bf16[2,6,48,768]{3,2,1,0:T(8,128)(2,1)}, bf16[2,6,48,768]{3,2,1,0:T(8,128)(2,1)S(1)}, u32[]{:S(2)}, u32[]{:S(2)}) collective-permute-start(bf16[2,6,48,768]{3,2,1,0:T(8,128)(2,1)} %get-tuple-element.117), channel_id=1, source_target_pairs={{0,2},{1,3},{2,0},{3,1},{4,6},{5,7},{6,4},{7,5},{8,10},{9,11},{10,... | collective-permute-start | bytes 2654216 | tf_op jit(solution)/shard_map/ppermute | solution.py:548
  199.9 22.8 %collective-permute-start.38 = (bf16[2,6,48,768]{3,2,1,0:T(8,128)(2,1)}, bf16[2,6,48,768]{3,2,1,0:T(8,128)(2,1)S(1)}, u32[]{:S(2)}, u32[]{:S(2)}) collective-permute-start(bf16[2,6,48,768]{3,2,1,0:T(8,128)(2,1)} %get-tuple-element.110.rest_0_), channel_id=1, source_target_pairs={{0,16},{16,0},{1,17},{17,1},{2,18},{18,2},{3,19},{19,3},{4,20},{20... | collective-permute-start | bytes 2654216 | tf_op jit(solution)/shard_map/ppermute | solution.py:544
  200.8 27.1 %collective-permute-start.37 = (bf16[1,3,48,768]{3,2,1,0:T(8,128)(2,1)}, bf16[1,3,48,768]{3,2,1,0:T(8,128)(2,1)S(1)}, u32[]{:S(2)}, u32[]{:S(2)}) collective-permute-start(bf16[1,3,48,768]{3,2,1,0:T(8,128)(2,1)} %get-tuple-element.114), channel_id=1, source_target_pairs={{0,16},{16,0},{1,17},{17,1},{2,18},{18,2},{3,19},{19,3},{4,20},{20... | collective-permute-start | bytes 663560 | tf_op jit(solution)/shard_map/ppermute | solution.py:544
  201.9 26.0 %collective-permute-start.36 = (bf16[1,3,48,768]{3,2,1,0:T(8,128)(2,1)}, bf16[1,3,48,768]{3,2,1,0:T(8,128)(2,1)S(1)}, u32[]{:S(2)}, u32[]{:S(2)}) collective-permute-start(bf16[1,3,48,768]{3,2,1,0:T(8,128)(2,1)} %get-tuple-element.108.rest_2_), channel_id=1, source_target_pairs={{0,2},{1,3},{2,0},{3,1},{4,6},{5,7},{6,4},{7,5},{8,10},{9,11},{10,... | collective-permute-start | bytes 663560 | tf_op jit(solution)/shard_map/ppermute | solution.py:548
  227.5 16.9 %collective-permute-start.42 = (bf16[2,3,48,768]{3,2,1,0:T(8,128)(2,1)}, bf16[2,3,48,768]{3,2,1,0:T(8,128)(2,1)S(1)}, u32[]{:S(2)}, u32[]{:S(2)}) collective-permute-start(bf16[2,3,48,768]{3,2,1,0:T(8,128)(2,1)} %get-tuple-element.118.rest_0_), channel_id=1, source_target_pairs={{0,2},{1,3},{2,0},{3,1},{4,6},{5,7},{6,4},{7,5},{8,10},{9,11},{10,... | collective-permute-start | bytes 1327112 | tf_op jit(solution)/shard_map/ppermute | solution.py:548
  248.0 22.4 %collective-permute-start.48 = (bf16[6,48,768]{2,1,0:T(8,128)(2,1)}, bf16[6,48,768]{2,1,0:T(8,128)(2,1)S(1)}, u32[]{:S(2)}, u32[]{:S(2)}) collective-permute-start(bf16[6,48,768]{2,1,0:T(8,128)(2,1)} %get-tuple-element.131), channel_id=1, source_target_pairs={{0,12},{1,13},{2,14},{3,15},{4,0},{5,1},{6,2},{7,3},{8,4},{9,5},{1... | collective-permute-start | bytes 1327112 | tf_op jit(solution)/shard_map/ppermute | solution.py:556
  249.8 20.7 %collective-permute-start.47 = (bf16[6,48,768]{2,1,0:T(8,128)(2,1)}, bf16[6,48,768]{2,1,0:T(8,128)(2,1)S(1)}, u32[]{:S(2)}, u32[]{:S(2)}) collective-permute-start(bf16[6,48,768]{2,1,0:T(8,128)(2,1)} %get-tuple-element.126.rest_0_), channel_id=1, source_target_pairs={{0,4},{1,5},{2,6},{3,7},{4,8},{5,9},{6,10},{7,11},{8,12},{9,13},{1... | collective-permute-start | bytes 1327112 | tf_op jit(solution)/shard_map/ppermute | solution.py:556
  303.8 51.1 %all-to-all-start.1 = ((bf16[16,48,768]{2,1,0:T(8,128)(2,1)}), bf16[16,48,768]{2,1,0:T(8,128)(2,1)S(1)}, u32[]{:S(2)}, u32[]{:S(2)}) async-start(bf16[16,48,768]{2,1,0:T(8,128)(2,1)} %pick_blocks.3.rest_1_), calls=%async_computation.1 | async-start | bytes 2359296 | tf_op jit(solution)/shard_map/all_to_all | solution.py:1025
  307.6 76.4 %all-gather.4.cloned.1.call-start = ((), (), s32[]{:S(2)}) async-start(), calls=%async_computation.2 | async-start | bytes 1622016 | tf_op jit(solution)/shard_map/all_gather | solution.py:1016
  308.4 39.9 %collective-permute-start.59 = (bf16[12,48,768]{2,1,0:T(8,128)(2,1)S(1)}, bf16[12,48,768]{2,1,0:T(8,128)(2,1)S(1)}, u32[]{:S(2)}, u32[]{:S(2)}) collective-permute-start(bf16[12,48,768]{2,1,0:T(8,128)(2,1)S(1)} %copy-done.4), channel_id=1, source_target_pairs={{0,2},{1,3},{2,0},{3,1},{4,6},{5,7},{6,4},{7,5},{8,10},{9,11},{10,... | collective-permute-start | bytes 2654216 | tf_op jit(solution)/shard_map/ppermute | solution.py:548
  310.2 38.0 %collective-permute-start.58 = (bf16[12,48,768]{2,1,0:T(8,128)(2,1)S(1)}, bf16[12,48,768]{2,1,0:T(8,128)(2,1)}, u32[]{:S(2)}, u32[]{:S(2)}) collective-permute-start(bf16[12,48,768]{2,1,0:T(8,128)(2,1)S(1)} %copy-done.4), channel_id=1, source_target_pairs={{0,16},{16,0},{1,17},{17,1},{2,18},{18,2},{3,19},{19,3},{4,20},{20... | collective-permute-start | bytes 2654216 | tf_op jit(solution)/shard_map/ppermute | solution.py:544
  310.9 31.3 %collective-permute-start.55 = (bf16[6,48,768]{2,1,0:T(8,128)(2,1)S(1)}, bf16[6,48,768]{2,1,0:T(8,128)(2,1)S(1)}, u32[]{:S(2)}, u32[]{:S(2)}) collective-permute-start(bf16[6,48,768]{2,1,0:T(8,128)(2,1)S(1)} %copy-done.21), channel_id=1, source_target_pairs={{0,4},{1,5},{2,6},{3,7},{4,8},{5,9},{6,10},{7,11},{8,12},{9,13},{1... | collective-permute-start | bytes 1327112 | tf_op jit(solution)/shard_map/ppermute | solution.py:556
  312.4 34.0 %collective-permute-start.54 = (bf16[3,48,768]{2,1,0:T(8,128)(2,1)}, bf16[3,48,768]{2,1,0:T(8,128)(2,1)}, u32[]{:S(2)}, u32[]{:S(2)}) collective-permute-start(bf16[3,48,768]{2,1,0:T(8,128)(2,1)} %get-tuple-element.142), channel_id=1, source_target_pairs={{0,16},{16,0},{1,17},{17,1},{2,18},{18,2},{3,19},{19,3},{4,20},{20... | collective-permute-start | bytes 663560 | tf_op jit(solution)/shard_map/ppermute | solution.py:544
  313.8 34.5 %collective-permute-start.53 = (bf16[3,48,768]{2,1,0:T(8,128)(2,1)}, bf16[3,48,768]{2,1,0:T(8,128)(2,1)}, u32[]{:S(2)}, u32[]{:S(2)}) collective-permute-start(bf16[3,48,768]{2,1,0:T(8,128)(2,1)} %get-tuple-element.137.refs_2_), channel_id=1, source_target_pairs={{0,2},{1,3},{2,0},{3,1},{4,6},{5,7},{6,4},{7,5},{8,10},{9,11},{10,... | collective-permute-start | bytes 663560 | tf_op jit(solution)/shard_map/ppermute | solution.py:548
  351.6 21.5 %collective-permute-start.63 = (bf16[6,48,768]{2,1,0:T(8,128)(2,1)}, bf16[6,48,768]{2,1,0:T(8,128)(2,1)S(1)}, u32[]{:S(2)}, u32[]{:S(2)}) collective-permute-start(bf16[6,48,768]{2,1,0:T(8,128)(2,1)} %get-tuple-element.146), channel_id=1, source_target_pairs={{0,16},{16,0},{1,17},{17,1},{2,18},{18,2},{3,19},{19,3},{4,20},{20... | collective-permute-start | bytes 1327112 | tf_op jit(solution)/shard_map/ppermute | solution.py:544
  353.1 20.1 %collective-permute-start.62 = (bf16[6,48,768]{2,1,0:T(8,128)(2,1)}, bf16[6,48,768]{2,1,0:T(8,128)(2,1)S(1)}, u32[]{:S(2)}, u32[]{:S(2)}) collective-permute-start(bf16[6,48,768]{2,1,0:T(8,128)(2,1)} %get-tuple-element.143.refs_1_), channel_id=1, source_target_pairs={{0,2},{1,3},{2,0},{3,1},{4,6},{5,7},{6,4},{7,5},{8,10},{9,11},{10,... | collective-permute-start | bytes 1327112 | tf_op jit(solution)/shard_map/ppermute | solution.py:548
  366.1 29.2 %collective-permute-start.65 = (bf16[12,48,768]{2,1,0:T(8,128)(2,1)S(1)}, bf16[12,48,768]{2,1,0:T(8,128)(2,1)S(1)}, u32[]{:S(2)}, u32[]{:S(2)}) collective-permute-start(bf16[12,48,768]{2,1,0:T(8,128)(2,1)S(1)} %copy-done.3), channel_id=1, source_target_pairs={{0,16},{16,0},{1,17},{17,1},{2,18},{18,2},{3,19},{19,3},{4,20},{20... | collective-permute-start | bytes 2654216 | tf_op jit(solution)/shard_map/ppermute | solution.py:544
  382.6 19.3 %collective-permute-start.64 = (bf16[12,48,768]{2,1,0:T(8,128)(2,1)}, bf16[12,48,768]{2,1,0:T(8,128)(2,1)}, u32[]{:S(2)}, u32[]{:S(2)}) collective-permute-start(bf16[12,48,768]{2,1,0:T(8,128)(2,1)} %get-tuple-element.149), channel_id=1, source_target_pairs={{0,1},{1,0},{2,3},{3,2},{4,5},{5,4},{6,7},{7,6},{8,9},{9,8},{10,11... | collective-permute-start | bytes 2654216 | tf_op jit(solution)/shard_map/ppermute | solution.py:552
  (90 other events, 823.9 us)
Sparse Core Ops, SparseCore 0:
  311.9 68.5 all-gather.3
